TPU v7x, 256 devices: a whole 4x4x8 slice. The times are simulated.
256 devices in a mesh: dom: 64 (over x_lo, z, y), vec: 4 (over x_hi, core).
Axes of the slice: x: 4 (x_hi: 2, x_lo: 2; x = x_hi * 2 + x_lo), y: 4, z: 8, core: 2. Of those that a mesh axis runs over, the one named last changes fastest.
Arguments:
- vectors: float32 [4, 32, 2048, 1024], P(None, 'vec', 'dom'), may hold values from -6 to 6
- hoppings: float32 [2, 3, 2048, 1024], P(None, None, 'dom'), may hold values from 0.5 to 1.5
- potential: float32 [4, 2048, 1024], P(None, 'dom'), may hold values from -1 to 1
- stacking: int32 [2048, 1024], P('dom'), may hold values from 0 to 7
- interlayer: float32 [2, 8], replicated, may hold values from 0.2 to 1
- filling: float32 [1], replicated, may hold values from 0.3 to 0.7
Outputs:
- new_potential: float32 [4, 2048, 1024], P(None, 'dom')
All inputs are finite; a program needn't handle non-finite values.
Results may differ from a plain program's by a relative error of at most 0.0003.
Values sent between devices are 32-bit elements; how exact they have to be, the bound alone decides.
No kernel may reach another device: no remote copies, remote signals or barrier semaphores. Data moves between devices by JAX's collectives and lax.ppermute only.
A program may use at most 128 MiB of HBM per device.

v0:
```python
import math

import jax
import jax.numpy as jnp
from jax import lax
from jax.sharding import PartitionSpec as P

CHEB = 4
BISECT = 16


def passed_along(block, axis, distance):
    devices = range(lax.axis_size(axis))
    route = [((i - distance) % len(devices), i) for i in devices]
    return lax.ppermute(block, axis, route)


def padded_2(value, sides, width):
    for axis, dim in sides:
        size, length = (lax.axis_size(axis), value.shape[dim])
        up = [(i, (i + 1) % size) for i in range(size)]
        down = [(j, i) for i, j in up]
        last = lax.slice_in_dim(value, length - width, length, axis=dim)
        leading = lax.slice_in_dim(value, 0, width, axis=dim)
        before = lax.ppermute(last, axis, up)
        after = lax.ppermute(leading, axis, down)
        value = jnp.concatenate([before, value, after], axis=dim)
    return value


def jackson(count):
    angle = math.pi / (count + 1)
    return [
        ((count - m + 1) * math.cos(angle * m) + math.sin(angle * m) / math.tan(angle))
        / (count + 1)
        for m in range(count)
    ]


def weights_at(energy, count):
    gains = jnp.array(jackson(count), dtype=jnp.float32)
    theta = jnp.arccos(energy)
    orders = jnp.arange(count).astype(jnp.float32)
    first = 1.0 - theta / math.pi
    rest = -2.0 * jnp.sin(orders * theta) / (math.pi * jnp.maximum(orders, 1.0))
    return jnp.where(orders == 0.0, first, rest) * gains


def couplings(stacking, interlayer):
    coup_aa = jnp.zeros(stacking.shape, jnp.float32)
    coup_ab = jnp.zeros(stacking.shape, jnp.float32)
    for klass in range(interlayer.shape[1]):
        hit = stacking == klass
        coup_aa = coup_aa + jnp.where(hit, interlayer[0, klass], 0.0)
        coup_ab = coup_ab + jnp.where(hit, interlayer[1, klass], 0.0)
    return (coup_aa, coup_ab)


def remote_rows(b_rows, lower_bond):
    below = passed_along(b_rows[:, :, -1:, :], "dom", 1)
    b_down = jnp.concatenate([below, b_rows[:, :, :-1, :]], axis=2)
    above = passed_along(lower_bond[:, :, :1, :], "dom", -1)
    lower_up = jnp.concatenate([lower_bond[:, :, 1:, :], above], axis=2)
    return (b_down, lower_up)


def apply_ham(field, hoppings, coup_aa, coup_ab, potential, neighbours):
    a_rows = field[0::2]
    b_rows = field[1::2]
    t_zero = hoppings[:, 0][:, None]
    t_one = hoppings[:, 1][:, None]
    t_two = hoppings[:, 2][:, None]
    lower_bond = t_two * a_rows
    b_down, lower_up = neighbours(b_rows, lower_bond)
    h_a = -(t_zero * b_rows + t_one * jnp.roll(b_rows, 1, axis=3) + t_two * b_down)
    h_b = -(t_zero * a_rows + jnp.roll(t_one * a_rows, -1, axis=3) + lower_up)
    h_a1 = h_a[0] + coup_aa * a_rows[1] + coup_ab * b_rows[1]
    h_a2 = h_a[1] + coup_aa * a_rows[0]
    h_b2 = h_b[1] + coup_ab * a_rows[0]
    total = jnp.stack([h_a1, h_b[0], h_a2, h_b2]) + potential[:, None] * field
    return total / 8.0


def recursion(vectors, field, hoppings, coup_aa, coup_ab, potential, neighbours):
    prev = field
    cur = apply_ham(field, hoppings, coup_aa, coup_ab, potential, neighbours)
    terms = [jnp.sum(vectors * vectors, axis=1), jnp.sum(vectors * cur, axis=1)]
    for step in range(CHEB - 1):
        nxt = 2.0 * apply_ham(cur, hoppings, coup_aa, coup_ab, potential, neighbours) - prev
        prev, cur = (cur, nxt)
        terms.append(jnp.sum(vectors * cur, axis=1))
    return terms


def combine(coeff, fields):
    result = coeff[0] * fields[0]
    for order in range(1, fields.shape[0]):
        result = result + coeff[order] * fields[order]
    return result


def per_device(vectors, hoppings, potential, stacking, interlayer, filling):
    coup_aa, coup_ab = couplings(stacking, interlayer)
    total_vectors = float(vectors.shape[1] * lax.axis_size("vec"))
    terms = recursion(vectors, vectors, hoppings, coup_aa, coup_ab, potential, remote_rows)
    local_moments = jnp.stack(terms) / total_vectors
    count_m = local_moments.shape[0]
    local_totals = jnp.sum(local_moments, axis=(1, 2, 3))
    sites_all = 4 * potential.shape[1] * potential.shape[2] * lax.axis_size("dom")
    target = filling[0] * float(sites_all)

    def bisect(step, carry):
        low, high = carry
        mid = 0.5 * (low + high)
        count = lax.psum(jnp.sum(weights_at(mid, count_m) * local_totals), ("dom", "vec"))
        below_goal = count < target
        return (jnp.where(below_goal, mid, low), jnp.where(below_goal, high, mid))

    low, high = lax.fori_loop(
        0, BISECT, bisect, (jnp.array(-1.0, jnp.float32), jnp.array(1.0, jnp.float32))
    )
    chem = 0.5 * (low + high)
    coeff = weights_at(chem, count_m)
    summed = lax.psum(local_moments, "vec")
    density = combine(coeff, summed)
    charge = jnp.sum(density - 0.5, axis=0)
    padded = padded_2(charge, (("dom", 0),), 1)
    near = padded[:-2] + padded[2:] + jnp.roll(charge, 1, axis=1) + jnp.roll(charge, -1, axis=1)
    return 3.0 * (density - 0.5) + 0.5 * charge + 0.25 * near


def solution(mesh):
    placed = (
        P(None, "vec", "dom", None),
        P(None, None, "dom", None),
        P(None, "dom", None),
        P("dom", None),
        P(),
        P(),
    )
    return jax.shard_map(
        per_device, mesh=mesh, in_specs=placed, out_specs=P(None, "dom", None), check_vma=False
    )
```

profile of v0, /device:TPU:1, one launch (start us, length us, event | category | flops | bytes accessed | tf_op | source)
XLA Modules:
  0.0 1334.7 jit_solution(3295207423575736823)
XLA Ops:
  6.5 1.2 slice_bitcast_fusion.2
  7.7 2.9 fusion.56
  10.7 2.2 collective-permute-start
  12.9 7.8 collective-permute-start.1
  21.4 5.2 select_add_fusion.1
  26.6 5.1 select_add_fusion
  32.8 1.5 copy-done
  34.4 2.3 fusion.13
  36.6 1.3 fusion.37
  38.0 1.5 broadcast_multiply_fusion
  39.5 1.0 fusion.55
  40.7 5.9 collective-permute-start.3
  48.0 2.1 fusion.18
  50.1 1.2 fusion.35
  51.3 1.9 fusion.4
  53.2 1.2 fusion.54
  54.6 6.1 collective-permute-start.5
  62.2 2.0 fusion.23
  64.2 1.3 fusion.33
  65.6 2.3 fusion.6
  67.9 1.2 fusion.53
  69.3 6.1 collective-permute-start.7
  76.7 2.0 fusion.28
  78.8 1.3 fusion.31
  80.1 3.5 fusion.10
  83.8 1.8 fusion.50
  86.3 1227.8 %while.13 = (s32[]{:T(128)}, f32[]{:T(128)}, f32[]{:T(128)}, f32[5]{0:T(128)S(1)}, f32[]{:T(128)}, /*index=5*/s32[]{:T(128)}, f32[5]{0:T(128)S(1)}, f32[]{:T(128)}, f32[]{:T(128)}, f32[]{:T(128)}) while((s32[]{:T(128)}, f32[]{:T(128)}, f32[]{:T(128)}, f32[5]{0:T(128)S(1)}, f32[]{:T(128)}, /*index=5*/s32[]{:T(128)}, ...), condition=%wide.region_9.10_spmd.clone, body=%wide.region_6.9_spmd.sunk.clone.sunk | while | flops 67 | bytes 300 | solution.py:119
  87.1 97.8 %psum.18 = f32[]{:T(128)} all-reduce(f32[]{:T(128)} %fusion.63), channel_id=1, replica_groups=mesh['dom'=64,'vec'=4] {'dom','vec'}, use_global_device_ids=true, to_apply=%region_8.8 | all-reduce | flops 1 | bytes 8 | tf_op jit(solution)/shard_map/while/body/eval_jaxpr/psum | solution.py:115
  186.4 74.0 %psum.18 = f32[]{:T(128)} all-reduce(f32[]{:T(128)} %fusion.63), channel_id=1, replica_groups=mesh['dom'=64,'vec'=4] {'dom','vec'}, use_global_device_ids=true, to_apply=%region_8.8 | all-reduce | flops 1 | bytes 8 | tf_op jit(solution)/shard_map/while/body/eval_jaxpr/psum | solution.py:115
  261.8 73.8 %psum.18 = f32[]{:T(128)} all-reduce(f32[]{:T(128)} %fusion.63), channel_id=1, replica_groups=mesh['dom'=64,'vec'=4] {'dom','vec'}, use_global_device_ids=true, to_apply=%region_8.8 | all-reduce | flops 1 | bytes 8 | tf_op jit(solution)/shard_map/while/body/eval_jaxpr/psum | solution.py:115
  337.1 73.8 %psum.18 = f32[]{:T(128)} all-reduce(f32[]{:T(128)} %fusion.63), channel_id=1, replica_groups=mesh['dom'=64,'vec'=4] {'dom','vec'}, use_global_device_ids=true, to_apply=%region_8.8 | all-reduce | flops 1 | bytes 8 | tf_op jit(solution)/shard_map/while/body/eval_jaxpr/psum | solution.py:115
  412.3 73.8 %psum.18 = f32[]{:T(128)} all-reduce(f32[]{:T(128)} %fusion.63), channel_id=1, replica_groups=mesh['dom'=64,'vec'=4] {'dom','vec'}, use_global_device_ids=true, to_apply=%region_8.8 | all-reduce | flops 1 | bytes 8 | tf_op jit(solution)/shard_map/while/body/eval_jaxpr/psum | solution.py:115
  487.5 73.8 %psum.18 = f32[]{:T(128)} all-reduce(f32[]{:T(128)} %fusion.63), channel_id=1, replica_groups=mesh['dom'=64,'vec'=4] {'dom','vec'}, use_global_device_ids=true, to_apply=%region_8.8 | all-reduce | flops 1 | bytes 8 | tf_op jit(solution)/shard_map/while/body/eval_jaxpr/psum | solution.py:115
  562.8 73.8 %psum.18 = f32[]{:T(128)} all-reduce(f32[]{:T(128)} %fusion.63), channel_id=1, replica_groups=mesh['dom'=64,'vec'=4] {'dom','vec'}, use_global_device_ids=true, to_apply=%region_8.8 | all-reduce | flops 1 | bytes 8 | tf_op jit(solution)/shard_map/while/body/eval_jaxpr/psum | solution.py:115
  638.0 73.8 %psum.18 = f32[]{:T(128)} all-reduce(f32[]{:T(128)} %fusion.63), channel_id=1, replica_groups=mesh['dom'=64,'vec'=4] {'dom','vec'}, use_global_device_ids=true, to_apply=%region_8.8 | all-reduce | flops 1 | bytes 8 | tf_op jit(solution)/shard_map/while/body/eval_jaxpr/psum | solution.py:115
  713.2 73.8 %psum.18 = f32[]{:T(128)} all-reduce(f32[]{:T(128)} %fusion.63), channel_id=1, replica_groups=mesh['dom'=64,'vec'=4] {'dom','vec'}, use_global_device_ids=true, to_apply=%region_8.8 | all-reduce | flops 1 | bytes 8 | tf_op jit(solution)/shard_map/while/body/eval_jaxpr/psum | solution.py:115
  788.4 73.8 %psum.18 = f32[]{:T(128)} all-reduce(f32[]{:T(128)} %fusion.63), channel_id=1, replica_groups=mesh['dom'=64,'vec'=4] {'dom','vec'}, use_global_device_ids=true, to_apply=%region_8.8 | all-reduce | flops 1 | bytes 8 | tf_op jit(solution)/shard_map/while/body/eval_jaxpr/psum | solution.py:115
  863.6 73.8 %psum.18 = f32[]{:T(128)} all-reduce(f32[]{:T(128)} %fusion.63), channel_id=1, replica_groups=mesh['dom'=64,'vec'=4] {'dom','vec'}, use_global_device_ids=true, to_apply=%region_8.8 | all-reduce | flops 1 | bytes 8 | tf_op jit(solution)/shard_map/while/body/eval_jaxpr/psum | solution.py:115
  938.9 73.8 %psum.18 = f32[]{:T(128)} all-reduce(f32[]{:T(128)} %fusion.63), channel_id=1, replica_groups=mesh['dom'=64,'vec'=4] {'dom','vec'}, use_global_device_ids=true, to_apply=%region_8.8 | all-reduce | flops 1 | bytes 8 | tf_op jit(solution)/shard_map/while/body/eval_jaxpr/psum | solution.py:115
  1014.1 73.8 %psum.18 = f32[]{:T(128)} all-reduce(f32[]{:T(128)} %fusion.63), channel_id=1, replica_groups=mesh['dom'=64,'vec'=4] {'dom','vec'}, use_global_device_ids=true, to_apply=%region_8.8 | all-reduce | flops 1 | bytes 8 | tf_op jit(solution)/shard_map/while/body/eval_jaxpr/psum | solution.py:115
  1089.3 73.8 %psum.18 = f32[]{:T(128)} all-reduce(f32[]{:T(128)} %fusion.63), channel_id=1, replica_groups=mesh['dom'=64,'vec'=4] {'dom','vec'}, use_global_device_ids=true, to_apply=%region_8.8 | all-reduce | flops 1 | bytes 8 | tf_op jit(solution)/shard_map/while/body/eval_jaxpr/psum | solution.py:115
  1164.5 73.8 %psum.18 = f32[]{:T(128)} all-reduce(f32[]{:T(128)} %fusion.63), channel_id=1, replica_groups=mesh['dom'=64,'vec'=4] {'dom','vec'}, use_global_device_ids=true, to_apply=%region_8.8 | all-reduce | flops 1 | bytes 8 | tf_op jit(solution)/shard_map/while/body/eval_jaxpr/psum | solution.py:115
  1239.8 73.8 %psum.18 = f32[]{:T(128)} all-reduce(f32[]{:T(128)} %fusion.63), channel_id=1, replica_groups=mesh['dom'=64,'vec'=4] {'dom','vec'}, use_global_device_ids=true, to_apply=%region_8.8 | all-reduce | flops 1 | bytes 8 | tf_op jit(solution)/shard_map/while/body/eval_jaxpr/psum | solution.py:115
  1315.0 5.1 fusion.51
  1320.1 1.2 collective-permute-start.8
  1321.3 4.6 collective-permute-start.9
  1326.0 0.9 collective-permute-done.8
  1327.0 0.9 fusion.44
  (77 shorter events, 18.5 us)
Async XLA Ops:
  6.5 1308.4 %all-reduce.2.cloned.1.call-start = ((), (), s32[]{:S(2)}) async-start(), calls=%async_computation | async-start | bytes 5242880 | tf_op jit(solution)/shard_map/psum | solution.py:124
  7.7 13.0 copy-start.3
  7.7 13.7 %copy-start.2 = (s32[32,1024]{1,0:T(8,128)S(1)}, s32[32,1024]{1,0:T(8,128)}, u32[]{:S(2)}) copy-start(s32[32,1024]{1,0:T(8,128)} %param.13) | copy-start | bytes 393220
  10.7 22.1 %collective-permute-start = (f32[2,8,1,1024]{3,2,1,0:T(1,128)S(1)}, f32[2,8,1,1024]{3,2,1,0:T(1,128)S(1)}, u32[]{:S(2)}, u32[]{:S(2)}) collective-permute-start(f32[2,8,1,1024]{3,2,1,0:T(1,128)S(1)} %slice.445), channel_id=1, source_target_pairs={{252,0},{0,4},{4,8},{8,12},{12,16},{16,20},{20,24},{24,28},{28,32}... | collective-permute-start | bytes 196616 | tf_op jit(solution)/shard_map/ppermute | solution.py:15
  12.9 19.9 %collective-permute-start.1 = (f32[2,8,1,1024]{3,2,1,0:T(1,128)S(1)}, f32[2,8,1,1024]{3,2,1,0:T(1,128)S(1)}, u32[]{:S(2)}, u32[]{:S(2)}) collective-permute-start(f32[2,8,1,1024]{3,2,1,0:T(1,128)S(1)} %slice.453), channel_id=1, source_target_pairs={{4,0},{8,4},{12,8},{16,12},{20,16},{24,20},{28,24},{32,28},{36,32}... | collective-permute-start | bytes 196616 | tf_op jit(solution)/shard_map/ppermute | solution.py:15
  32.2 2.2 copy-start
  36.6 1.4 copy-start.1
  40.6 7.4 collective-permute-start.2
  40.7 7.3 collective-permute-start.3
  54.5 7.7 collective-permute-start.4
  54.6 7.6 collective-permute-start.5
  69.2 7.5 collective-permute-start.6
  69.3 7.4 collective-permute-start.7
  85.7 0.7 copy-start.4
  1320.1 6.8 collective-permute-start.8
  1321.3 5.6 collective-permute-start.9
Sparse Core Ops, SparseCore 0:
  85.8 75.6 all-reduce.1
where the time goes:
time: 1340 us; the launch traced here: 1330 us
  blocking collectives  1200 us (90%)
  other arithmetic  58 us (4%)
  starting transfers between devices  34 us (3%)
  between operations  14.6 us (1%)
    psum x16, blocking collectives, bisect(): lax.psum(jnp.sum(weights_at(mid, count_m) * local_totals), ('dom', 'vec'))  1200 us
    ppermute x8, starting transfers between devices, passed_along(): return lax.ppermute(block, axis, route)  28.3 us
  transfers between devices with their start and end apart: 11, of which 4 were waited for; matrix products, arithmetic and copies ran while one was open for 2% of the time, Pallas kernels for 0%

commit v1 on v0

v1 whole, which is shorter than its diff:
```python
import functools
import math

import jax
import jax.numpy as jnp
from jax import lax
from jax.experimental import pallas as pl
from jax.experimental.pallas import tpu as pltpu
from jax.sharding import PartitionSpec as P

CHEB = 4
BISECT = 16
LANES = 128
SUB = 8
REC = 48
COEF = 32
F32 = jnp.float32
VMEM_LIMIT = 44 * 1024 * 1024


def jackson(count):
    angle = math.pi / (count + 1)
    return [
        ((count - m + 1) * math.cos(angle * m) + math.sin(angle * m) / math.tan(angle))
        / (count + 1)
        for m in range(count)
    ]


def lane_is(where, shape=(SUB, LANES)):
    return lax.broadcasted_iota(jnp.int32, shape, 1) == where


def from_left(here, left):
    return jnp.where(lane_is(0, here.shape), left, here)


def from_right(here, right):
    return jnp.where(lane_is(LANES - 1, here.shape), right, here)


def roll_left(x):
    return pltpu.roll(x, LANES - 1, 1)


def roll_right(x):
    return pltpu.roll(x, 1, 1)


def pick(classes, table):
    values = list(table)
    bit = 1
    while len(values) > 1:
        hit = (classes & bit) != 0
        values = [jnp.where(hit, values[i + 1], values[i]) for i in range(0, len(values), 2)]
        bit *= 2
    return values[0]


def hop_apply(a, b, a_right, b_left, a_down, b_up, coef, t2_down):
    pot = coef[8:12]
    aa, ab = coef[12:14]
    out = []
    for layer in range(2):
        t0, t1, t2, t1r = coef[4 * layer : 4 * layer + 4]
        h_a = t0 * b[layer] + t1 * b_left[layer] + t2 * b_up[layer] + pot[2 * layer] * a[layer]
        h_b = (
            t0 * a[layer]
            + t1r * a_right[layer]
            + t2_down[layer] * a_down[layer]
            + pot[2 * layer + 1] * b[layer]
        )
        out.append([h_a, h_b])
    out[0][0] = out[0][0] + aa * a[1] + ab * b[1]
    out[1][0] = out[1][0] + aa * a[0]
    out[1][1] = out[1][1] + ab * a[0]
    return [out[0][0], out[0][1], out[1][0], out[1][1]]


def pack_kernel(rows, chunks, idx, inter, vec, hop, pot, stk, long_out, short_out, extra,
                v8, h8, p8, s8, rec, sems):
    copies = []
    n = 0
    for band in range(2):
        at = pl.ds(band * (rows - SUB), SUB)
        for c in range(chunks):
            lanes = pl.ds(c * LANES, LANES)
            for src, dst in (
                (hop.at[:, at, lanes], h8.at[band, c]),
                (pot.at[:, at, lanes], p8.at[band, c]),
                (stk.at[at, lanes], s8.at[band, c]),
                (vec.at[:, at, lanes], v8.at[band, c]),
            ):
                copies.append(pltpu.make_async_copy(src, dst, sems.at[n]))
                n += 1
    for copy in copies:
        copy.start()
    for copy in copies:
        copy.wait()
    nf = vec.shape[0]
    flat = v8.reshape(2, chunks, nf * SUB, LANES)
    odd = idx[0]
    outs = []
    for band in range(2):
        for c in range(chunks):
            first = 0 if band == 0 else SUB - 4
            for r in range(4):
                for s in range(nf // SUB):
                    rec[band, c, pl.ds(r * REC + s * SUB, SUB), :] = flat[
                        band, c, pl.ds(s * SUB * SUB + first + r, SUB, stride=SUB), :
                    ]
            after = (c + 1) % chunks
            coef = []
            for layer in range(2):
                for k in range(3):
                    coef.append(h8[band, c, 3 * layer + k] * -0.25)
                    if k == 1:
                        here = h8[band, c, 3 * layer + 1]
                        there = h8[band, after, 3 * layer + 1]
                        shifted = from_right(roll_left(here), roll_left(there)) * -0.25
                coef.append(shifted)
            for s in range(4):
                coef.append(p8[band, c, s] * 0.25)
            classes = s8[band, c]
            for w in range(2):
                table = [inter[w, k] * 0.25 for k in range(inter.shape[1])]
                coef.append(pick(classes, table))
            for k, value in enumerate(coef):
                rec[band, c, pl.ds(COEF + k, 4, stride=REC), :] = value[first : first + 4]
            zero = jnp.zeros((4, LANES), F32)
            for k in range(len(coef), REC - COEF):
                rec[band, c, pl.ds(COEF + k, 4, stride=REC), :] = zero
        message = rec.at[band, :, pl.ds(band * REC, 3 * REC)]
        spare = rec.at[band, :, pl.ds((1 - band) * 3 * REC, REC)]
        away = pltpu.make_async_copy(spare, extra.at[band], sems.at[n])
        away.start()
        outs.append(away)
        n += 1

        @pl.when(odd == band)
        def _():
            pltpu.make_async_copy(message, long_out, sems.at[n]).start()

        @pl.when(odd != band)
        def _():
            pltpu.make_async_copy(message, short_out, sems.at[n]).start()

        outs.append(pltpu.make_async_copy(message, long_out, sems.at[n]))
        n += 1
    for copy in outs:
        copy.wait()


def pack(idx, inter, vec, hop, pot, stk):
    fields, rows, width = vec.shape
    chunks = width // LANES
    any_ = pl.BlockSpec(memory_space=pl.ANY)
    smem = pl.BlockSpec(memory_space=pltpu.SMEM)
    message = jax.ShapeDtypeStruct((chunks, 3 * REC, LANES), F32)
    n_in = 2 * chunks * 4
    return pl.pallas_call(
        functools.partial(pack_kernel, rows, chunks),
        out_shape=[message, message, jax.ShapeDtypeStruct((2, chunks, REC, LANES), F32)],
        in_specs=[smem, smem, any_, any_, any_, any_],
        out_specs=[any_, any_, any_],
        scratch_shapes=[
            pltpu.VMEM((2, chunks, fields, SUB, LANES), F32),
            pltpu.VMEM((2, chunks, 6, SUB, LANES), F32),
            pltpu.VMEM((2, chunks, 4, SUB, LANES), F32),
            pltpu.VMEM((2, chunks, SUB, LANES), jnp.int32),
            pltpu.VMEM((2, chunks, 4 * REC, LANES), F32),
            pltpu.SemaphoreType.DMA((n_in + 4,)),
        ],
        compiler_params=pltpu.CompilerParams(vmem_limit_bytes=VMEM_LIMIT),
        cost_estimate=pl.CostEstimate(flops=1_000_000, bytes_accessed=4_000_000, transcendentals=0),
        name="pack",
    )(idx, inter, vec, hop, pot, stk)


PAD = 8


def interior_kernel(rows, chunks, nvec, group, idx, inter, vec, hop, pot, stk, keep, send, tot,
                    x, t1, t2, hp, pt, st, ww, mom, sems):
    halves = nvec // group
    copies = []
    n = 0
    for c in range(chunks):
        lanes = pl.ds(c * LANES, LANES)
        for src, dst in (
            (hop.at[:, :, :, lanes], hp.at[:, 0:3, c, pl.ds(0, rows)]),
            (pot.at[:, :, lanes], pt.at[:, c]),
            (stk.at[:, lanes], st.at[c]),
        ):
            copies.append(pltpu.make_async_copy(src, dst, sems.at[n]))
            n += 1
    late = []
    for q in range(halves):
        part = []
        for c in range(chunks):
            lanes = pl.ds(c * LANES, LANES)
            part.append(
                pltpu.make_async_copy(
                    vec.at[:, pl.ds(q * group, group), :, lanes],
                    x.at[:, pl.ds(q * group, group), c, pl.ds(PAD, rows)],
                    sems.at[n],
                )
            )
            n += 1
        late.append(part)
    for copy in copies + [copy for part in late for copy in part]:
        copy.start()
    for copy in copies:
        copy.wait()

    groups = rows // SUB

    def prepare(g, carry):
        at = pl.ds(pl.multiple_of(g * SUB, SUB), SUB)
        for layer in range(2):
            rolled = {}
            for c in range(chunks):
                rolled[c] = roll_left(hp[layer, 1, c, at, :])
            for c in range(chunks):
                hp[layer, 3, c, at, :] = (
                    from_right(rolled[c], rolled[(c + 1) % chunks]) * -0.25
                )
            for k in range(3):
                for c in range(chunks):
                    hp[layer, k, c, at, :] = hp[layer, k, c, at, :] * -0.25
        for c in range(chunks):
            for s in range(4):
                pt[s, c, at, :] = pt[s, c, at, :] * 0.25
            classes = st[c, at, :]
            for w in range(2):
                table = [inter[w, k] * 0.25 for k in range(inter.shape[1])]
                ww[w, c, at, :] = pick(classes, table)
        return carry

    lax.fori_loop(0, groups, prepare, 0)

    def sweep(order, q, source, before, target):
        def load(ref, s, v, c, at):
            return ref[s, v, c, at, :]

        def body(g, carry):
            base = pl.multiple_of(g * SUB, SUB)
            mid = pl.ds(base + PAD, SUB)
            up = pl.ds(base + PAD - 1, SUB)
            down = pl.ds(base + PAD + 1, SUB)
            plain = pl.ds(base, SUB)
            plain_down = pl.ds(base + 1, SUB)
            vs = range(group)
            src, off = source

            def rolled(site, c, fn):
                return [fn(load(src, site, v + off, c, mid)) for v in vs]

            b_prev = [rolled(2 * l + 1, chunks - 1, roll_right) for l in range(2)]
            a_here = [rolled(2 * l, 0, roll_left) for l in range(2)]
            for c in range(chunks):
                nxt = (c + 1) % chunks
                a_next = [rolled(2 * l, nxt, roll_left) for l in range(2)]
                b_here = [rolled(2 * l + 1, c, roll_right) for l in range(2)]
                coef = []
                for layer in range(2):
                    for k in range(4):
                        coef.append(hp[layer, k, c, plain, :])
                for s in range(4):
                    coef.append(pt[s, c, plain, :])
                for w in range(2):
                    coef.append(ww[w, c, plain, :])
                t2_down = [hp[layer, 2, c, plain_down, :] for layer in range(2)]
                sums = [None] * 4
                squares = [None] * 4
                for v in vs:
                    a = [load(src, 2 * l, v + off, c, mid) for l in range(2)]
                    b = [load(src, 2 * l + 1, v + off, c, mid) for l in range(2)]
                    a_down = [load(src, 2 * l, v + off, c, down) for l in range(2)]
                    b_up = [load(src, 2 * l + 1, v + off, c, up) for l in range(2)]
                    a_right = [from_right(a_here[l][v], a_next[l][v]) for l in range(2)]
                    b_left = [from_left(b_here[l][v], b_prev[l][v]) for l in range(2)]
                    new = hop_apply(a, b, a_right, b_left, a_down, b_up, coef, t2_down)
                    for s in range(4):
                        if order == 1:
                            value = new[s] * 0.5
                        else:
                            ref, shift = before
                            value = new[s] - load(ref, s, v + shift, c, mid)
                        if target is not None:
                            target[s, v, c, mid, :] = value
                        first = load(x, s, v + q * group, c, mid)
                        term = first * value
                        sums[s] = term if sums[s] is None else sums[s] + term
                        if order == 1:
                            sq = first * first
                            squares[s] = sq if squares[s] is None else squares[s] + sq
                for s in range(4):
                    if q > 0:
                        sums[s] = sums[s] + mom[order, s, c, plain, :]
                    mom[order, s, c, plain, :] = sums[s]
                    if order == 1:
                        if q > 0:
                            squares[s] = squares[s] + mom[0, s, c, plain, :]
                        mom[0, s, c, plain, :] = squares[s]
                a_here = a_next
                b_prev = b_here
            return carry

        lax.fori_loop(0, groups, body, 0)

    for q in range(halves):
        for copy in late[q]:
            copy.wait()
        start = (x, q * group)
        sweep(1, q, start, None, t1)
        sweep(2, q, (t1, 0), start, t2)
        sweep(3, q, (t2, 0), (t1, 0), t1)
        sweep(4, q, (t1, 0), (t2, 0), None)

    half = rows // 2
    core = idx[1]
    kept = pltpu.make_async_copy(
        mom.at[:, :, :, pl.ds(pl.multiple_of(core * half, SUB), half)], keep, sems.at[n]
    )
    sent = pltpu.make_async_copy(
        mom.at[:, :, :, pl.ds(pl.multiple_of((1 - core) * half, SUB), half)], send, sems.at[n + 1]
    )
    kept.start()
    sent.start()

    def add_up(g, carry):
        base = pl.multiple_of(g * SUB, SUB)
        row = lax.broadcasted_iota(jnp.int32, (SUB, LANES), 0) + base
        inside = (row >= 2) & (row < rows - 2)
        result = []
        for m in range(CHEB + 1):
            acc = None
            for s in range(4):
                for c in range(chunks):
                    value = mom[m, s, c, pl.ds(base, SUB), :]
                    acc = value if acc is None else acc + value
            result.append(carry[m] + jnp.where(inside, acc, 0.0))
        return tuple(result)

    sums = lax.fori_loop(
        0, groups, add_up, tuple(jnp.zeros((SUB, LANES), F32) for _ in range(CHEB + 1))
    )
    for m in range(CHEB + 1):
        tot[m] = sums[m]
    kept.wait()
    sent.wait()


def interior(idx, inter, vec, hop, pot, stk):
    _, nvec, rows, width = vec.shape
    chunks = width // LANES
    group = 4
    any_ = pl.BlockSpec(memory_space=pl.ANY)
    smem = pl.BlockSpec(memory_space=pltpu.SMEM)
    half = jax.ShapeDtypeStruct((CHEB + 1, 4, chunks, rows // 2, LANES), F32)
    n = chunks * (3 + nvec // group) + 2
    return pl.pallas_call(
        functools.partial(interior_kernel, rows, chunks, nvec, group),
        out_shape=[half, half, jax.ShapeDtypeStruct((CHEB + 1, SUB, LANES), F32)],
        in_specs=[smem, smem, any_, any_, any_, any_],
        out_specs=[any_, any_, pl.BlockSpec(memory_space=pltpu.VMEM)],
        scratch_shapes=[
            pltpu.VMEM((4, nvec, chunks, rows + 2 * PAD, LANES), F32),
            pltpu.VMEM((4, group, chunks, rows + 2 * PAD, LANES), F32),
            pltpu.VMEM((4, group, chunks, rows + 2 * PAD, LANES), F32),
            pltpu.VMEM((2, 4, chunks, rows + SUB, LANES), F32),
            pltpu.VMEM((4, chunks, rows, LANES), F32),
            pltpu.VMEM((chunks, rows, LANES), jnp.int32),
            pltpu.VMEM((2, chunks, rows, LANES), F32),
            pltpu.VMEM((CHEB + 1, 4, chunks, rows, LANES), F32),
            pltpu.SemaphoreType.DMA((n,)),
        ],
        compiler_params=pltpu.CompilerParams(vmem_limit_bytes=VMEM_LIMIT),
        cost_estimate=pl.CostEstimate(
            flops=60_000_000, bytes_accessed=9_000_000, transcendentals=0
        ),
        name="interior",
    )(idx, inter, vec, hop, pot, stk)


WIN = 7


def edges_kernel(chunks, parts, idx, own_long, own_short, got_long, got_short, extra, part, keep,
                 send, tot, w, t1, t2, res, sems):
    odd, core = idx[0], idx[1]
    three = 3 * REC

    def both(refs, when, dst, sem):
        @pl.when(when)
        def _():
            pltpu.make_async_copy(refs[0], dst, sem).start()

        @pl.when(jnp.logical_not(when))
        def _():
            pltpu.make_async_copy(refs[1], dst, sem).start()

        return pltpu.make_async_copy(refs[0], dst, sem)

    even = odd == 0
    guard = REC
    copies = [
        both((got_long, got_short), even, w.at[0, :, pl.ds(guard, three)], sems.at[0]),
        both((own_long, own_short), even, w.at[0, :, pl.ds(guard + three, three)], sems.at[1]),
        both((own_short, own_long), even, w.at[1, :, pl.ds(guard + REC, three)], sems.at[2]),
        both((got_short, got_long), even, w.at[1, :, pl.ds(guard + REC + three, three)], sems.at[3]),
    ]
    for band, place in ((0, 6), (1, 0)):
        copy = pltpu.make_async_copy(
            extra.at[band], w.at[band, :, pl.ds(guard + place * REC, REC)], sems.at[4 + band]
        )
        copy.start()
        copies.append(copy)
    for copy in copies:
        copy.wait()

    def sweep(order, first, last):
        def body(j, carry):
            band = lax.rem(j, 2)
            i = first + lax.div(j, 2)
            rec0 = guard + i * REC

            def here(ref, site, c, shift=0):
                if ref is w:
                    at = pl.multiple_of(rec0 + shift * REC + site * SUB, SUB)
                else:
                    at = pl.multiple_of((i + 1 + shift) * 32 + site * SUB, SUB)
                return ref[band, c, pl.ds(at, SUB), :]

            def coef_at(k, c, shift=0):
                at = rec0 + shift * REC + COEF + k
                return jnp.broadcast_to(w[band, c, pl.ds(at, 1), :], (SUB, LANES))

            source, before, target = {
                1: (w, None, t1),
                2: (t1, w, t2),
                3: (t2, t1, t1),
                4: (t1, t2, None),
            }[order]
            centre = order == 4
            b_prev = [roll_right(here(source, 2 * l + 1, chunks - 1)) for l in range(2)]
            a_here = [roll_left(here(source, 2 * l, 0)) for l in range(2)]
            for c in range(chunks):
                nxt = (c + 1) % chunks
                a_next = [roll_left(here(source, 2 * l, nxt)) for l in range(2)]
                b_here = [roll_right(here(source, 2 * l + 1, c)) for l in range(2)]
                coef = [coef_at(k, c) for k in range(14)]
                t2_down = [coef_at(4 * l + 2, c, 1) for l in range(2)]
                a = [here(source, 2 * l, c) for l in range(2)]
                b = [here(source, 2 * l + 1, c) for l in range(2)]
                a_down = [here(source, 2 * l, c, 1) for l in range(2)]
                b_up = [here(source, 2 * l + 1, c, -1) for l in range(2)]
                a_right = [from_right(a_here[l], a_next[l]) for l in range(2)]
                b_left = [from_left(b_here[l], b_prev[l]) for l in range(2)]
                new = hop_apply(a, b, a_right, b_left, a_down, b_up, coef, t2_down)
                for s in range(4):
                    if order == 1:
                        value = new[s] * 0.5
                    else:
                        value = new[s] - here(before, s, c)
                    if target is not None:
                        at = pl.multiple_of((i + 1) * 32 + s * SUB, SUB)
                        target[band, c, pl.ds(at, SUB), :] = value
                    new[s] = value
                if centre:
                    moments(band, i, c, 4, new, here)
                a_here = a_next
                b_prev = b_here
            return carry

        lax.fori_loop(0, 2 * (last - first + 1), body, 0)

    def moments(band, i, c, order, values, here):
        for s in range(4):
            first = here(w, s, c)
            term = jnp.sum(first * values[s], axis=0, keepdims=True)
            res[band, i - 2, c, pl.ds(order * 4 + s, 1), :] = term

    def collect(order, ref):
        def body(j, carry):
            band = lax.rem(j, 2)
            i = 2 + lax.div(j, 2)

            def here(source, site, c):
                at = pl.multiple_of(guard + i * REC + site * SUB, SUB)
                return source[band, c, pl.ds(at, SUB), :]

            for c in range(chunks):
                values = []
                for s in range(4):
                    if ref is w:
                        values.append(here(w, s, c))
                    else:
                        at = pl.multiple_of((i + 1) * 32 + s * SUB, SUB)
                        values.append(ref[band, c, pl.ds(at, SUB), :])
                moments(band, i, c, order, values, here)
            return carry

        lax.fori_loop(0, 6, body, 0)

    collect(0, w)
    sweep(1, 0, 6)
    collect(1, t1)
    sweep(2, 1, 5)
    collect(2, t2)
    sweep(3, 1, 5)
    collect(3, t1)
    sweep(4, 2, 4)
    out = [
        pltpu.make_async_copy(res.at[core], keep, sems.at[6]),
        pltpu.make_async_copy(res.at[1 - core], send, sems.at[7]),
    ]
    for copy in out:
        copy.start()
    lane = lax.broadcasted_iota(jnp.int32, (SUB, LANES), 1)
    row = jnp.zeros((SUB, LANES), F32)
    for m in range(CHEB + 1):
        acc = part[m]
        inner = None
        for band in range(2):
            for r in ((1, 2), (0, 1))[band]:
                for c in range(chunks):
                    value = res[band, r, c, pl.ds(4 * m, 4), :]
                    inner = value if inner is None else inner + value
        total = jnp.sum(acc) + jnp.sum(inner)
        row = jnp.where(lane == m, total, row)
    for k in range(parts // SUB):
        tot[pl.ds(k * SUB, SUB), :] = row
    for copy in out:
        copy.wait()


def edges(idx, own_long, own_short, got_long, got_short, extra, part, parts):
    chunks = own_long.shape[0]
    any_ = pl.BlockSpec(memory_space=pl.ANY)
    smem = pl.BlockSpec(memory_space=pltpu.SMEM)
    vmem = pl.BlockSpec(memory_space=pltpu.VMEM)
    edge = jax.ShapeDtypeStruct((3, chunks, 24, LANES), F32)
    return pl.pallas_call(
        functools.partial(edges_kernel, chunks, parts),
        out_shape=[edge, edge, jax.ShapeDtypeStruct((parts, LANES), F32)],
        in_specs=[smem, any_, any_, any_, any_, any_, vmem],
        out_specs=[any_, any_, vmem],
        scratch_shapes=[
            pltpu.VMEM((2, chunks, (WIN + 2) * REC, LANES), F32),
            pltpu.VMEM((2, chunks, (WIN + 2) * 32, LANES), F32),
            pltpu.VMEM((2, chunks, (WIN + 2) * 32, LANES), F32),
            pltpu.VMEM((2, 3, chunks, 24, LANES), F32),
            pltpu.SemaphoreType.DMA((8,)),
        ],
        compiler_params=pltpu.CompilerParams(vmem_limit_bytes=VMEM_LIMIT),
        cost_estimate=pl.CostEstimate(
            flops=20_000_000, bytes_accessed=4_000_000, transcendentals=0
        ),
        name="edges",
    )(idx, own_long, own_short, got_long, got_short, extra, part)


ACOS = (
    1.5707963050,
    -0.2145988016,
    0.0889789874,
    -0.0501743046,
    0.0308918810,
    -0.0170881256,
    0.0066700901,
    -0.0012624911,
)


def arccos(e):
    size = jnp.abs(e)
    poly = jnp.full_like(size, ACOS[-1])
    for value in ACOS[-2::-1]:
        poly = poly * size + value
    angle = jnp.sqrt(1.0 - size) * poly
    return jnp.where(e < 0.0, math.pi - angle, angle)


def weights_of(e):
    gain = jackson(CHEB + 1)
    sine = jnp.sqrt((1.0 - e) * (1.0 + e))
    square = e * e
    sines = [sine, 2.0 * e * sine, (4.0 * square - 1.0) * sine, 4.0 * e * (2.0 * square - 1.0) * sine]
    out = [gain[0] * (1.0 - arccos(e) / math.pi)]
    for m in range(1, CHEB + 1):
        out.append(sines[m - 1] * (-2.0 * gain[m] / (math.pi * m)))
    return out


def density_kernel(chunks, half, scale, sites, idx, filling, sums, mine, other, my_edge, other_edge,
                   out):
    core = idx[1]
    added = jnp.sum(sums[...], axis=0, keepdims=True) * scale
    lane = lax.broadcasted_iota(jnp.int32, (1, LANES), 1)
    totals = [jnp.sum(jnp.where(lane == m, added, 0.0)) for m in range(CHEB + 1)]
    target = filling[0] * sites

    point = (
        lax.broadcasted_iota(jnp.int32, (SUB, LANES), 0) * LANES
        + lax.broadcasted_iota(jnp.int32, (SUB, LANES), 1)
        + 1
    )
    ways = 2 ** (BISECT // 2)
    valid = point < ways
    low = jnp.float32(-1.0)
    step = 2.0
    for _ in range(2):
        step = step / ways
        mids = jnp.where(valid, low + point.astype(F32) * step, 0.0)
        count = None
        for value, total in zip(weights_of(mids), totals):
            term = value * total
            count = term if count is None else count + term
        below = jnp.sum(jnp.where(valid & (count < target), 1.0, 0.0))
        low = low + below * step
    chem = jnp.full((SUB, LANES), low + 0.5 * step, F32)
    weights = [value * scale for value in weights_of(chem)]

    for c in range(chunks):
        for s in range(4):
            for g in range(half // SUB):
                at = pl.ds(g * SUB, SUB)
                acc = None
                for m in range(CHEB + 1):
                    term = weights[m] * (mine[m, s, c, at, :] + other[m, s, c, at, :])
                    acc = term if acc is None else acc + term
                out[c, pl.ds(s * half + g * SUB, SUB), :] = acc
        rows = []
        for r in range(3):
            acc = None
            for m in range(CHEB + 1):
                at = pl.ds(4 * m, 4)
                term = weights[m][0:4] * (my_edge[r, c, at, :] + other_edge[r, c, at, :])
                acc = term if acc is None else acc + term
            rows.append(acc)
        halo = jnp.where(core == 0, rows[0], rows[2])
        out[c, pl.ds(4 * half, SUB), :] = jnp.broadcast_to(
            jnp.sum(halo, axis=0, keepdims=True), (SUB, LANES)
        )

        @pl.when(core == 0)
        def _():
            for s in range(4):
                out[c, pl.ds(s * half, 1), :] = rows[1][s : s + 1]
                out[c, pl.ds(s * half + 1, 1), :] = rows[2][s : s + 1]

        @pl.when(core != 0)
        def _():
            for s in range(4):
                out[c, pl.ds(s * half + half - 2, 1), :] = rows[0][s : s + 1]
                out[c, pl.ds(s * half + half - 1, 1), :] = rows[1][s : s + 1]


def density(idx, filling, sums, mine, other, my_edge, other_edge, vectors, sites):
    _, _, chunks, half, _ = mine.shape
    smem = pl.BlockSpec(memory_space=pltpu.SMEM)
    vmem = pl.BlockSpec(memory_space=pltpu.VMEM)
    return pl.pallas_call(
        functools.partial(density_kernel, chunks, half, 1.0 / vectors, float(sites)),
        out_shape=jax.ShapeDtypeStruct((chunks, 4 * half + SUB, LANES), F32),
        in_specs=[smem, smem, vmem, vmem, vmem, vmem, vmem],
        out_specs=vmem,
        compiler_params=pltpu.CompilerParams(vmem_limit_bytes=VMEM_LIMIT),
        cost_estimate=pl.CostEstimate(flops=2_000_000, bytes_accessed=4_000_000, transcendentals=0),
        name="density",
    )(idx, filling, sums, mine, other, my_edge, other_edge)


def potential_kernel(chunks, half, idx, mine, other, out, charge):
    first = idx[1] == 0
    guard = SUB

    def rows_of(ref, c):
        total = None
        for s in range(4):
            value = ref[c, pl.ds(s * half, half), :]
            total = value if total is None else total + value
        return total - 2.0

    for c in range(chunks):
        m, o = rows_of(mine, c), rows_of(other, c)
        charge[c, pl.ds(guard, half), :] = jnp.where(first, m, o)
        charge[c, pl.ds(guard + half, half), :] = jnp.where(first, o, m)
        m, o = (ref[c, pl.ds(4 * half, 1), :] - 2.0 for ref in (mine, other))
        charge[c, pl.ds(guard - 1, 1), :] = jnp.where(first, m, o)
        charge[c, pl.ds(guard + 2 * half, 1), :] = jnp.where(first, o, m)
    for g in range(2 * half // SUB):
        at = pl.ds(guard + g * SUB, SUB)
        for c in range(chunks):
            here = charge[c, at, :]
            left = from_left(roll_right(here), roll_right(charge[(c - 1) % chunks, at, :]))
            right = from_right(roll_left(here), roll_left(charge[(c + 1) % chunks, at, :]))
            near = (
                charge[c, pl.ds(guard + g * SUB - 1, SUB), :]
                + charge[c, pl.ds(guard + g * SUB + 1, SUB), :]
                + left
                + right
            )
            base = 0.5 * here + 0.25 * near
            in_first = g * SUB < half
            row = g * SUB - (0 if in_first else half)
            for s in range(4):
                rows = pl.ds(s * half + row, SUB)
                a, b = mine[c, rows, :], other[c, rows, :]
                dens = jnp.where(first, a, b) if in_first else jnp.where(first, b, a)
                out[s, pl.ds(g * SUB, SUB), pl.ds(c * LANES, LANES)] = 3.0 * (dens - 0.5) + base


def new_potential(idx, mine, other):
    chunks, height, _ = mine.shape
    half = (height - SUB) // 4
    smem = pl.BlockSpec(memory_space=pltpu.SMEM)
    vmem = pl.BlockSpec(memory_space=pltpu.VMEM)
    return pl.pallas_call(
        functools.partial(potential_kernel, chunks, half),
        out_shape=jax.ShapeDtypeStruct((4, 2 * half, chunks * LANES), F32),
        in_specs=[smem, vmem, vmem],
        out_specs=vmem,
        scratch_shapes=[pltpu.VMEM((chunks, 2 * half + 2 * SUB, LANES), F32)],
        compiler_params=pltpu.CompilerParams(vmem_limit_bytes=VMEM_LIMIT),
        cost_estimate=pl.CostEstimate(flops=1_000_000, bytes_accessed=2_000_000, transcendentals=0),
        name="new_potential",
    )(idx, mine, other)


def per_device(vectors, hoppings, potential, stacking, interlayer, filling):
    strips, ranks = lax.axis_size("dom"), lax.axis_size("vec")
    _, nvec, rows, width = vectors.shape
    dom, vec = lax.axis_index("dom"), lax.axis_index("vec")
    idx = jnp.stack([dom % 2, vec % 2]).astype(jnp.int32)
    long_way = [(i, (i - 1 if i % 2 == 0 else i + 1) % strips) for i in range(strips)]
    short_way = [(i, i ^ 1) for i in range(strips)]
    sibling = [(i, i ^ 1) for i in range(ranks)]
    across = [(i, i ^ 2) for i in range(ranks)]

    own_long, own_short, extra = pack(
        idx,
        interlayer,
        vectors.reshape(4 * nvec, rows, width),
        hoppings.reshape(6, rows, width),
        potential,
        stacking,
    )
    got_long = lax.ppermute(own_long, "dom", long_way)
    got_short = lax.ppermute(own_short, "dom", short_way)
    mine, yours, part = interior(idx, interlayer, vectors, hoppings, potential, stacking)
    my_edge, your_edge, totals = edges(
        idx, own_long, own_short, got_long, got_short, extra, part, strips * ranks
    )
    other = lax.ppermute(yours, "vec", sibling)
    other_edge = lax.ppermute(your_edge, "vec", sibling)
    sums = lax.all_to_all(totals, ("dom", "vec"), 0, 0, tiled=True)
    sites = 4 * rows * width * strips
    chip = density(
        idx, filling, sums, mine, other, my_edge, other_edge, nvec * ranks, sites
    )
    whole = chip + lax.ppermute(chip, "vec", across)
    return new_potential(idx, whole, lax.ppermute(whole, "vec", sibling))


def solution(mesh):
    placed = (
        P(None, "vec", "dom", None),
        P(None, None, "dom", None),
        P(None, "dom", None),
        P("dom", None),
        P(),
        P(),
    )
    return jax.shard_map(
        per_device, mesh=mesh, in_specs=placed, out_specs=P(None, "dom", None), check_vma=False
    )
```

time: 1340 us -> 95 us (0.07)
  blocking collectives: 1200 us -> 0 us
  other arithmetic: 58 us -> 0.11 us
  waiting for transfers between devices: 1.82 us -> 37.1 us
  Pallas kernels: 0 us -> 28.8 us
  between operations: 14.6 us -> 0.7 us
    psum x16 -> x0, blocking collectives: 1200 us -> none  [bisect(): lax.psum(jnp.sum(weights_at(mid, count_m) * local_totals), ('dom', 'vec'))]
    pallas_call x0 -> x5, Pallas kernels: none -> 28.8 us  [the longest x1 15.3 us: interior(): pl.pallas_call(functools.partial(interior_kernel, rows, chunks, nvec, gro...]
    ppermute x10 -> x6, waiting for transfers between devices: 1.8 us -> 24.6 us  [the longest x1 13.7 us: per_device(): got_long = lax.ppermute(own_long, 'dom', long_way)]
    reduce_sum x19 -> x0, other arithmetic: 21.1 us -> none  [the longest x16 10.7 us: bisect(): jnp.sum(weights_at(mid, count_m) * local_totals)]
    ppermute x10 -> x6, starting transfers between devices: 34 us -> 14.1 us  [the longest x1 7.3 us: per_device(): got_long = lax.ppermute(own_long, 'dom', long_way)]
    add x7 -> x1, other arithmetic: 16.4 us -> 0.03 us  [per_device(): whole = chip + lax.ppermute(chip, 'vec', across)]
  transfers between devices with their start and end apart: 11 -> 7, of which waited for: 4 -> 5; matrix products, arithmetic and copies ran while one was open for 2% -> 0% of each run, Pallas kernels for 0% -> 11%
where the time goes in v1:
time: 95 us; the launch traced here: 94.8 us
  waiting for transfers between devices  37.1 us (39%)
  Pallas kernels  28.8 us (30%)
  starting transfers between devices  22.2 us (23%)
  local copies, waits for them, and re-layouts  5.94 us (6%)
    pallas_call x1, Pallas kernels, interior(): pl.pallas_call(functools.partial(interior_kernel, rows, chunks, nvec, gro...  15.3 us
    ppermute x1, waiting for transfers between devices, per_device(): got_long = lax.ppermute(own_long, 'dom', long_way)  13.7 us
    all_to_all x1, waiting for transfers between devices, per_device(): sums = lax.all_to_all(totals, ('dom', 'vec'), 0, 0, tiled=True)  12.4 us
    ppermute x1, waiting for transfers between devices, per_device(): whole = chip + lax.ppermute(chip, 'vec', across)  8.8 us
    pallas_call x1, Pallas kernels, edges(): pl.pallas_call(functools.partial(edges_kernel, chunks, parts), out_shape=...  8.12 us
    all_to_all x1, starting transfers between devices, per_device(): sums = lax.all_to_all(totals, ('dom', 'vec'), 0, 0, tiled=True)  8.02 us
    ppermute x1, starting transfers between devices, per_device(): got_long = lax.ppermute(own_long, 'dom', long_way)  7.3 us
    unnamed x10, local copies, waits for them, and re-layouts  5.94 us
  transfers between devices with their start and end apart: 7, of which 5 were waited for; matrix products, arithmetic and copies ran while one was open for 0% of the time, Pallas kernels for 11%

profile of v1, /device:TPU:1, one launch (start us, length us, event | category | flops | bytes accessed | tf_op | source)
XLA Modules:
  0.0 94.8 jit_solution(16361663930903898922)
XLA Ops:
  0.0 0.1 pad_add_fusion.idx
  0.1 0.0 copy-start
  0.1 2.2 %copy-done = f32[4,8,32,1024]{3,2,1,0:T(8,128)S(1)} copy-done((f32[4,8,32,1024]{3,2,1,0:T(8,128)S(1)}, f32[4,8,32,1024]{3,2,1,0:T(8,128)}, u32[]{:S(2)}) %copy-start) | copy-done | bytes 4194328
  2.3 0.0 copy-start.1
  2.3 1.1 %copy-done.1 = f32[2,3,32,1024]{3,2,1,0:T(8,128)S(1)} copy-done((f32[2,3,32,1024]{3,2,1,0:T(8,128)S(1)}, f32[2,3,32,1024]{3,2,1,0:T(8,128)}, u32[]{:S(2)}) %copy-start.1) | copy-done | bytes 786456
  3.4 0.0 copy-start.2
  3.4 1.0 %copy-done.2 = f32[4,32,1024]{2,1,0:T(8,128)S(1)} copy-done((f32[4,32,1024]{2,1,0:T(8,128)S(1)}, f32[4,32,1024]{2,1,0:T(8,128)}, u32[]{:S(2)}) %copy-start.2) | copy-done | bytes 524312
  4.4 0.0 copy-start.3
  4.4 0.9 copy-done.3
  5.3 0.0 copy-start.4
  5.3 0.7 copy-done.4
  6.0 15.3 %interior.1 = (f32[5,4,8,16,128]{4,3,2,1,0:T(8,128)S(1)}, f32[5,4,8,16,128]{4,3,2,1,0:T(8,128)}, f32[5,8,128]{2,1,0:T(8,128)S(1)}) custom-call(s32[2]{0:T(128)S(1)} %pad_add_fusion.idx, f32[2,8]{1,0:T(2,128)S(1)} %copy-done.4, f32[4,8,32,1024]{3,2,1,0:T(8,128)S(1)} %copy-done, f32[2,3,32,1024]{3,2,1,0:T(8,128)S(1)} %copy-done.1, ...), custom_call_target="tpu_custom_call" | custom-call | flops 60000000 | bytes 9000000 | tf_op jit(solution)/shard_map/interior/pallas_call | solution.py:363
  21.4 3.3 %collective-permute-start.2 = (f32[5,4,8,16,128]{4,3,2,1,0:T(8,128)}, f32[5,4,8,16,128]{4,3,2,1,0:T(8,128)S(1)}, u32[]{:S(2)}, u32[]{:S(2)}) collective-permute-start(f32[5,4,8,16,128]{4,3,2,1,0:T(8,128)} %get-tuple-element.20), channel_id=1, source_target_pairs={{0,1},{1,0},{2,3},{3,2},{4,5},{5,4},{6,7},{7,6},{8,9},{9,8},{10,11... | collective-permute-start | bytes 3932168 | tf_op jit(solution)/shard_map/ppermute | solution.py:757
  24.7 2.5 %pack.1 = (f32[8,144,128]{2,1,0:T(8,128)S(1)}, f32[8,144,128]{2,1,0:T(8,128)S(1)}, f32[2,8,48,128]{3,2,1,0:T(8,128)S(1)}) custom-call(s32[2]{0:T(128)S(1)} %pad_add_fusion.idx, f32[2,8]{1,0:T(2,128)S(1)} %copy-done.4, f32[32,32,1024]{2,1,0:T(8,128)S(1)} %bitcast.8, f32[6,32,1024]{2,1,0:T(8,128)S(1)} %bitcast.9, f32[4,32,1024]{2,1,0:T(8,128)S(1)} %copy-done.2, ...), custom_call_target="tpu_custom_call" | custom-call | flops 1000000 | bytes 4000000 | tf_op jit(solution)/shard_map/pack/pallas_call | solution.py:161
  27.2 7.3 %collective-permute-start = (f32[8,144,128]{2,1,0:T(8,128)S(1)}, f32[8,144,128]{2,1,0:T(8,128)S(1)}, u32[]{:S(2)}, u32[]{:S(2)}) collective-permute-start(f32[8,144,128]{2,1,0:T(8,128)S(1)} %get-tuple-element.14.own_long), channel_id=1, source_target_pairs={{0,252},{4,8},{8,4},{12,16},{16,12},{20,24},{24,20},{28,32},{32,28... | collective-permute-start | bytes 1769480 | tf_op jit(solution)/shard_map/ppermute | solution.py:751
  34.5 0.0 collective-permute-start.1
  34.5 13.7 %collective-permute-done.got_long = f32[8,144,128]{2,1,0:T(8,128)S(1)} collective-permute-done((f32[8,144,128]{2,1,0:T(8,128)S(1)}, f32[8,144,128]{2,1,0:T(8,128)S(1)}, u32[]{:S(2)}, u32[]{:S(2)}) %collective-permute-start) | collective-permute-done | bytes 589856 | tf_op jit(solution)/shard_map/ppermute | solution.py:751
  48.2 0.9 collective-permute-done.1.got_short
  49.1 8.1 %edges.1 = (f32[3,8,24,128]{3,2,1,0:T(8,128)S(1)}, f32[3,8,24,128]{3,2,1,0:T(8,128)}, f32[256,128]{1,0:T(8,128)}) custom-call(s32[2]{0:T(128)S(1)} %pad_add_fusion.idx, f32[8,144,128]{2,1,0:T(8,128)S(1)} %get-tuple-element.14.own_long, f32[8,144,128]{2,1,0:T(8,128)S(1)} %get-tuple-element.15.own_short, f32[8,144,128]{2,1,0:T(8,128)S(1)} %collective-permute-done.got_long, ...), custom_call_target="tpu_custom_call" | custom-call | flops 20000000 | bytes 4000000 | tf_op jit(solution)/shard_map/edges/pallas_call | solution.py:545
  57.2 1.2 %collective-permute-start.3 = (f32[3,8,24,128]{3,2,1,0:T(8,128)}, f32[3,8,24,128]{3,2,1,0:T(8,128)S(1)}, u32[]{:S(2)}, u32[]{:S(2)}) collective-permute-start(f32[3,8,24,128]{3,2,1,0:T(8,128)} %get-tuple-element.22), channel_id=1, source_target_pairs={{0,1},{1,0},{2,3},{3,2},{4,5},{5,4},{6,7},{7,6},{8,9},{9,8},{10,11... | collective-permute-start | bytes 884744 | tf_op jit(solution)/shard_map/ppermute | solution.py:758
  58.4 8.0 %all-to-all-start = ((f32[256,1,128]{2,1,0:T(1,128)}), f32[256,1,128]{2,1,0:T(1,128)S(1)}, u32[]{:S(2)}, u32[]{:S(2)}) async-start(f32[256,1,128]{2,1,0:T(1,128)} %bitcast.5), calls=%async_computation | async-start | bytes 262144 | tf_op jit(solution)/shard_map/all_to_all | solution.py:759
  67.1 12.4 %all-to-all-done = f32[256,1,128]{2,1,0:T(1,128)S(1)} async-done(((f32[256,1,128]{2,1,0:T(1,128)}), f32[256,1,128]{2,1,0:T(1,128)S(1)}, u32[]{:S(2)}, u32[]{:S(2)}) %all-to-all-start) | async-done | bytes 131104 | tf_op jit(solution)/shard_map/all_to_all | solution.py:759
  79.5 0.0 collective-permute-done.3.other_edge
  79.5 0.0 collective-permute-done.2.other
  79.5 1.3 %density.1 = f32[8,72,128]{2,1,0:T(8,128)S(1)} custom-call(s32[2]{0:T(128)S(1)} %pad_add_fusion.idx, f32[1]{0:T(128)S(6)} %copy.8.filling, f32[256,128]{1,0:T(8,128)S(1)} %bitcast.10, f32[5,4,8,16,128]{4,3,2,1,0:T(8,128)S(1)} %get-tuple-element.19.mine, f32[5,4,8,16,128]{4,3,2,1,0:T(8,128)S(1)} %collective-permute-done.2.other, ...), custom_call_target="tpu_custom_call" | custom-call | flops 2000000 | bytes 4000000 | tf_op jit(solution)/shard_map/density/pallas_call | solution.py:665
  80.8 1.0 %collective-permute-start.4 = (f32[8,72,128]{2,1,0:T(8,128)S(1)}, f32[8,72,128]{2,1,0:T(8,128)S(1)}, u32[]{:S(2)}, u32[]{:S(2)}) collective-permute-start(f32[8,72,128]{2,1,0:T(8,128)S(1)} %density.1), channel_id=1, source_target_pairs={{0,2},{1,3},{2,0},{3,1},{4,6},{5,7},{6,4},{7,5},{8,10},{9,11},{10,... | collective-permute-start | bytes 884744 | tf_op jit(solution)/shard_map/ppermute | solution.py:764
  81.8 8.8 %collective-permute-done.4 = f32[8,72,128]{2,1,0:T(8,128)S(1)} collective-permute-done((f32[8,72,128]{2,1,0:T(8,128)S(1)}, f32[8,72,128]{2,1,0:T(8,128)S(1)}, u32[]{:S(2)}, u32[]{:S(2)}) %collective-permute-start.4) | collective-permute-done | bytes 294944 | tf_op jit(solution)/shard_map/ppermute | solution.py:764
  90.6 1.3 %collective-permute-start.5 = (f32[8,72,128]{2,1,0:T(8,128)S(1)}, f32[8,72,128]{2,1,0:T(8,128)S(1)}, u32[]{:S(2)}, u32[]{:S(2)}) collective-permute-start(f32[8,72,128]{2,1,0:T(8,128)S(1)} %add.12.mine), channel_id=1, source_target_pairs={{0,1},{1,0},{2,3},{3,2},{4,5},{5,4},{6,7},{7,6},{8,9},{9,8},{10,11... | collective-permute-start | bytes 884744 | tf_op jit(solution)/shard_map/ppermute | solution.py:765
  92.0 1.2 %collective-permute-done.5.other = f32[8,72,128]{2,1,0:T(8,128)S(1)} collective-permute-done((f32[8,72,128]{2,1,0:T(8,128)S(1)}, f32[8,72,128]{2,1,0:T(8,128)S(1)}, u32[]{:S(2)}, u32[]{:S(2)}) %collective-permute-start.5) | collective-permute-done | bytes 294944 | tf_op jit(solution)/shard_map/ppermute | solution.py:765
  93.2 1.6 %new_potential.1 = f32[4,32,1024]{2,1,0:T(8,128)} custom-call(s32[2]{0:T(128)S(1)} %pad_add_fusion.idx, f32[8,72,128]{2,1,0:T(8,128)S(1)} %add.12.mine, f32[8,72,128]{2,1,0:T(8,128)S(1)} %collective-permute-done.5.other), custom_call_target="tpu_custom_call" | custom-call | flops 1000000 | bytes 2000000 | tf_op jit(solution)/shard_map/new_potential/pallas_call | solution.py:721
  (1 shorter events, 0.0 us)
Async XLA Ops:
  0.1 2.2 %copy-start = (f32[4,8,32,1024]{3,2,1,0:T(8,128)S(1)}, f32[4,8,32,1024]{3,2,1,0:T(8,128)}, u32[]{:S(2)}) copy-start(f32[4,8,32,1024]{3,2,1,0:T(8,128)} %vec.1) | copy-start | bytes 12582916
  2.3 1.1 %copy-start.1 = (f32[2,3,32,1024]{3,2,1,0:T(8,128)S(1)}, f32[2,3,32,1024]{3,2,1,0:T(8,128)}, u32[]{:S(2)}) copy-start(f32[2,3,32,1024]{3,2,1,0:T(8,128)} %hop.1) | copy-start | bytes 2359300
  3.4 1.0 %copy-start.2 = (f32[4,32,1024]{2,1,0:T(8,128)S(1)}, f32[4,32,1024]{2,1,0:T(8,128)}, u32[]{:S(2)}) copy-start(f32[4,32,1024]{2,1,0:T(8,128)} %pot.3) | copy-start | bytes 1572868
  4.4 0.9 copy-start.3
  5.3 0.7 copy-start.4
  21.4 58.2 %collective-permute-start.2 = (f32[5,4,8,16,128]{4,3,2,1,0:T(8,128)}, f32[5,4,8,16,128]{4,3,2,1,0:T(8,128)S(1)}, u32[]{:S(2)}, u32[]{:S(2)}) collective-permute-start(f32[5,4,8,16,128]{4,3,2,1,0:T(8,128)} %get-tuple-element.20), channel_id=1, source_target_pairs={{0,1},{1,0},{2,3},{3,2},{4,5},{5,4},{6,7},{7,6},{8,9},{9,8},{10,11... | collective-permute-start | bytes 3932168 | tf_op jit(solution)/shard_map/ppermute | solution.py:757
  27.2 21.0 %collective-permute-start = (f32[8,144,128]{2,1,0:T(8,128)S(1)}, f32[8,144,128]{2,1,0:T(8,128)S(1)}, u32[]{:S(2)}, u32[]{:S(2)}) collective-permute-start(f32[8,144,128]{2,1,0:T(8,128)S(1)} %get-tuple-element.14.own_long), channel_id=1, source_target_pairs={{0,252},{4,8},{8,4},{12,16},{16,12},{20,24},{24,20},{28,32},{32,28... | collective-permute-start | bytes 1769480 | tf_op jit(solution)/shard_map/ppermute | solution.py:751
  34.5 14.6 %collective-permute-start.1 = (f32[8,144,128]{2,1,0:T(8,128)S(1)}, f32[8,144,128]{2,1,0:T(8,128)S(1)}, u32[]{:S(2)}, u32[]{:S(2)}) collective-permute-start(f32[8,144,128]{2,1,0:T(8,128)S(1)} %get-tuple-element.15.own_short), channel_id=1, source_target_pairs={{0,4},{4,0},{8,12},{12,8},{16,20},{20,16},{24,28},{28,24},{32,36},... | collective-permute-start | bytes 1769480 | tf_op jit(solution)/shard_map/ppermute | solution.py:752
  57.2 22.3 %collective-permute-start.3 = (f32[3,8,24,128]{3,2,1,0:T(8,128)}, f32[3,8,24,128]{3,2,1,0:T(8,128)S(1)}, u32[]{:S(2)}, u32[]{:S(2)}) collective-permute-start(f32[3,8,24,128]{3,2,1,0:T(8,128)} %get-tuple-element.22), channel_id=1, source_target_pairs={{0,1},{1,0},{2,3},{3,2},{4,5},{5,4},{6,7},{7,6},{8,9},{9,8},{10,11... | collective-permute-start | bytes 884744 | tf_op jit(solution)/shard_map/ppermute | solution.py:758
  58.4 21.1 %all-to-all-start = ((f32[256,1,128]{2,1,0:T(1,128)}), f32[256,1,128]{2,1,0:T(1,128)S(1)}, u32[]{:S(2)}, u32[]{:S(2)}) async-start(f32[256,1,128]{2,1,0:T(1,128)} %bitcast.5), calls=%async_computation | async-start | bytes 262144 | tf_op jit(solution)/shard_map/all_to_all | solution.py:759
  80.8 9.8 %collective-permute-start.4 = (f32[8,72,128]{2,1,0:T(8,128)S(1)}, f32[8,72,128]{2,1,0:T(8,128)S(1)}, u32[]{:S(2)}, u32[]{:S(2)}) collective-permute-start(f32[8,72,128]{2,1,0:T(8,128)S(1)} %density.1), channel_id=1, source_target_pairs={{0,2},{1,3},{2,0},{3,1},{4,6},{5,7},{6,4},{7,5},{8,10},{9,11},{10,... | collective-permute-start | bytes 884744 | tf_op jit(solution)/shard_map/ppermute | solution.py:764
  90.6 2.5 %collective-permute-start.5 = (f32[8,72,128]{2,1,0:T(8,128)S(1)}, f32[8,72,128]{2,1,0:T(8,128)S(1)}, u32[]{:S(2)}, u32[]{:S(2)}) collective-permute-start(f32[8,72,128]{2,1,0:T(8,128)S(1)} %add.12.mine), channel_id=1, source_target_pairs={{0,1},{1,0},{2,3},{3,2},{4,5},{5,4},{6,7},{7,6},{8,9},{9,8},{10,11... | collective-permute-start | bytes 884744 | tf_op jit(solution)/shard_map/ppermute | solution.py:765

commit v2 on v1

--- a/solution.py
+++ b/solution.py
@@ -16,6 +16,7 @@
 COEF = 32
 F32 = jnp.float32
 VMEM_LIMIT = 44 * 1024 * 1024
+VMEM_WIDE = 64 * 1024 * 1024 - 256 * 1024
 
 
 def jackson(count):
@@ -95,13 +96,13 @@
                 n += 1
     for copy in copies:
         copy.start()
-    for copy in copies:
-        copy.wait()
     nf = vec.shape[0]
     flat = v8.reshape(2, chunks, nf * SUB, LANES)
     odd = idx[0]
     outs = []
     for band in range(2):
+        for copy in copies[4 * chunks * band : 4 * chunks * (band + 1)]:
+            copy.wait()
         for c in range(chunks):
             first = 0 if band == 0 else SUB - 4
             for r in range(4):
@@ -171,7 +172,7 @@
             pltpu.VMEM((2, chunks, 4 * REC, LANES), F32),
             pltpu.SemaphoreType.DMA((n_in + 4,)),
         ],
-        compiler_params=pltpu.CompilerParams(vmem_limit_bytes=VMEM_LIMIT),
+        compiler_params=pltpu.CompilerParams(vmem_limit_bytes=VMEM_WIDE),
         cost_estimate=pl.CostEstimate(flops=1_000_000, bytes_accessed=4_000_000, transcendentals=0),
         name="pack",
     )(idx, inter, vec, hop, pot, stk)
@@ -180,8 +181,9 @@
 PAD = 8
 
 
-def interior_kernel(rows, chunks, nvec, group, idx, inter, vec, hop, pot, stk, keep, send, tot,
-                    x, t1, t2, hp, pt, st, ww, mom, sems):
+def interior_kernel(rows, chunks, nvec, group, idx, inter, vec, hop, pot, stk, after, keep, send,
+                    tot, x, t1, t2, hp, pt, st, ww, mom, dots, sems):
+    del after
     halves = nvec // group
     copies = []
     n = 0
@@ -256,6 +258,7 @@
             def rolled(site, c, fn):
                 return [fn(load(src, site, v + off, c, mid)) for v in vs]
 
+            products = [None] * 2
             b_prev = [rolled(2 * l + 1, chunks - 1, roll_right) for l in range(2)]
             a_here = [rolled(2 * l, 0, roll_left) for l in range(2)]
             for c in range(chunks):
@@ -292,6 +295,10 @@
                         first = load(x, s, v + q * group, c, mid)
                         term = first * value
                         sums[s] = term if sums[s] is None else sums[s] + term
+                        if order == 2:
+                            prior = load(src, s, v + off, c, mid)
+                            for k, pair in enumerate((prior * value, value * value)):
+                                products[k] = pair if products[k] is None else products[k] + pair
                         if order == 1:
                             sq = first * first
                             squares[s] = sq if squares[s] is None else squares[s] + sq
@@ -305,10 +312,16 @@
                         mom[0, s, c, plain, :] = squares[s]
                 a_here = a_next
                 b_prev = b_here
+            if order == 2:
+                row = lax.broadcasted_iota(jnp.int32, (SUB, LANES), 0) + base
+                inside = (row >= 2) & (row < rows - 2)
+                for k in range(2):
+                    dots[k] = dots[k] + jnp.where(inside, products[k], 0.0)
             return carry
 
         lax.fori_loop(0, groups, body, 0)
 
+    dots[...] = jnp.zeros_like(dots)
     for q in range(halves):
         for copy in late[q]:
             copy.wait()
@@ -334,7 +347,7 @@
         row = lax.broadcasted_iota(jnp.int32, (SUB, LANES), 0) + base
         inside = (row >= 2) & (row < rows - 2)
         result = []
-        for m in range(CHEB + 1):
+        for m in range(3):
             acc = None
             for s in range(4):
                 for c in range(chunks):
@@ -343,16 +356,16 @@
             result.append(carry[m] + jnp.where(inside, acc, 0.0))
         return tuple(result)
 
-    sums = lax.fori_loop(
-        0, groups, add_up, tuple(jnp.zeros((SUB, LANES), F32) for _ in range(CHEB + 1))
-    )
-    for m in range(CHEB + 1):
+    sums = lax.fori_loop(0, groups, add_up, tuple(jnp.zeros((SUB, LANES), F32) for _ in range(3)))
+    for m in range(3):
         tot[m] = sums[m]
+    for k in range(2):
+        tot[3 + k] = dots[k]
     kept.wait()
     sent.wait()
 
 
-def interior(idx, inter, vec, hop, pot, stk):
+def interior(idx, inter, vec, hop, pot, stk, after):
     _, nvec, rows, width = vec.shape
     chunks = width // LANES
     group = 4
@@ -363,7 +376,7 @@
     return pl.pallas_call(
         functools.partial(interior_kernel, rows, chunks, nvec, group),
         out_shape=[half, half, jax.ShapeDtypeStruct((CHEB + 1, SUB, LANES), F32)],
-        in_specs=[smem, smem, any_, any_, any_, any_],
+        in_specs=[smem, smem, any_, any_, any_, any_, any_],
         out_specs=[any_, any_, pl.BlockSpec(memory_space=pltpu.VMEM)],
         scratch_shapes=[
             pltpu.VMEM((4, nvec, chunks, rows + 2 * PAD, LANES), F32),
@@ -374,135 +387,206 @@
             pltpu.VMEM((chunks, rows, LANES), jnp.int32),
             pltpu.VMEM((2, chunks, rows, LANES), F32),
             pltpu.VMEM((CHEB + 1, 4, chunks, rows, LANES), F32),
+            pltpu.VMEM((2, SUB, LANES), F32),
             pltpu.SemaphoreType.DMA((n,)),
         ],
-        compiler_params=pltpu.CompilerParams(vmem_limit_bytes=VMEM_LIMIT),
+        compiler_params=pltpu.CompilerParams(vmem_limit_bytes=VMEM_WIDE),
         cost_estimate=pl.CostEstimate(
             flops=60_000_000, bytes_accessed=9_000_000, transcendentals=0
         ),
         name="interior",
-    )(idx, inter, vec, hop, pot, stk)
+    )(idx, inter, vec, hop, pot, stk, after)
 
 
 WIN = 7
-
-
-def edges_kernel(chunks, parts, idx, own_long, own_short, got_long, got_short, extra, part, keep,
-                 send, tot, w, t1, t2, res, sems):
-    odd, core = idx[0], idx[1]
+GUARD = REC
+
+
+def gather_window(odd, refs, w, sems):
+    own_long, own_short, got_long, got_short, extra = refs
     three = 3 * REC
-
-    def both(refs, when, dst, sem):
-        @pl.when(when)
+    even = odd == 0
+
+    def both(first, second, dst, sem):
+        @pl.when(even)
         def _():
-            pltpu.make_async_copy(refs[0], dst, sem).start()
-
-        @pl.when(jnp.logical_not(when))
+            pltpu.make_async_copy(first, dst, sem).start()
+
+        @pl.when(jnp.logical_not(even))
         def _():
-            pltpu.make_async_copy(refs[1], dst, sem).start()
-
-        return pltpu.make_async_copy(refs[0], dst, sem)
-
-    even = odd == 0
-    guard = REC
+            pltpu.make_async_copy(second, dst, sem).start()
+
+        return pltpu.make_async_copy(first, dst, sem)
+
     copies = [
-        both((got_long, got_short), even, w.at[0, :, pl.ds(guard, three)], sems.at[0]),
-        both((own_long, own_short), even, w.at[0, :, pl.ds(guard + three, three)], sems.at[1]),
-        both((own_short, own_long), even, w.at[1, :, pl.ds(guard + REC, three)], sems.at[2]),
-        both((got_short, got_long), even, w.at[1, :, pl.ds(guard + REC + three, three)], sems.at[3]),
+        both(got_long, got_short, w.at[0, :, pl.ds(GUARD, three)], sems.at[0]),
+        both(own_long, own_short, w.at[0, :, pl.ds(GUARD + three, three)], sems.at[1]),
+        both(own_short, own_long, w.at[1, :, pl.ds(GUARD + REC, three)], sems.at[2]),
+        both(got_short, got_long, w.at[1, :, pl.ds(GUARD + REC + three, three)], sems.at[3]),
     ]
     for band, place in ((0, 6), (1, 0)):
         copy = pltpu.make_async_copy(
-            extra.at[band], w.at[band, :, pl.ds(guard + place * REC, REC)], sems.at[4 + band]
+            extra.at[band], w.at[band, :, pl.ds(GUARD + place * REC, REC)], sems.at[4 + band]
         )
         copy.start()
         copies.append(copy)
     for copy in copies:
         copy.wait()
 
+
+def window_slice(ref, is_w, band, c, i, site):
+    start = GUARD + i * REC + site * SUB if is_w else (i + 1) * 32 + site * SUB
+    return ref[band, c, pl.ds(pl.multiple_of(start, SUB), SUB), :]
+
+
+def window_step(chunks, order, w, source, before, band, i, emit):
+    from_w = order == 1
+
+    def here(site, c, shift=0):
+        return window_slice(source, from_w, band, c, i + shift, site)
+
+    def coef_at(k, c, shift=0):
+        at = GUARD + (i + shift) * REC + COEF + k
+        return jnp.broadcast_to(w[band, c, pl.ds(at, 1), :], (SUB, LANES))
+
+    b_prev = [roll_right(here(2 * l + 1, chunks - 1)) for l in range(2)]
+    a_here = [roll_left(here(2 * l, 0)) for l in range(2)]
+    for c in range(chunks):
+        nxt = (c + 1) % chunks
+        a_next = [roll_left(here(2 * l, nxt)) for l in range(2)]
+        b_here = [roll_right(here(2 * l + 1, c)) for l in range(2)]
+        coef = [coef_at(k, c) for k in range(14)]
+        t2_down = [coef_at(4 * l + 2, c, 1) for l in range(2)]
+        a = [here(2 * l, c) for l in range(2)]
+        b = [here(2 * l + 1, c) for l in range(2)]
+        a_down = [here(2 * l, c, 1) for l in range(2)]
+        b_up = [here(2 * l + 1, c, -1) for l in range(2)]
+        a_right = [from_right(a_here[l], a_next[l]) for l in range(2)]
+        b_left = [from_left(b_here[l], b_prev[l]) for l in range(2)]
+        new = hop_apply(a, b, a_right, b_left, a_down, b_up, coef, t2_down)
+        for s in range(4):
+            if order == 1:
+                new[s] = new[s] * 0.5
+            else:
+                new[s] = new[s] - window_slice(before, order == 2, band, c, i, s)
+        emit(c, new)
+        a_here = a_next
+        b_prev = b_here
+
+
+def store_row(target, band, i):
+    def emit(c, values):
+        for s in range(4):
+            at = pl.multiple_of((i + 1) * 32 + s * SUB, SUB)
+            target[band, c, pl.ds(at, SUB), :] = values[s]
+
+    return emit
+
+
+def totals_kernel(chunks, parts, idx, own_long, own_short, got_long, got_short, extra, part, tot,
+                  w, t1, dots, sems):
+    gather_window(idx[0], (own_long, own_short, got_long, got_short, extra), w, sems)
+
+    def first(j, carry):
+        for band in range(2):
+            i = 2 - band + j
+            window_step(chunks, 1, w, w, None, band, i, store_row(t1, band, i))
+        return carry
+
+    lax.fori_loop(0, 4, first, 0)
+    dots[...] = part[...]
+
+    def second(j, carry):
+        for band in range(2):
+            i = 3 - band + j
+            sums = [None] * 5
+
+            def emit(c, values):
+                for s in range(4):
+                    zero = window_slice(w, True, band, c, i, s)
+                    one = window_slice(t1, False, band, c, i, s)
+                    two = values[s]
+                    terms = (zero * zero, zero * one, zero * two, one * two, two * two)
+                    for k, term in enumerate(terms):
+                        sums[k] = term if sums[k] is None else sums[k] + term
+
+            window_step(chunks, 2, w, t1, w, band, i, emit)
+            for k in range(5):
+                dots[k] = dots[k] + sums[k]
+        return carry
+
+    lax.fori_loop(0, 2, second, 0)
+    lane = lax.broadcasted_iota(jnp.int32, (SUB, LANES), 1)
+    row = jnp.zeros((SUB, LANES), F32)
+    for m in range(5):
+        row = jnp.where(lane == m, jnp.sum(dots[m]), row)
+    for k in range(parts // SUB):
+        tot[pl.ds(k * SUB, SUB), :] = row
+
+
+def totals_of(idx, records, part, parts):
+    chunks = records[0].shape[0]
+    any_ = pl.BlockSpec(memory_space=pl.ANY)
+    smem = pl.BlockSpec(memory_space=pltpu.SMEM)
+    vmem = pl.BlockSpec(memory_space=pltpu.VMEM)
+    return pl.pallas_call(
+        functools.partial(totals_kernel, chunks, parts),
+        out_shape=jax.ShapeDtypeStruct((parts, LANES), F32),
+        in_specs=[smem, any_, any_, any_, any_, any_, vmem],
+        out_specs=vmem,
+        scratch_shapes=[
+            pltpu.VMEM((2, chunks, (WIN + 2) * REC, LANES), F32),
+            pltpu.VMEM((2, chunks, (WIN + 2) * 32, LANES), F32),
+            pltpu.VMEM((5, SUB, LANES), F32),
+            pltpu.SemaphoreType.DMA((6,)),
+        ],
+        compiler_params=pltpu.CompilerParams(vmem_limit_bytes=VMEM_WIDE),
+        cost_estimate=pl.CostEstimate(flops=8_000_000, bytes_accessed=4_000_000, transcendentals=0),
+        name="totals",
+    )(idx, *records, part)
+
+
+def edges_kernel(chunks, idx, own_long, own_short, got_long, got_short, extra, after, out, w, t1,
+                 t2, res, sems):
+    del after
+    gather_window(idx[0], (own_long, own_short, got_long, got_short, extra), w, sems)
+
+    def moments(band, i, c, order, values):
+        for s in range(4):
+            zero = window_slice(w, True, band, c, i, s)
+            term = jnp.sum(zero * values[s], axis=0, keepdims=True)
+            res[band, i - 2, c, pl.ds(order * 4 + s, 1), :] = term
+
     def sweep(order, first, last):
+        source, before, target = {
+            1: (w, None, t1),
+            2: (t1, w, t2),
+            3: (t2, t1, t1),
+            4: (t1, t2, None),
+        }[order]
+
         def body(j, carry):
-            band = lax.rem(j, 2)
-            i = first + lax.div(j, 2)
-            rec0 = guard + i * REC
-
-            def here(ref, site, c, shift=0):
-                if ref is w:
-                    at = pl.multiple_of(rec0 + shift * REC + site * SUB, SUB)
+            i = first + j
+            for band in range(2):
+                if order < 4:
+                    emit = store_row(target, band, i)
                 else:
-                    at = pl.multiple_of((i + 1 + shift) * 32 + site * SUB, SUB)
-                return ref[band, c, pl.ds(at, SUB), :]
-
-            def coef_at(k, c, shift=0):
-                at = rec0 + shift * REC + COEF + k
-                return jnp.broadcast_to(w[band, c, pl.ds(at, 1), :], (SUB, LANES))
-
-            source, before, target = {
-                1: (w, None, t1),
-                2: (t1, w, t2),
-                3: (t2, t1, t1),
-                4: (t1, t2, None),
-            }[order]
-            centre = order == 4
-            b_prev = [roll_right(here(source, 2 * l + 1, chunks - 1)) for l in range(2)]
-            a_here = [roll_left(here(source, 2 * l, 0)) for l in range(2)]
-            for c in range(chunks):
-                nxt = (c + 1) % chunks
-                a_next = [roll_left(here(source, 2 * l, nxt)) for l in range(2)]
-                b_here = [roll_right(here(source, 2 * l + 1, c)) for l in range(2)]
-                coef = [coef_at(k, c) for k in range(14)]
-                t2_down = [coef_at(4 * l + 2, c, 1) for l in range(2)]
-                a = [here(source, 2 * l, c) for l in range(2)]
-                b = [here(source, 2 * l + 1, c) for l in range(2)]
-                a_down = [here(source, 2 * l, c, 1) for l in range(2)]
-                b_up = [here(source, 2 * l + 1, c, -1) for l in range(2)]
-                a_right = [from_right(a_here[l], a_next[l]) for l in range(2)]
-                b_left = [from_left(b_here[l], b_prev[l]) for l in range(2)]
-                new = hop_apply(a, b, a_right, b_left, a_down, b_up, coef, t2_down)
-                for s in range(4):
-                    if order == 1:
-                        value = new[s] * 0.5
-                    else:
-                        value = new[s] - here(before, s, c)
-                    if target is not None:
-                        at = pl.multiple_of((i + 1) * 32 + s * SUB, SUB)
-                        target[band, c, pl.ds(at, SUB), :] = value
-                    new[s] = value
-                if centre:
-                    moments(band, i, c, 4, new, here)
-                a_here = a_next
-                b_prev = b_here
+                    emit = lambda c, values, band=band: moments(band, i, c, 4, values)
+                window_step(chunks, order, w, source, before, band, i, emit)
             return carry
 
-        lax.fori_loop(0, 2 * (last - first + 1), body, 0)
-
-    def moments(band, i, c, order, values, here):
-        for s in range(4):
-            first = here(w, s, c)
-            term = jnp.sum(first * values[s], axis=0, keepdims=True)
-            res[band, i - 2, c, pl.ds(order * 4 + s, 1), :] = term
+        lax.fori_loop(0, last - first + 1, body, 0)
 
     def collect(order, ref):
         def body(j, carry):
-            band = lax.rem(j, 2)
-            i = 2 + lax.div(j, 2)
-
-            def here(source, site, c):
-                at = pl.multiple_of(guard + i * REC + site * SUB, SUB)
-                return source[band, c, pl.ds(at, SUB), :]
-
-            for c in range(chunks):
-                values = []
-                for s in range(4):
-                    if ref is w:
-                        values.append(here(w, s, c))
-                    else:
-                        at = pl.multiple_of((i + 1) * 32 + s * SUB, SUB)
-                        values.append(ref[band, c, pl.ds(at, SUB), :])
-                moments(band, i, c, order, values, here)
+            i = 2 + j
+            for band in range(2):
+                for c in range(chunks):
+                    values = [window_slice(ref, ref is w, band, c, i, s) for s in range(4)]
+                    moments(band, i, c, order, values)
             return carry
 
-        lax.fori_loop(0, 6, body, 0)
+        lax.fori_loop(0, 3, body, 0)
 
     collect(0, w)
     sweep(1, 0, 6)
@@ -512,54 +596,33 @@
     sweep(3, 1, 5)
     collect(3, t1)
     sweep(4, 2, 4)
-    out = [
-        pltpu.make_async_copy(res.at[core], keep, sems.at[6]),
-        pltpu.make_async_copy(res.at[1 - core], send, sems.at[7]),
-    ]
-    for copy in out:
-        copy.start()
-    lane = lax.broadcasted_iota(jnp.int32, (SUB, LANES), 1)
-    row = jnp.zeros((SUB, LANES), F32)
-    for m in range(CHEB + 1):
-        acc = part[m]
-        inner = None
-        for band in range(2):
-            for r in ((1, 2), (0, 1))[band]:
-                for c in range(chunks):
-                    value = res[band, r, c, pl.ds(4 * m, 4), :]
-                    inner = value if inner is None else inner + value
-        total = jnp.sum(acc) + jnp.sum(inner)
-        row = jnp.where(lane == m, total, row)
-    for k in range(parts // SUB):
-        tot[pl.ds(k * SUB, SUB), :] = row
-    for copy in out:
-        copy.wait()
-
-
-def edges(idx, own_long, own_short, got_long, got_short, extra, part, parts):
-    chunks = own_long.shape[0]
+    away = pltpu.make_async_copy(res, out, sems.at[6])
+    away.start()
+    away.wait()
+
+
+def edges(idx, records, after):
+    chunks = records[0].shape[0]
     any_ = pl.BlockSpec(memory_space=pl.ANY)
     smem = pl.BlockSpec(memory_space=pltpu.SMEM)
-    vmem = pl.BlockSpec(memory_space=pltpu.VMEM)
-    edge = jax.ShapeDtypeStruct((3, chunks, 24, LANES), F32)
     return pl.pallas_call(
-        functools.partial(edges_kernel, chunks, parts),
-        out_shape=[edge, edge, jax.ShapeDtypeStruct((parts, LANES), F32)],
-        in_specs=[smem, any_, any_, any_, any_, any_, vmem],
-        out_specs=[any_, any_, vmem],
+        functools.partial(edges_kernel, chunks),
+        out_shape=jax.ShapeDtypeStruct((2, 3, chunks, 24, LANES), F32),
+        in_specs=[smem, any_, any_, any_, any_, any_, any_],
+        out_specs=any_,
         scratch_shapes=[
             pltpu.VMEM((2, chunks, (WIN + 2) * REC, LANES), F32),
             pltpu.VMEM((2, chunks, (WIN + 2) * 32, LANES), F32),
             pltpu.VMEM((2, chunks, (WIN + 2) * 32, LANES), F32),
             pltpu.VMEM((2, 3, chunks, 24, LANES), F32),
-            pltpu.SemaphoreType.DMA((8,)),
+            pltpu.SemaphoreType.DMA((7,)),
         ],
         compiler_params=pltpu.CompilerParams(vmem_limit_bytes=VMEM_LIMIT),
         cost_estimate=pl.CostEstimate(
             flops=20_000_000, bytes_accessed=4_000_000, transcendentals=0
         ),
         name="edges",
-    )(idx, own_long, own_short, got_long, got_short, extra, part)
+    )(idx, *records, after)
 
 
 ACOS = (
@@ -594,12 +657,13 @@
     return out
 
 
-def density_kernel(chunks, half, scale, sites, idx, filling, sums, mine, other, my_edge, other_edge,
-                   out):
+def density_kernel(chunks, half, scale, sites, idx, filling, sums, mine, other, edge, out):
     core = idx[1]
     added = jnp.sum(sums[...], axis=0, keepdims=True) * scale
     lane = lax.broadcasted_iota(jnp.int32, (1, LANES), 1)
     totals = [jnp.sum(jnp.where(lane == m, added, 0.0)) for m in range(CHEB + 1)]
+    totals[3] = 2.0 * totals[3] - totals[1]
+    totals[4] = 2.0 * totals[4] - totals[0]
     target = filling[0] * sites
 
     point = (
@@ -622,6 +686,7 @@
         low = low + below * step
     chem = jnp.full((SUB, LANES), low + 0.5 * step, F32)
     weights = [value * scale for value in weights_of(chem)]
+    tall = 4 * half + SUB
 
     for c in range(chunks):
         for s in range(4):
@@ -631,66 +696,77 @@
                 for m in range(CHEB + 1):
                     term = weights[m] * (mine[m, s, c, at, :] + other[m, s, c, at, :])
                     acc = term if acc is None else acc + term
-                out[c, pl.ds(s * half + g * SUB, SUB), :] = acc
-        rows = []
-        for r in range(3):
-            acc = None
-            for m in range(CHEB + 1):
-                at = pl.ds(4 * m, 4)
-                term = weights[m][0:4] * (my_edge[r, c, at, :] + other_edge[r, c, at, :])
-                acc = term if acc is None else acc + term
-            rows.append(acc)
-        halo = jnp.where(core == 0, rows[0], rows[2])
-        out[c, pl.ds(4 * half, SUB), :] = jnp.broadcast_to(
-            jnp.sum(halo, axis=0, keepdims=True), (SUB, LANES)
-        )
+                out[pl.ds(c * tall + s * half + g * SUB, SUB), :] = acc
+        bands = []
+        for band in range(2):
+            rows = []
+            for r in range(3):
+                acc = None
+                for m in range(CHEB + 1):
+                    term = weights[m][0:4] * edge[band, r, c, pl.ds(4 * m, 4), :]
+                    acc = term if acc is None else acc + term
+                rows.append(acc)
+            bands.append(rows)
+            halo = rows[0] if band == 0 else rows[2]
+            out[pl.ds(chunks * tall + band * SUB + c, 1), :] = jnp.sum(halo, axis=0, keepdims=True)
+        upper, lower = bands[0][1:], bands[1][:2]
 
         @pl.when(core == 0)
         def _():
-            for s in range(4):
-                out[c, pl.ds(s * half, 1), :] = rows[1][s : s + 1]
-                out[c, pl.ds(s * half + 1, 1), :] = rows[2][s : s + 1]
+            for r in range(2):
+                for s in range(4):
+                    out[pl.ds(c * tall + s * half + r, 1), :] = upper[r][s : s + 1]
+                out[pl.ds(c * tall + 4 * half + 4 * r, 4), :] = lower[r]
 
         @pl.when(core != 0)
         def _():
-            for s in range(4):
-                out[c, pl.ds(s * half + half - 2, 1), :] = rows[0][s : s + 1]
-                out[c, pl.ds(s * half + half - 1, 1), :] = rows[1][s : s + 1]
-
-
-def density(idx, filling, sums, mine, other, my_edge, other_edge, vectors, sites):
+            for r in range(2):
+                for s in range(4):
+                    out[pl.ds(c * tall + s * half + half - 2 + r, 1), :] = lower[r][s : s + 1]
+                out[pl.ds(c * tall + 4 * half + 4 * r, 4), :] = upper[r]
+
+
+def density(idx, filling, sums, mine, other, edge, vectors, sites):
     _, _, chunks, half, _ = mine.shape
     smem = pl.BlockSpec(memory_space=pltpu.SMEM)
     vmem = pl.BlockSpec(memory_space=pltpu.VMEM)
     return pl.pallas_call(
         functools.partial(density_kernel, chunks, half, 1.0 / vectors, float(sites)),
-        out_shape=jax.ShapeDtypeStruct((chunks, 4 * half + SUB, LANES), F32),
-        in_specs=[smem, smem, vmem, vmem, vmem, vmem, vmem],
+        out_shape=jax.ShapeDtypeStruct((chunks * (4 * half + SUB) + 2 * SUB, LANES), F32),
+        in_specs=[smem, smem, vmem, vmem, vmem, vmem],
         out_specs=vmem,
         compiler_params=pltpu.CompilerParams(vmem_limit_bytes=VMEM_LIMIT),
         cost_estimate=pl.CostEstimate(flops=2_000_000, bytes_accessed=4_000_000, transcendentals=0),
         name="density",
-    )(idx, filling, sums, mine, other, my_edge, other_edge)
-
-
-def potential_kernel(chunks, half, idx, mine, other, out, charge):
+    )(idx, filling, sums, mine, other, edge)
+
+
+def potential_kernel(chunks, half, idx, mine, other, out, dens, charge):
     first = idx[1] == 0
+    tall = 4 * half + SUB
     guard = SUB
 
-    def rows_of(ref, c):
-        total = None
+    for c in range(chunks):
         for s in range(4):
-            value = ref[c, pl.ds(s * half, half), :]
-            total = value if total is None else total + value
-        return total - 2.0
-
-    for c in range(chunks):
-        m, o = rows_of(mine, c), rows_of(other, c)
-        charge[c, pl.ds(guard, half), :] = jnp.where(first, m, o)
-        charge[c, pl.ds(guard + half, half), :] = jnp.where(first, o, m)
-        m, o = (ref[c, pl.ds(4 * half, 1), :] - 2.0 for ref in (mine, other))
-        charge[c, pl.ds(guard - 1, 1), :] = jnp.where(first, m, o)
-        charge[c, pl.ds(guard + 2 * half, 1), :] = jnp.where(first, o, m)
+            at = pl.ds(c * tall + s * half, half)
+            m, o = mine[at, :], other[at, :]
+            dens[s, c, pl.ds(0, half), :] = jnp.where(first, m, o)
+            dens[s, c, pl.ds(half, half), :] = jnp.where(first, o, m)
+        at = pl.ds(c * tall + 4 * half, SUB)
+        m, o = mine[at, :], other[at, :]
+        upper, lower = jnp.where(first, o, m), jnp.where(first, m, o)
+        for r in range(2):
+            for s in range(4):
+                k = 4 * r + s
+                for row, more in ((r, upper), (2 * half - 2 + r, lower)):
+                    dens[s, c, pl.ds(row, 1), :] = dens[s, c, pl.ds(row, 1), :] + more[k : k + 1]
+        for g in range(2 * half // SUB):
+            at = pl.ds(g * SUB, SUB)
+            total = (dens[0, c, at, :] + dens[1, c, at, :]) + (dens[2, c, at, :] + dens[3, c, at, :])
+            charge[c, pl.ds(guard + g * SUB, SUB), :] = total - 2.0
+        for band, row in ((0, guard - 1), (1, guard + 2 * half)):
+            at = pl.ds(chunks * tall + band * SUB + c, 1)
+            charge[c, pl.ds(row, 1), :] = mine[at, :] + other[at, :] - 2.0
     for g in range(2 * half // SUB):
         at = pl.ds(guard + g * SUB, SUB)
         for c in range(chunks):
@@ -704,18 +780,13 @@
                 + right
             )
             base = 0.5 * here + 0.25 * near
-            in_first = g * SUB < half
-            row = g * SUB - (0 if in_first else half)
             for s in range(4):
-                rows = pl.ds(s * half + row, SUB)
-                a, b = mine[c, rows, :], other[c, rows, :]
-                dens = jnp.where(first, a, b) if in_first else jnp.where(first, b, a)
-                out[s, pl.ds(g * SUB, SUB), pl.ds(c * LANES, LANES)] = 3.0 * (dens - 0.5) + base
-
-
-def new_potential(idx, mine, other):
-    chunks, height, _ = mine.shape
-    half = (height - SUB) // 4
+                value = dens[s, c, pl.ds(g * SUB, SUB), :]
+                out[s, pl.ds(g * SUB, SUB), pl.ds(c * LANES, LANES)] = 3.0 * (value - 0.5) + base
+
+
+def new_potential(idx, mine, other, chunks):
+    half = ((mine.shape[0] - 2 * SUB) // chunks - SUB) // 4
     smem = pl.BlockSpec(memory_space=pltpu.SMEM)
     vmem = pl.BlockSpec(memory_space=pltpu.VMEM)
     return pl.pallas_call(
@@ -723,7 +794,10 @@
         out_shape=jax.ShapeDtypeStruct((4, 2 * half, chunks * LANES), F32),
         in_specs=[smem, vmem, vmem],
         out_specs=vmem,
-        scratch_shapes=[pltpu.VMEM((chunks, 2 * half + 2 * SUB, LANES), F32)],
+        scratch_shapes=[
+            pltpu.VMEM((4, chunks, 2 * half, LANES), F32),
+            pltpu.VMEM((chunks, 2 * half + 2 * SUB, LANES), F32),
+        ],
         compiler_params=pltpu.CompilerParams(vmem_limit_bytes=VMEM_LIMIT),
         cost_estimate=pl.CostEstimate(flops=1_000_000, bytes_accessed=2_000_000, transcendentals=0),
         name="new_potential",
@@ -750,19 +824,19 @@
     )
     got_long = lax.ppermute(own_long, "dom", long_way)
     got_short = lax.ppermute(own_short, "dom", short_way)
-    mine, yours, part = interior(idx, interlayer, vectors, hoppings, potential, stacking)
-    my_edge, your_edge, totals = edges(
-        idx, own_long, own_short, got_long, got_short, extra, part, strips * ranks
+    mine, yours, part = interior(
+        idx, interlayer, vectors, hoppings, potential, stacking, own_short
     )
+    records = (own_long, own_short, got_long, got_short, extra)
+    totals = totals_of(idx, records, part, strips * ranks)
+    edge = edges(idx, records, totals)
+    yours, ready = lax.optimization_barrier((yours, totals))
     other = lax.ppermute(yours, "vec", sibling)
-    other_edge = lax.ppermute(your_edge, "vec", sibling)
-    sums = lax.all_to_all(totals, ("dom", "vec"), 0, 0, tiled=True)
+    sums = lax.all_to_all(ready, ("dom", "vec"), 0, 0, tiled=True)
     sites = 4 * rows * width * strips
-    chip = density(
-        idx, filling, sums, mine, other, my_edge, other_edge, nvec * ranks, sites
-    )
+    chip = density(idx, filling, sums, mine, other, edge, nvec * ranks, sites)
     whole = chip + lax.ppermute(chip, "vec", across)
-    return new_potential(idx, whole, lax.ppermute(whole, "vec", sibling))
+    return new_potential(idx, whole, lax.ppermute(whole, "vec", sibling), width // LANES)
 
 
 def solution(mesh):

time: 95 us -> 74.1 us (0.78)
  waiting for transfers between devices: 37.1 us -> 11.8 us
  Pallas kernels: 28.8 us -> 35.9 us
  local copies, waits for them, and re-layouts: 5.94 us -> 4.03 us
  starting transfers between devices: 22.2 us -> 20.4 us
    ppermute x1, waiting for transfers between devices: 13.7 us -> 0.01 us  [per_device(): got_long = lax.ppermute(own_long, 'dom', long_way)]
    all_to_all x1, waiting for transfers between devices: 12.4 us -> 1.83 us  [per_device(): sums = lax.all_to_all(ready, ('dom', 'vec'), 0, 0, tiled=True)]
    pallas_call x1 -> x2, Pallas kernels: 8.12 us -> 11 us  [the longest x1 6.56 us: edges(): pl.pallas_call(functools.partial(edges_kernel, chunks), out_shape=jax.Sha...]
    ppermute x1, starting transfers between devices: 7.3 us -> 9.87 us  [per_device(): got_long = lax.ppermute(own_long, 'dom', long_way)]
    pallas_call x1, Pallas kernels: 15.3 us -> 17.6 us  [interior(): pl.pallas_call(functools.partial(interior_kernel, rows, chunks, nvec, gro...]
    ppermute x1, starting transfers between devices: 3.33 us -> 1.04 us  [per_device(): other = lax.ppermute(yours, 'vec', sibling)]
    unnamed x10 -> x12, local copies, waits for them, and re-layouts: 5.94 us -> 4.03 us
    pallas_call x1, Pallas kernels: 2.46 us -> 4.31 us  [pack(): pl.pallas_call(functools.partial(pack_kernel, rows, chunks), out_shape=[m...]
  transfers between devices with their start and end apart: 7 -> 6, of which waited for: 5 -> 3; matrix products, arithmetic and copies ran while one was open for 0% -> 0% of each run, Pallas kernels for 11% -> 33%
where the time goes in v2:
time: 74.1 us; the launch traced here: 73.7 us
  Pallas kernels  35.9 us (48%)
  starting transfers between devices  20.4 us (28%)
  waiting for transfers between devices  11.8 us (16%)
  local copies, waits for them, and re-layouts  4.03 us (5%)
    pallas_call x1, Pallas kernels, interior(): pl.pallas_call(functools.partial(interior_kernel, rows, chunks, nvec, gro...  17.6 us
    ppermute x1, starting transfers between devices, per_device(): got_long = lax.ppermute(own_long, 'dom', long_way)  9.87 us
    ppermute x1, waiting for transfers between devices, per_device(): whole = chip + lax.ppermute(chip, 'vec', across)  8.77 us
    all_to_all x1, starting transfers between devices, per_device(): sums = lax.all_to_all(ready, ('dom', 'vec'), 0, 0, tiled=True)  6.99 us
    pallas_call x1, Pallas kernels, edges(): pl.pallas_call(functools.partial(edges_kernel, chunks), out_shape=jax.Sha...  6.56 us
    pallas_call x1, Pallas kernels, totals_of(): pl.pallas_call(functools.partial(totals_kernel, chunks, parts), out_shape...  4.47 us
    pallas_call x1, Pallas kernels, pack(): pl.pallas_call(functools.partial(pack_kernel, rows, chunks), out_shape=[m...  4.31 us
    unnamed x12, local copies, waits for them, and re-layouts  4.03 us
  transfers between devices with their start and end apart: 6, of which 3 were waited for; matrix products, arithmetic and copies ran while one was open for 0% of the time, Pallas kernels for 33%

profile of v2, /device:TPU:1, one launch (start us, length us, event | category | flops | bytes accessed | tf_op | source)
XLA Modules:
  0.0 73.7 jit_solution(1254762237222265569)
XLA Ops:
  0.0 0.7 pad_add_fusion.idx
  0.7 4.3 %pack.1 = (f32[8,144,128]{2,1,0:T(8,128)}, f32[8,144,128]{2,1,0:T(8,128)}, f32[2,8,48,128]{3,2,1,0:T(8,128)}) custom-call(s32[2]{0:T(128)} %pad_add_fusion.idx, f32[2,8]{1,0:T(2,128)} %inter.3, f32[32,32,1024]{2,1,0:T(8,128)} %bitcast.10, f32[6,32,1024]{2,1,0:T(8,128)} %bitcast.11, f32[4,32,1024]{2,1,0:T(8,128)} %pot.3, s32[32,1024]{1,0:T(8,128)} %stk.3), custom_call_target="tpu_custom_call" | custom-call | flops 1000000 | bytes 4000000 | tf_op jit(solution)/shard_map/pack/pallas_call | solution.py:162
  5.0 9.9 %collective-permute-start = (f32[8,144,128]{2,1,0:T(8,128)}, f32[8,144,128]{2,1,0:T(8,128)}, u32[]{:S(2)}, u32[]{:S(2)}) collective-permute-start(f32[8,144,128]{2,1,0:T(8,128)} %get-tuple-element.15.own_long), channel_id=1, source_target_pairs={{0,252},{4,8},{8,4},{12,16},{16,12},{20,24},{24,20},{28,32},{32,28... | collective-permute-start | bytes 1769480 | tf_op jit(solution)/shard_map/ppermute | solution.py:825
  14.9 0.0 collective-permute-start.1
  14.9 17.6 %interior.1 = (f32[5,4,8,16,128]{4,3,2,1,0:T(8,128)}, f32[5,4,8,16,128]{4,3,2,1,0:T(8,128)}, f32[5,8,128]{2,1,0:T(8,128)}) custom-call(s32[2]{0:T(128)} %pad_add_fusion.idx, f32[2,8]{1,0:T(2,128)} %inter.3, f32[4,8,32,1024]{3,2,1,0:T(8,128)} %vec.1, f32[2,3,32,1024]{3,2,1,0:T(8,128)} %hop.1, f32[4,32,1024]{2,1,0:T(8,128)} %pot.3, s32[32,1024]{1,0:T(8,128)} %stk.3, ...), custom_call_target="tpu_custom_call" | custom-call | flops 60000000 | bytes 9000000 | tf_op jit(solution)/shard_map/interior/pallas_call | solution.py:376
  32.5 0.0 collective-permute-done.got_long
  32.5 0.0 collective-permute-done.1.got_short
  32.5 0.0 copy-start.5
  32.5 4.5 %totals.1.after = f32[256,128]{1,0:T(8,128)} custom-call(s32[2]{0:T(128)} %pad_add_fusion.idx, f32[8,144,128]{2,1,0:T(8,128)} %get-tuple-element.15.own_long, f32[8,144,128]{2,1,0:T(8,128)} %get-tuple-element.13.after.own_short, f32[8,144,128]{2,1,0:T(8,128)} %collective-permute-done.got_long, f32[8,144,128]{2,1,0:T(8,128)} %collective-permute-done.1.got_short, ...), custom_call_target="tpu_custom_call" | custom-call | flops 8000000 | bytes 4000000 | tf_op jit(solution)/shard_map/totals/pallas_call | solution.py:532
  37.0 1.0 %collective-permute-start.2 = (f32[5,4,8,16,128]{4,3,2,1,0:T(8,128)}, f32[5,4,8,16,128]{4,3,2,1,0:T(8,128)S(1)}, u32[]{:S(2)}, u32[]{:S(2)}) collective-permute-start(f32[5,4,8,16,128]{4,3,2,1,0:T(8,128)} %get-tuple-element.20), channel_id=1, source_target_pairs={{0,1},{1,0},{2,3},{3,2},{4,5},{5,4},{6,7},{7,6},{8,9},{9,8},{10,11... | collective-permute-start | bytes 3932168 | tf_op jit(solution)/shard_map/ppermute | solution.py:834
  38.1 7.0 %all-to-all-start = ((f32[256,1,128]{2,1,0:T(1,128)}), f32[256,1,128]{2,1,0:T(1,128)S(1)}, u32[]{:S(2)}, u32[]{:S(2)}) async-start(f32[256,1,128]{2,1,0:T(1,128)} %bitcast.8), calls=%async_computation | async-start | bytes 262144 | tf_op jit(solution)/shard_map/all_to_all | solution.py:835
  45.7 0.0 copy-done.5
  45.7 0.0 copy-start
  45.7 1.1 %copy-done = f32[8,144,128]{2,1,0:T(8,128)S(1)} copy-done((f32[8,144,128]{2,1,0:T(8,128)S(1)}, f32[8,144,128]{2,1,0:T(8,128)}, u32[]{:S(2)}) %copy-start) | copy-done | bytes 589848
  46.8 0.0 copy-start.1
  46.8 1.1 %copy-done.1 = f32[8,144,128]{2,1,0:T(8,128)S(1)} copy-done((f32[8,144,128]{2,1,0:T(8,128)S(1)}, f32[8,144,128]{2,1,0:T(8,128)}, u32[]{:S(2)}) %copy-start.1) | copy-done | bytes 589848
  47.8 0.0 copy-start.2
  47.8 1.0 %copy-done.2 = f32[2,8,48,128]{3,2,1,0:T(8,128)S(1)} copy-done((f32[2,8,48,128]{3,2,1,0:T(8,128)S(1)}, f32[2,8,48,128]{3,2,1,0:T(8,128)}, u32[]{:S(2)}) %copy-start.2) | copy-done | bytes 393240
  48.8 0.0 copy-start.4
  48.8 0.9 %copy-done.4 = f32[256,128]{1,0:T(8,128)S(1)} copy-done((f32[256,128]{1,0:T(8,128)S(1)}, f32[256,128]{1,0:T(8,128)}, u32[]{:S(2)}) %copy-start.4) | copy-done | bytes 131096
  49.7 0.0 copy-start.3
  49.7 6.6 %edges.1.edge = f32[2,3,8,24,128]{4,3,2,1,0:T(8,128)S(1)} custom-call(s32[2]{0:T(128)S(1)} %copy-done.5, f32[8,144,128]{2,1,0:T(8,128)S(1)} %copy-done.1, f32[8,144,128]{2,1,0:T(8,128)S(1)} %copy-done, f32[8,144,128]{2,1,0:T(8,128)} %collective-permute-done.got_long, f32[8,144,128]{2,1,0:T(8,128)} %collective-permute-done.1.got_short, ...), custom_call_target="tpu_custom_call" | custom-call | flops 20000000 | bytes 4000000 | tf_op jit(solution)/shard_map/edges/pallas_call | solution.py:608
  56.3 1.8 %all-to-all-done = f32[256,1,128]{2,1,0:T(1,128)S(1)} async-done(((f32[256,1,128]{2,1,0:T(1,128)}), f32[256,1,128]{2,1,0:T(1,128)S(1)}, u32[]{:S(2)}, u32[]{:S(2)}) %all-to-all-start) | async-done | bytes 131104 | tf_op jit(solution)/shard_map/all_to_all | solution.py:835
  58.2 0.0 collective-permute-done.2.other
  58.2 0.0 copy-done.3
  58.2 1.3 %density.1 = f32[592,128]{1,0:T(8,128)S(1)} custom-call(s32[2]{0:T(128)S(1)} %copy-done.5, f32[1]{0:T(128)S(6)} %copy.8.filling, f32[256,128]{1,0:T(8,128)S(1)} %bitcast.9, f32[5,4,8,16,128]{4,3,2,1,0:T(8,128)S(1)} %copy-done.3, f32[5,4,8,16,128]{4,3,2,1,0:T(8,128)S(1)} %collective-permute-done.2.other, f32[2,3,8,24,128]{4,3,2,1,0:T(8,128)S(1)} %edges.1.edge), custom_call_target="tpu_custom_call" | custom-call | flops 2000000 | bytes 4000000 | tf_op jit(solution)/shard_map/density/pallas_call | solution.py:733
  59.5 1.2 %collective-permute-start.3 = (f32[592,128]{1,0:T(8,128)S(1)}, f32[592,128]{1,0:T(8,128)S(1)}, u32[]{:S(2)}, u32[]{:S(2)}) collective-permute-start(f32[592,128]{1,0:T(8,128)S(1)} %density.1), channel_id=1, source_target_pairs={{0,2},{1,3},{2,0},{3,1},{4,6},{5,7},{6,4},{7,5},{8,10},{9,11},{10,... | collective-permute-start | bytes 909320 | tf_op jit(solution)/shard_map/ppermute | solution.py:838
  60.6 8.8 %collective-permute-done.3 = f32[592,128]{1,0:T(8,128)S(1)} collective-permute-done((f32[592,128]{1,0:T(8,128)S(1)}, f32[592,128]{1,0:T(8,128)S(1)}, u32[]{:S(2)}, u32[]{:S(2)}) %collective-permute-start.3) | collective-permute-done | bytes 303136 | tf_op jit(solution)/shard_map/ppermute | solution.py:838
  69.5 1.3 %collective-permute-start.4 = (f32[592,128]{1,0:T(8,128)S(1)}, f32[592,128]{1,0:T(8,128)S(1)}, u32[]{:S(2)}, u32[]{:S(2)}) collective-permute-start(f32[592,128]{1,0:T(8,128)S(1)} %add.12.mine), channel_id=1, source_target_pairs={{0,1},{1,0},{2,3},{3,2},{4,5},{5,4},{6,7},{7,6},{8,9},{9,8},{10,11... | collective-permute-start | bytes 909320 | tf_op jit(solution)/shard_map/ppermute | solution.py:839
  70.8 1.2 %collective-permute-done.4.other = f32[592,128]{1,0:T(8,128)S(1)} collective-permute-done((f32[592,128]{1,0:T(8,128)S(1)}, f32[592,128]{1,0:T(8,128)S(1)}, u32[]{:S(2)}, u32[]{:S(2)}) %collective-permute-start.4) | collective-permute-done | bytes 303136 | tf_op jit(solution)/shard_map/ppermute | solution.py:839
  72.0 1.6 %new_potential.1 = f32[4,32,1024]{2,1,0:T(8,128)} custom-call(s32[2]{0:T(128)S(1)} %copy-done.5, f32[592,128]{1,0:T(8,128)S(1)} %add.12.mine, f32[592,128]{1,0:T(8,128)S(1)} %collective-permute-done.4.other), custom_call_target="tpu_custom_call" | custom-call | flops 1000000 | bytes 2000000 | tf_op jit(solution)/shard_map/new_potential/pallas_call | solution.py:792
  (1 shorter events, 0.0 us)
Async XLA Ops:
  5.0 27.5 %collective-permute-start = (f32[8,144,128]{2,1,0:T(8,128)}, f32[8,144,128]{2,1,0:T(8,128)}, u32[]{:S(2)}, u32[]{:S(2)}) collective-permute-start(f32[8,144,128]{2,1,0:T(8,128)} %get-tuple-element.15.own_long), channel_id=1, source_target_pairs={{0,252},{4,8},{8,4},{12,16},{16,12},{20,24},{24,20},{28,32},{32,28... | collective-permute-start | bytes 1769480 | tf_op jit(solution)/shard_map/ppermute | solution.py:825
  14.9 17.7 %collective-permute-start.1 = (f32[8,144,128]{2,1,0:T(8,128)}, f32[8,144,128]{2,1,0:T(8,128)}, u32[]{:S(2)}, u32[]{:S(2)}) collective-permute-start(f32[8,144,128]{2,1,0:T(8,128)} %get-tuple-element.13.after.own_short), channel_id=1, source_target_pairs={{0,4},{4,0},{8,12},{12,8},{16,20},{20,16},{24,28},{28,24},{32,36},... | collective-permute-start | bytes 1769480 | tf_op jit(solution)/shard_map/ppermute | solution.py:826
  32.5 13.2 %copy-start.5 = (s32[2]{0:T(128)S(1)}, s32[2]{0:T(128)}, u32[]{:S(2)}) copy-start(s32[2]{0:T(128)} %pad_add_fusion.idx) | copy-start | bytes 28
  37.0 21.1 %collective-permute-start.2 = (f32[5,4,8,16,128]{4,3,2,1,0:T(8,128)}, f32[5,4,8,16,128]{4,3,2,1,0:T(8,128)S(1)}, u32[]{:S(2)}, u32[]{:S(2)}) collective-permute-start(f32[5,4,8,16,128]{4,3,2,1,0:T(8,128)} %get-tuple-element.20), channel_id=1, source_target_pairs={{0,1},{1,0},{2,3},{3,2},{4,5},{5,4},{6,7},{7,6},{8,9},{9,8},{10,11... | collective-permute-start | bytes 3932168 | tf_op jit(solution)/shard_map/ppermute | solution.py:834
  38.1 20.1 %all-to-all-start = ((f32[256,1,128]{2,1,0:T(1,128)}), f32[256,1,128]{2,1,0:T(1,128)S(1)}, u32[]{:S(2)}, u32[]{:S(2)}) async-start(f32[256,1,128]{2,1,0:T(1,128)} %bitcast.8), calls=%async_computation | async-start | bytes 262144 | tf_op jit(solution)/shard_map/all_to_all | solution.py:835
  45.7 1.1 %copy-start = (f32[8,144,128]{2,1,0:T(8,128)S(1)}, f32[8,144,128]{2,1,0:T(8,128)}, u32[]{:S(2)}) copy-start(f32[8,144,128]{2,1,0:T(8,128)} %get-tuple-element.13.after.own_short) | copy-start | bytes 1769476
  46.8 1.1 %copy-start.1 = (f32[8,144,128]{2,1,0:T(8,128)S(1)}, f32[8,144,128]{2,1,0:T(8,128)}, u32[]{:S(2)}) copy-start(f32[8,144,128]{2,1,0:T(8,128)} %get-tuple-element.15.own_long) | copy-start | bytes 1769476
  47.8 1.0 %copy-start.2 = (f32[2,8,48,128]{3,2,1,0:T(8,128)S(1)}, f32[2,8,48,128]{3,2,1,0:T(8,128)}, u32[]{:S(2)}) copy-start(f32[2,8,48,128]{3,2,1,0:T(8,128)} %get-tuple-element.16.extra) | copy-start | bytes 1179652
  48.8 0.9 %copy-start.4 = (f32[256,128]{1,0:T(8,128)S(1)}, f32[256,128]{1,0:T(8,128)}, u32[]{:S(2)}) copy-start(f32[256,128]{1,0:T(8,128)} %totals.1.after) | copy-start | bytes 393220
  49.7 8.4 %copy-start.3 = (f32[5,4,8,16,128]{4,3,2,1,0:T(8,128)S(1)}, f32[5,4,8,16,128]{4,3,2,1,0:T(8,128)}, u32[]{:S(2)}) copy-start(f32[5,4,8,16,128]{4,3,2,1,0:T(8,128)} %get-tuple-element.19.mine) | copy-start | bytes 3932164
  59.5 9.9 %collective-permute-start.3 = (f32[592,128]{1,0:T(8,128)S(1)}, f32[592,128]{1,0:T(8,128)S(1)}, u32[]{:S(2)}, u32[]{:S(2)}) collective-permute-start(f32[592,128]{1,0:T(8,128)S(1)} %density.1), channel_id=1, source_target_pairs={{0,2},{1,3},{2,0},{3,1},{4,6},{5,7},{6,4},{7,5},{8,10},{9,11},{10,... | collective-permute-start | bytes 909320 | tf_op jit(solution)/shard_map/ppermute | solution.py:838
  69.5 2.6 %collective-permute-start.4 = (f32[592,128]{1,0:T(8,128)S(1)}, f32[592,128]{1,0:T(8,128)S(1)}, u32[]{:S(2)}, u32[]{:S(2)}) collective-permute-start(f32[592,128]{1,0:T(8,128)S(1)} %add.12.mine), channel_id=1, source_target_pairs={{0,1},{1,0},{2,3},{3,2},{4,5},{5,4},{6,7},{7,6},{8,9},{9,8},{10,11... | collective-permute-start | bytes 909320 | tf_op jit(solution)/shard_map/ppermute | solution.py:839

commit v3 on v2

--- a/solution.py
+++ b/solution.py
@@ -78,10 +78,14 @@
     return [out[0][0], out[0][1], out[1][0], out[1][1]]
 
 
-def pack_kernel(rows, chunks, idx, inter, vec, hop, pot, stk, long_out, short_out, extra,
-                v8, h8, p8, s8, rec, sems):
-    copies = []
-    n = 0
+def place():
+    return lax.rem(lax.axis_index("dom"), 2), lax.rem(lax.axis_index("vec"), 2)
+
+
+def pack_kernel(rows, chunks, table, vec, hop, pot, stk, long_out, short_out, extra, inter, v8, h8,
+                p8, s8, rec, sems):
+    copies = [pltpu.make_async_copy(table, inter, sems.at[0])]
+    n = 1
     for band in range(2):
         at = pl.ds(band * (rows - SUB), SUB)
         for c in range(chunks):
@@ -98,12 +102,20 @@
         copy.start()
     nf = vec.shape[0]
     flat = v8.reshape(2, chunks, nf * SUB, LANES)
-    odd = idx[0]
+    odd = place()[0]
     outs = []
+    copies[0].wait()
+    waited = set()
+
+    def wait_tile(band, c):
+        if (band, c) not in waited:
+            waited.add((band, c))
+            for copy in copies[1 + 4 * (chunks * band + c) :][:4]:
+                copy.wait()
+
     for band in range(2):
-        for copy in copies[4 * chunks * band : 4 * chunks * (band + 1)]:
-            copy.wait()
         for c in range(chunks):
+            wait_tile(band, c)
             first = 0 if band == 0 else SUB - 4
             for r in range(4):
                 for s in range(nf // SUB):
@@ -111,6 +123,7 @@
                         band, c, pl.ds(s * SUB * SUB + first + r, SUB, stride=SUB), :
                     ]
             after = (c + 1) % chunks
+            wait_tile(band, after)
             coef = []
             for layer in range(2):
                 for k in range(3):
@@ -131,62 +144,62 @@
             zero = jnp.zeros((4, LANES), F32)
             for k in range(len(coef), REC - COEF):
                 rec[band, c, pl.ds(COEF + k, 4, stride=REC), :] = zero
-        message = rec.at[band, :, pl.ds(band * REC, 3 * REC)]
-        spare = rec.at[band, :, pl.ds((1 - band) * 3 * REC, REC)]
-        away = pltpu.make_async_copy(spare, extra.at[band], sems.at[n])
-        away.start()
-        outs.append(away)
-        n += 1
-
-        @pl.when(odd == band)
-        def _():
-            pltpu.make_async_copy(message, long_out, sems.at[n]).start()
-
-        @pl.when(odd != band)
-        def _():
-            pltpu.make_async_copy(message, short_out, sems.at[n]).start()
-
-        outs.append(pltpu.make_async_copy(message, long_out, sems.at[n]))
-        n += 1
+            message = rec.at[band, c, pl.ds(band * REC, 3 * REC)]
+            spare = rec.at[band, c, pl.ds((1 - band) * 3 * REC, REC)]
+            away = pltpu.make_async_copy(spare, extra.at[band, c], sems.at[n])
+            away.start()
+            outs.append(away)
+            n += 1
+
+            @pl.when(odd == band)
+            def _():
+                pltpu.make_async_copy(message, long_out.at[c], sems.at[n]).start()
+
+            @pl.when(odd != band)
+            def _():
+                pltpu.make_async_copy(message, short_out.at[c], sems.at[n]).start()
+
+            outs.append(pltpu.make_async_copy(message, long_out.at[c], sems.at[n]))
+            n += 1
     for copy in outs:
         copy.wait()
 
 
-def pack(idx, inter, vec, hop, pot, stk):
+def pack(inter, vec, hop, pot, stk):
     fields, rows, width = vec.shape
     chunks = width // LANES
     any_ = pl.BlockSpec(memory_space=pl.ANY)
-    smem = pl.BlockSpec(memory_space=pltpu.SMEM)
     message = jax.ShapeDtypeStruct((chunks, 3 * REC, LANES), F32)
-    n_in = 2 * chunks * 4
+    n_in = 2 * chunks * 4 + 1
     return pl.pallas_call(
         functools.partial(pack_kernel, rows, chunks),
         out_shape=[message, message, jax.ShapeDtypeStruct((2, chunks, REC, LANES), F32)],
-        in_specs=[smem, smem, any_, any_, any_, any_],
+        in_specs=[any_, any_, any_, any_, any_],
         out_specs=[any_, any_, any_],
         scratch_shapes=[
+            pltpu.SMEM(inter.shape, F32),
             pltpu.VMEM((2, chunks, fields, SUB, LANES), F32),
             pltpu.VMEM((2, chunks, 6, SUB, LANES), F32),
             pltpu.VMEM((2, chunks, 4, SUB, LANES), F32),
             pltpu.VMEM((2, chunks, SUB, LANES), jnp.int32),
             pltpu.VMEM((2, chunks, 4 * REC, LANES), F32),
-            pltpu.SemaphoreType.DMA((n_in + 4,)),
+            pltpu.SemaphoreType.DMA((n_in + 4 * chunks,)),
         ],
         compiler_params=pltpu.CompilerParams(vmem_limit_bytes=VMEM_WIDE),
         cost_estimate=pl.CostEstimate(flops=1_000_000, bytes_accessed=4_000_000, transcendentals=0),
         name="pack",
-    )(idx, inter, vec, hop, pot, stk)
+    )(inter, vec, hop, pot, stk)
 
 
 PAD = 8
 
 
-def interior_kernel(rows, chunks, nvec, group, idx, inter, vec, hop, pot, stk, after, keep, send,
-                    tot, x, t1, t2, hp, pt, st, ww, mom, dots, sems):
+def interior_kernel(rows, chunks, nvec, group, table, vec, hop, pot, stk, after, keep, send, tot,
+                    inter, x, t1, t2, hp, pt, st, ww, mom, dots, sems):
     del after
     halves = nvec // group
-    copies = []
-    n = 0
+    copies = [pltpu.make_async_copy(table, inter, sems.at[0])]
+    n = 1
     for c in range(chunks):
         lanes = pl.ds(c * LANES, LANES)
         for src, dst in (
@@ -319,28 +332,34 @@
                     dots[k] = dots[k] + jnp.where(inside, products[k], 0.0)
             return carry
 
-        lax.fori_loop(0, groups, body, 0)
+        lax.fori_loop(0, groups, body, 0, unroll=4)
+
+    half = rows // 2
+    core = place()[1]
+    keep_at = pl.ds(pl.multiple_of(core * half, SUB), half)
+    send_at = pl.ds(pl.multiple_of((1 - core) * half, SUB), half)
+    outs = []
+
+    def write_out(order):
+        for rows_at, dst, k in ((keep_at, keep, 0), (send_at, send, 1)):
+            copy = pltpu.make_async_copy(
+                mom.at[order, :, :, rows_at], dst.at[order], sems.at[n + 2 * order + k]
+            )
+            copy.start()
+            outs.append(copy)
 
     dots[...] = jnp.zeros_like(dots)
     for q in range(halves):
         for copy in late[q]:
             copy.wait()
         start = (x, q * group)
-        sweep(1, q, start, None, t1)
-        sweep(2, q, (t1, 0), start, t2)
-        sweep(3, q, (t2, 0), (t1, 0), t1)
-        sweep(4, q, (t1, 0), (t2, 0), None)
-
-    half = rows // 2
-    core = idx[1]
-    kept = pltpu.make_async_copy(
-        mom.at[:, :, :, pl.ds(pl.multiple_of(core * half, SUB), half)], keep, sems.at[n]
-    )
-    sent = pltpu.make_async_copy(
-        mom.at[:, :, :, pl.ds(pl.multiple_of((1 - core) * half, SUB), half)], send, sems.at[n + 1]
-    )
-    kept.start()
-    sent.start()
+        steps = ((start, None, t1), ((t1, 0), start, t2), ((t2, 0), (t1, 0), t1), ((t1, 0), (t2, 0), None))
+        for order, (source, before, target) in enumerate(steps, 1):
+            sweep(order, q, source, before, target)
+            if q == halves - 1:
+                if order == 1:
+                    write_out(0)
+                write_out(order)
 
     def add_up(g, carry):
         base = pl.multiple_of(g * SUB, SUB)
@@ -361,24 +380,24 @@
         tot[m] = sums[m]
     for k in range(2):
         tot[3 + k] = dots[k]
-    kept.wait()
-    sent.wait()
-
-
-def interior(idx, inter, vec, hop, pot, stk, after):
+    for copy in outs:
+        copy.wait()
+
+
+def interior(inter, vec, hop, pot, stk, after):
     _, nvec, rows, width = vec.shape
     chunks = width // LANES
-    group = 4
+    group = 2
     any_ = pl.BlockSpec(memory_space=pl.ANY)
-    smem = pl.BlockSpec(memory_space=pltpu.SMEM)
     half = jax.ShapeDtypeStruct((CHEB + 1, 4, chunks, rows // 2, LANES), F32)
-    n = chunks * (3 + nvec // group) + 2
+    n = 1 + chunks * (3 + nvec // group) + 2 * (CHEB + 1)
     return pl.pallas_call(
         functools.partial(interior_kernel, rows, chunks, nvec, group),
         out_shape=[half, half, jax.ShapeDtypeStruct((CHEB + 1, SUB, LANES), F32)],
-        in_specs=[smem, smem, any_, any_, any_, any_, any_],
+        in_specs=[any_] * 6,
         out_specs=[any_, any_, pl.BlockSpec(memory_space=pltpu.VMEM)],
         scratch_shapes=[
+            pltpu.SMEM(inter.shape, F32),
             pltpu.VMEM((4, nvec, chunks, rows + 2 * PAD, LANES), F32),
             pltpu.VMEM((4, group, chunks, rows + 2 * PAD, LANES), F32),
             pltpu.VMEM((4, group, chunks, rows + 2 * PAD, LANES), F32),
@@ -395,41 +414,56 @@
             flops=60_000_000, bytes_accessed=9_000_000, transcendentals=0
         ),
         name="interior",
-    )(idx, inter, vec, hop, pot, stk, after)
+    )(inter, vec, hop, pot, stk, after)
 
 
 WIN = 7
 GUARD = REC
 
 
-def gather_window(odd, refs, w, sems):
+def gather_window(refs, w, sems, part=None, dots=None, beside=()):
     own_long, own_short, got_long, got_short, extra = refs
-    three = 3 * REC
+    odd = place()[0]
     even = odd == 0
-
-    def both(first, second, dst, sem):
+    copies = []
+
+    def both(first, second, take, band, place_at, count):
+        src_at, dst_at = pl.ds(take * REC, count * REC), pl.ds(GUARD + place_at * REC, count * REC)
+        dst, sem = w.at[band, :, dst_at], sems.at[len(copies)]
+
         @pl.when(even)
         def _():
-            pltpu.make_async_copy(first, dst, sem).start()
+            pltpu.make_async_copy(first.at[:, src_at], dst, sem).start()
 
         @pl.when(jnp.logical_not(even))
         def _():
-            pltpu.make_async_copy(second, dst, sem).start()
-
-        return pltpu.make_async_copy(first, dst, sem)
-
-    copies = [
-        both(got_long, got_short, w.at[0, :, pl.ds(GUARD, three)], sems.at[0]),
-        both(own_long, own_short, w.at[0, :, pl.ds(GUARD + three, three)], sems.at[1]),
-        both(own_short, own_long, w.at[1, :, pl.ds(GUARD + REC, three)], sems.at[2]),
-        both(got_short, got_long, w.at[1, :, pl.ds(GUARD + REC + three, three)], sems.at[3]),
-    ]
-    for band, place in ((0, 6), (1, 0)):
-        copy = pltpu.make_async_copy(
-            extra.at[band], w.at[band, :, pl.ds(GUARD + place * REC, REC)], sems.at[4 + band]
-        )
+            pltpu.make_async_copy(second.at[:, src_at], dst, sem).start()
+
+        copies.append(pltpu.make_async_copy(first.at[:, src_at], dst, sem))
+
+    few = part is not None
+    if few:
+        both(got_long, got_short, 2, 0, 2, 1)
+        both(got_short, got_long, 0, 1, 4, 1)
+    else:
+        both(got_long, got_short, 0, 0, 0, 3)
+        both(got_short, got_long, 0, 1, 4, 3)
+    both(own_long, own_short, 0, 0, 3, 3)
+    both(own_short, own_long, 0, 1, 1, 3)
+    if few:
+        copy = pltpu.make_async_copy(part, dots, sems.at[len(copies)])
         copy.start()
         copies.append(copy)
+    else:
+        for band, place_at in ((0, 6), (1, 0)):
+            copy = pltpu.make_async_copy(
+                extra.at[band], w.at[band, :, pl.ds(GUARD + place_at * REC, REC)],
+                sems.at[len(copies)],
+            )
+            copy.start()
+            copies.append(copy)
+    for copy in beside:
+        copy.start()
     for copy in copies:
         copy.wait()
 
@@ -483,9 +517,9 @@
     return emit
 
 
-def totals_kernel(chunks, parts, idx, own_long, own_short, got_long, got_short, extra, part, tot,
-                  w, t1, dots, sems):
-    gather_window(idx[0], (own_long, own_short, got_long, got_short, extra), w, sems)
+def totals_kernel(chunks, parts, own_long, own_short, got_long, got_short, part, tot, w, t1, dots,
+                  sems):
+    gather_window((own_long, own_short, got_long, got_short, None), w, sems, part, dots)
 
     def first(j, carry):
         for band in range(2):
@@ -493,8 +527,7 @@
             window_step(chunks, 1, w, w, None, band, i, store_row(t1, band, i))
         return carry
 
-    lax.fori_loop(0, 4, first, 0)
-    dots[...] = part[...]
+    lax.fori_loop(0, 4, first, 0, unroll=2)
 
     def second(j, carry):
         for band in range(2):
@@ -515,7 +548,7 @@
                 dots[k] = dots[k] + sums[k]
         return carry
 
-    lax.fori_loop(0, 2, second, 0)
+    lax.fori_loop(0, 2, second, 0, unroll=2)
     lane = lax.broadcasted_iota(jnp.int32, (SUB, LANES), 1)
     row = jnp.zeros((SUB, LANES), F32)
     for m in range(5):
@@ -524,38 +557,47 @@
         tot[pl.ds(k * SUB, SUB), :] = row
 
 
-def totals_of(idx, records, part, parts):
+def totals_of(records, part, parts):
     chunks = records[0].shape[0]
     any_ = pl.BlockSpec(memory_space=pl.ANY)
-    smem = pl.BlockSpec(memory_space=pltpu.SMEM)
     vmem = pl.BlockSpec(memory_space=pltpu.VMEM)
     return pl.pallas_call(
         functools.partial(totals_kernel, chunks, parts),
         out_shape=jax.ShapeDtypeStruct((parts, LANES), F32),
-        in_specs=[smem, any_, any_, any_, any_, any_, vmem],
+        in_specs=[any_] * 5,
         out_specs=vmem,
         scratch_shapes=[
             pltpu.VMEM((2, chunks, (WIN + 2) * REC, LANES), F32),
             pltpu.VMEM((2, chunks, (WIN + 2) * 32, LANES), F32),
             pltpu.VMEM((5, SUB, LANES), F32),
-            pltpu.SemaphoreType.DMA((6,)),
+            pltpu.SemaphoreType.DMA((5,)),
         ],
         compiler_params=pltpu.CompilerParams(vmem_limit_bytes=VMEM_WIDE),
         cost_estimate=pl.CostEstimate(flops=8_000_000, bytes_accessed=4_000_000, transcendentals=0),
         name="totals",
-    )(idx, *records, part)
-
-
-def edges_kernel(chunks, idx, own_long, own_short, got_long, got_short, extra, after, out, w, t1,
-                 t2, res, sems):
+    )(*records[:4], part)
+
+
+def edges_kernel(chunks, half, own_long, own_short, got_long, got_short, extra, mine_in, other_in,
+                 after, out, w, t1, t2, res, mine, other, slab, sems):
     del after
-    gather_window(idx[0], (own_long, own_short, got_long, got_short, extra), w, sems)
+    inner = [
+        pltpu.make_async_copy(src, dst, sems.at[7 + k])
+        for k, (src, dst) in enumerate(((mine_in, mine), (other_in, other)))
+    ]
+    gather_window((own_long, own_short, got_long, got_short, extra), w, sems, beside=inner)
+    row = lax.broadcasted_iota(jnp.int32, (SUB, LANES), 0)
+    single, double = (row & 1) != 0, (row & 2) != 0
+
+    def merged(hit, a, b, shift):
+        return jnp.where(hit, b, a) + pltpu.roll(jnp.where(hit, a, b), shift, 0)
 
     def moments(band, i, c, order, values):
-        for s in range(4):
-            zero = window_slice(w, True, band, c, i, s)
-            term = jnp.sum(zero * values[s], axis=0, keepdims=True)
-            res[band, i - 2, c, pl.ds(order * 4 + s, 1), :] = term
+        p = [window_slice(w, True, band, c, i, s) * values[s] for s in range(4)]
+        pairs = [merged(single, p[2 * k], p[2 * k + 1], 1) for k in range(2)]
+        both = merged(double, pairs[0], pairs[1], 2)
+        both = both + pltpu.roll(both, 4, 0)
+        res[band, i - 2, c, pl.ds(order * 4, 4), :] = both[0:4]
 
     def sweep(order, first, last):
         source, before, target = {
@@ -575,7 +617,7 @@
                 window_step(chunks, order, w, source, before, band, i, emit)
             return carry
 
-        lax.fori_loop(0, last - first + 1, body, 0)
+        lax.fori_loop(0, last - first + 1, body, 0, unroll=1 if order == 4 else 2)
 
     def collect(order, ref):
         def body(j, carry):
@@ -596,33 +638,67 @@
     sweep(3, 1, 5)
     collect(3, t1)
     sweep(4, 2, 4)
-    away = pltpu.make_async_copy(res, out, sems.at[6])
+    for copy in inner:
+        copy.wait()
+    tall = 4 * half + SUB
+    core = place()[1]
+
+    def assemble(m, carry):
+        for c in range(chunks):
+            for s in range(4):
+                for g in range(half // SUB):
+                    at = pl.ds(g * SUB, SUB)
+                    slab[m, pl.ds(c * tall + s * half + g * SUB, SUB), :] = (
+                        mine[m, s, c, at, :] + other[m, s, c, at, :]
+                    )
+            for band, r in ((0, 0), (1, 2)):
+                halo = res[band, r, c, pl.ds(4 * m, 4), :]
+                slab[m, pl.ds(chunks * tall + band * SUB + c, 1), :] = jnp.sum(
+                    halo, axis=0, keepdims=True
+                )
+            for r in range(2):
+                upper = res[0, r + 1, c, pl.ds(4 * m, 4), :]
+                lower = res[1, r, c, pl.ds(4 * m, 4), :]
+                here = jnp.where(core == 0, upper, lower)
+                place_at = jnp.where(core == 0, r, half - 2 + r)
+                for s in range(4):
+                    slab[m, pl.ds(c * tall + s * half + place_at, 1), :] = here[s : s + 1]
+                slab[m, pl.ds(c * tall + 4 * half + 4 * r, 4), :] = jnp.where(
+                    core == 0, lower, upper
+                )
+        return carry
+
+    lax.fori_loop(0, CHEB + 1, assemble, 0)
+    away = pltpu.make_async_copy(slab, out, sems.at[6])
     away.start()
     away.wait()
 
 
-def edges(idx, records, after):
-    chunks = records[0].shape[0]
+def edges(records, mine, other, after):
+    _, _, chunks, half, _ = mine.shape
+    slabs = (CHEB + 1, chunks * (4 * half + SUB) + 2 * SUB, LANES)
     any_ = pl.BlockSpec(memory_space=pl.ANY)
-    smem = pl.BlockSpec(memory_space=pltpu.SMEM)
     return pl.pallas_call(
-        functools.partial(edges_kernel, chunks),
-        out_shape=jax.ShapeDtypeStruct((2, 3, chunks, 24, LANES), F32),
-        in_specs=[smem, any_, any_, any_, any_, any_, any_],
+        functools.partial(edges_kernel, chunks, half),
+        out_shape=jax.ShapeDtypeStruct(slabs, F32),
+        in_specs=[any_] * 8,
         out_specs=any_,
         scratch_shapes=[
             pltpu.VMEM((2, chunks, (WIN + 2) * REC, LANES), F32),
             pltpu.VMEM((2, chunks, (WIN + 2) * 32, LANES), F32),
             pltpu.VMEM((2, chunks, (WIN + 2) * 32, LANES), F32),
             pltpu.VMEM((2, 3, chunks, 24, LANES), F32),
-            pltpu.SemaphoreType.DMA((7,)),
+            pltpu.VMEM(mine.shape, F32),
+            pltpu.VMEM(mine.shape, F32),
+            pltpu.VMEM(slabs, F32),
+            pltpu.SemaphoreType.DMA((9,)),
         ],
-        compiler_params=pltpu.CompilerParams(vmem_limit_bytes=VMEM_LIMIT),
+        compiler_params=pltpu.CompilerParams(vmem_limit_bytes=VMEM_WIDE),
         cost_estimate=pl.CostEstimate(
             flops=20_000_000, bytes_accessed=4_000_000, transcendentals=0
         ),
         name="edges",
-    )(idx, *records, after)
+    )(*records, mine, other, after)
 
 
 ACOS = (
@@ -657,8 +733,7 @@
     return out
 
 
-def density_kernel(chunks, half, scale, sites, idx, filling, sums, mine, other, edge, out):
-    core = idx[1]
+def density_kernel(scale, sites, filling, sums, slabs, out):
     added = jnp.sum(sums[...], axis=0, keepdims=True) * scale
     lane = lax.broadcasted_iota(jnp.int32, (1, LANES), 1)
     totals = [jnp.sum(jnp.where(lane == m, added, 0.0)) for m in range(CHEB + 1)]
@@ -686,63 +761,31 @@
         low = low + below * step
     chem = jnp.full((SUB, LANES), low + 0.5 * step, F32)
     weights = [value * scale for value in weights_of(chem)]
-    tall = 4 * half + SUB
-
-    for c in range(chunks):
-        for s in range(4):
-            for g in range(half // SUB):
-                at = pl.ds(g * SUB, SUB)
-                acc = None
-                for m in range(CHEB + 1):
-                    term = weights[m] * (mine[m, s, c, at, :] + other[m, s, c, at, :])
-                    acc = term if acc is None else acc + term
-                out[pl.ds(c * tall + s * half + g * SUB, SUB), :] = acc
-        bands = []
-        for band in range(2):
-            rows = []
-            for r in range(3):
-                acc = None
-                for m in range(CHEB + 1):
-                    term = weights[m][0:4] * edge[band, r, c, pl.ds(4 * m, 4), :]
-                    acc = term if acc is None else acc + term
-                rows.append(acc)
-            bands.append(rows)
-            halo = rows[0] if band == 0 else rows[2]
-            out[pl.ds(chunks * tall + band * SUB + c, 1), :] = jnp.sum(halo, axis=0, keepdims=True)
-        upper, lower = bands[0][1:], bands[1][:2]
-
-        @pl.when(core == 0)
-        def _():
-            for r in range(2):
-                for s in range(4):
-                    out[pl.ds(c * tall + s * half + r, 1), :] = upper[r][s : s + 1]
-                out[pl.ds(c * tall + 4 * half + 4 * r, 4), :] = lower[r]
-
-        @pl.when(core != 0)
-        def _():
-            for r in range(2):
-                for s in range(4):
-                    out[pl.ds(c * tall + s * half + half - 2 + r, 1), :] = lower[r][s : s + 1]
-                out[pl.ds(c * tall + 4 * half + 4 * r, 4), :] = upper[r]
-
-
-def density(idx, filling, sums, mine, other, edge, vectors, sites):
-    _, _, chunks, half, _ = mine.shape
+    for k in range(out.shape[0] // SUB):
+        at = pl.ds(k * SUB, SUB)
+        acc = None
+        for m in range(CHEB + 1):
+            term = weights[m] * slabs[m, at, :]
+            acc = term if acc is None else acc + term
+        out[at, :] = acc
+
+
+def density(filling, sums, slabs, vectors, sites):
     smem = pl.BlockSpec(memory_space=pltpu.SMEM)
     vmem = pl.BlockSpec(memory_space=pltpu.VMEM)
     return pl.pallas_call(
-        functools.partial(density_kernel, chunks, half, 1.0 / vectors, float(sites)),
-        out_shape=jax.ShapeDtypeStruct((chunks * (4 * half + SUB) + 2 * SUB, LANES), F32),
-        in_specs=[smem, smem, vmem, vmem, vmem, vmem],
+        functools.partial(density_kernel, 1.0 / vectors, float(sites)),
+        out_shape=jax.ShapeDtypeStruct(slabs.shape[1:], F32),
+        in_specs=[smem, vmem, vmem],
         out_specs=vmem,
         compiler_params=pltpu.CompilerParams(vmem_limit_bytes=VMEM_LIMIT),
         cost_estimate=pl.CostEstimate(flops=2_000_000, bytes_accessed=4_000_000, transcendentals=0),
         name="density",
-    )(idx, filling, sums, mine, other, edge)
-
-
-def potential_kernel(chunks, half, idx, mine, other, out, dens, charge):
-    first = idx[1] == 0
+    )(filling, sums, slabs)
+
+
+def potential_kernel(chunks, half, mine, other, out, dens, charge):
+    first = place()[1] == 0
     tall = 4 * half + SUB
     guard = SUB
 
@@ -785,14 +828,13 @@
                 out[s, pl.ds(g * SUB, SUB), pl.ds(c * LANES, LANES)] = 3.0 * (value - 0.5) + base
 
 
-def new_potential(idx, mine, other, chunks):
+def new_potential(mine, other, chunks):
     half = ((mine.shape[0] - 2 * SUB) // chunks - SUB) // 4
-    smem = pl.BlockSpec(memory_space=pltpu.SMEM)
     vmem = pl.BlockSpec(memory_space=pltpu.VMEM)
     return pl.pallas_call(
         functools.partial(potential_kernel, chunks, half),
         out_shape=jax.ShapeDtypeStruct((4, 2 * half, chunks * LANES), F32),
-        in_specs=[smem, vmem, vmem],
+        in_specs=[vmem, vmem],
         out_specs=vmem,
         scratch_shapes=[
             pltpu.VMEM((4, chunks, 2 * half, LANES), F32),
@@ -801,21 +843,18 @@
         compiler_params=pltpu.CompilerParams(vmem_limit_bytes=VMEM_LIMIT),
         cost_estimate=pl.CostEstimate(flops=1_000_000, bytes_accessed=2_000_000, transcendentals=0),
         name="new_potential",
-    )(idx, mine, other)
+    )(mine, other)
 
 
 def per_device(vectors, hoppings, potential, stacking, interlayer, filling):
     strips, ranks = lax.axis_size("dom"), lax.axis_size("vec")
     _, nvec, rows, width = vectors.shape
-    dom, vec = lax.axis_index("dom"), lax.axis_index("vec")
-    idx = jnp.stack([dom % 2, vec % 2]).astype(jnp.int32)
     long_way = [(i, (i - 1 if i % 2 == 0 else i + 1) % strips) for i in range(strips)]
     short_way = [(i, i ^ 1) for i in range(strips)]
     sibling = [(i, i ^ 1) for i in range(ranks)]
     across = [(i, i ^ 2) for i in range(ranks)]
 
     own_long, own_short, extra = pack(
-        idx,
         interlayer,
         vectors.reshape(4 * nvec, rows, width),
         hoppings.reshape(6, rows, width),
@@ -824,19 +863,17 @@
     )
     got_long = lax.ppermute(own_long, "dom", long_way)
     got_short = lax.ppermute(own_short, "dom", short_way)
-    mine, yours, part = interior(
-        idx, interlayer, vectors, hoppings, potential, stacking, own_short
-    )
+    mine, yours, part = interior(interlayer, vectors, hoppings, potential, stacking, own_short)
     records = (own_long, own_short, got_long, got_short, extra)
-    totals = totals_of(idx, records, part, strips * ranks)
-    edge = edges(idx, records, totals)
+    totals = totals_of(records, part, strips * ranks)
     yours, ready = lax.optimization_barrier((yours, totals))
     other = lax.ppermute(yours, "vec", sibling)
+    slabs = edges(records, mine, other, totals)
     sums = lax.all_to_all(ready, ("dom", "vec"), 0, 0, tiled=True)
     sites = 4 * rows * width * strips
-    chip = density(idx, filling, sums, mine, other, edge, nvec * ranks, sites)
+    chip = density(filling, sums, slabs, nvec * ranks, sites)
     whole = chip + lax.ppermute(chip, "vec", across)
-    return new_potential(idx, whole, lax.ppermute(whole, "vec", sibling), width // LANES)
+    return new_potential(whole, lax.ppermute(whole, "vec", sibling), width // LANES)
 
 
 def solution(mesh):

time: 74.1 us -> 70.6 us (0.953)
  Pallas kernels: 35.9 us -> 29.7 us
  waiting for transfers between devices: 11.8 us -> 15.7 us
  local copies, waits for them, and re-layouts: 4.03 us -> 1.39 us
  starting transfers between devices: 20.4 us -> 22.9 us
    all_to_all x1, waiting for transfers between devices: 1.83 us -> 5.56 us  [per_device(): sums = lax.all_to_all(ready, ('dom', 'vec'), 0, 0, tiled=True)]
    pallas_call x1, Pallas kernels: 17.6 us -> 14.2 us  [interior(): pl.pallas_call(functools.partial(interior_kernel, rows, chunks, nvec, gro...]
    unnamed x12 -> x2, local copies, waits for them, and re-layouts: 4.03 us -> 1.39 us
    ppermute x1, starting transfers between devices: 0.01 us -> 2.21 us  [per_device(): got_short = lax.ppermute(own_short, 'dom', short_way)]
    ppermute x1, starting transfers between devices: 9.87 us -> 8.12 us  [per_device(): got_long = lax.ppermute(own_long, 'dom', long_way)]
    all_to_all x1, starting transfers between devices: 6.99 us -> 8.63 us  [per_device(): sums = lax.all_to_all(ready, ('dom', 'vec'), 0, 0, tiled=True)]
    pallas_call x1, Pallas kernels: 4.47 us -> 3.22 us  [totals_of(): pl.pallas_call(functools.partial(totals_kernel, chunks, parts), out_shape...]
  transfers between devices with their start and end apart: 6 -> 6, of which waited for: 3 -> 3; matrix products, arithmetic and copies ran while one was open for 0% -> 0% of each run, Pallas kernels for 33% -> 30%
where the time goes in v3:
time: 70.6 us; the launch traced here: 70.4 us
  Pallas kernels  29.7 us (42%)
  starting transfers between devices  22.9 us (32%)
  waiting for transfers between devices  15.7 us (22%)
  local copies, waits for them, and re-layouts  1.39 us (2%)
  between operations  0.72 us (1%)
    pallas_call x1, Pallas kernels, interior(): pl.pallas_call(functools.partial(interior_kernel, rows, chunks, nvec, gro...  14.2 us
    ppermute x1, waiting for transfers between devices, per_device(): whole = chip + lax.ppermute(chip, 'vec', across)  8.9 us
    all_to_all x1, starting transfers between devices, per_device(): sums = lax.all_to_all(ready, ('dom', 'vec'), 0, 0, tiled=True)  8.63 us
    ppermute x1, starting transfers between devices, per_device(): got_long = lax.ppermute(own_long, 'dom', long_way)  8.12 us
    pallas_call x1, Pallas kernels, edges(): pl.pallas_call(functools.partial(edges_kernel, chunks, half), out_shape=j...  6.85 us
    all_to_all x1, waiting for transfers between devices, per_device(): sums = lax.all_to_all(ready, ('dom', 'vec'), 0, 0, tiled=True)  5.56 us
    pallas_call x1, Pallas kernels, pack(): pl.pallas_call(functools.partial(pack_kernel, rows, chunks), out_shape=[m...  3.82 us
    pallas_call x1, Pallas kernels, totals_of(): pl.pallas_call(functools.partial(totals_kernel, chunks, parts), out_shape...  3.22 us
  transfers between devices with their start and end apart: 6, of which 3 were waited for; matrix products, arithmetic and copies ran while one was open for 0% of the time, Pallas kernels for 30%

profile of v3, /device:TPU:1, one launch (start us, length us, event | category | flops | bytes accessed | tf_op | source)
XLA Modules:
  0.0 70.4 jit_solution(16974191508094168120)
XLA Ops:
  0.0 3.8 %pack.1 = (f32[8,144,128]{2,1,0:T(8,128)}, f32[8,144,128]{2,1,0:T(8,128)}, f32[2,8,48,128]{3,2,1,0:T(8,128)}) custom-call(f32[2,8]{1,0:T(2,128)} %table.3, f32[32,32,1024]{2,1,0:T(8,128)} %bitcast.7, f32[6,32,1024]{2,1,0:T(8,128)} %bitcast.8, f32[4,32,1024]{2,1,0:T(8,128)} %pot.3, s32[32,1024]{1,0:T(8,128)} %stk.3), custom_call_target="tpu_custom_call" | custom-call | flops 1000000 | bytes 4000000 | tf_op jit(solution)/shard_map/pack/pallas_call | solution.py:174
  3.8 2.2 %collective-permute-start.1 = (f32[8,144,128]{2,1,0:T(8,128)}, f32[8,144,128]{2,1,0:T(8,128)}, u32[]{:S(2)}, u32[]{:S(2)}) collective-permute-start(f32[8,144,128]{2,1,0:T(8,128)} %get-tuple-element.13.after.own_short), channel_id=1, source_target_pairs={{0,4},{4,0},{8,12},{12,8},{16,20},{20,16},{24,28},{28,24},{32,36},... | collective-permute-start | bytes 1769480 | tf_op jit(solution)/shard_map/ppermute | solution.py:865
  6.0 8.1 %collective-permute-start = (f32[8,144,128]{2,1,0:T(8,128)}, f32[8,144,128]{2,1,0:T(8,128)}, u32[]{:S(2)}, u32[]{:S(2)}) collective-permute-start(f32[8,144,128]{2,1,0:T(8,128)} %get-tuple-element.15.own_long), channel_id=1, source_target_pairs={{0,252},{4,8},{8,4},{12,16},{16,12},{20,24},{24,20},{28,32},{32,28... | collective-permute-start | bytes 1769480 | tf_op jit(solution)/shard_map/ppermute | solution.py:864
  14.2 14.2 %interior.1 = (f32[5,4,8,16,128]{4,3,2,1,0:T(8,128)}, f32[5,4,8,16,128]{4,3,2,1,0:T(8,128)}, f32[5,8,128]{2,1,0:T(8,128)}) custom-call(f32[2,8]{1,0:T(2,128)} %table.3, f32[4,8,32,1024]{3,2,1,0:T(8,128)} %vec.1, f32[2,3,32,1024]{3,2,1,0:T(8,128)} %hop.1, f32[4,32,1024]{2,1,0:T(8,128)} %pot.3, s32[32,1024]{1,0:T(8,128)} %stk.3, ...), custom_call_target="tpu_custom_call" | custom-call | flops 60000000 | bytes 9000000 | tf_op jit(solution)/shard_map/interior/pallas_call | solution.py:394
  28.3 0.0 collective-permute-done.1.got_short
  28.4 0.0 collective-permute-done.got_long
  28.4 3.2 %totals.1.after = f32[256,128]{1,0:T(8,128)} custom-call(f32[8,144,128]{2,1,0:T(8,128)} %get-tuple-element.15.own_long, f32[8,144,128]{2,1,0:T(8,128)} %get-tuple-element.13.after.own_short, f32[8,144,128]{2,1,0:T(8,128)} %collective-permute-done.got_long, f32[8,144,128]{2,1,0:T(8,128)} %collective-permute-done.1.got_short, f32[5,8,128]{2,1,0:T(8,128)} %get-tuple-element.16.part), custom_call_target="tpu_custom_call" | custom-call | flops 8000000 | bytes 4000000 | tf_op jit(solution)/shard_map/totals/pallas_call | solution.py:564
  31.6 1.5 %collective-permute-start.2 = (f32[5,4,8,16,128]{4,3,2,1,0:T(8,128)}, f32[5,4,8,16,128]{4,3,2,1,0:T(8,128)}, u32[]{:S(2)}, u32[]{:S(2)}) collective-permute-start(f32[5,4,8,16,128]{4,3,2,1,0:T(8,128)} %get-tuple-element.20), channel_id=1, source_target_pairs={{0,1},{1,0},{2,3},{3,2},{4,5},{5,4},{6,7},{7,6},{8,9},{9,8},{10,11... | collective-permute-start | bytes 3932168 | tf_op jit(solution)/shard_map/ppermute | solution.py:870
  33.1 8.6 %all-to-all-start = ((f32[256,1,128]{2,1,0:T(1,128)}), f32[256,1,128]{2,1,0:T(1,128)S(1)}, u32[]{:S(2)}, u32[]{:S(2)}) async-start(f32[256,1,128]{2,1,0:T(1,128)} %bitcast.9), calls=%async_computation | async-start | bytes 262144 | tf_op jit(solution)/shard_map/all_to_all | solution.py:872
  42.4 0.0 collective-permute-done.2.other_in
  42.4 6.8 %edges.1.slabs = f32[5,592,128]{2,1,0:T(8,128)} custom-call(f32[8,144,128]{2,1,0:T(8,128)} %get-tuple-element.15.own_long, f32[8,144,128]{2,1,0:T(8,128)} %get-tuple-element.13.after.own_short, f32[8,144,128]{2,1,0:T(8,128)} %collective-permute-done.got_long, f32[8,144,128]{2,1,0:T(8,128)} %collective-permute-done.1.got_short, ...), custom_call_target="tpu_custom_call" | custom-call | flops 20000000 | bytes 4000000 | tf_op jit(solution)/shard_map/edges/pallas_call | solution.py:681
  49.3 5.6 %all-to-all-done = f32[256,1,128]{2,1,0:T(1,128)S(1)} async-done(((f32[256,1,128]{2,1,0:T(1,128)}), f32[256,1,128]{2,1,0:T(1,128)S(1)}, u32[]{:S(2)}, u32[]{:S(2)}) %all-to-all-start) | async-done | bytes 131104 | tf_op jit(solution)/shard_map/all_to_all | solution.py:872
  54.8 0.0 copy-start
  54.8 1.4 %copy-done = f32[5,592,128]{2,1,0:T(8,128)S(1)} copy-done((f32[5,592,128]{2,1,0:T(8,128)S(1)}, f32[5,592,128]{2,1,0:T(8,128)}, u32[]{:S(2)}) %copy-start) | copy-done | bytes 1515544
  56.2 0.5 density.1
  56.8 1.0 %collective-permute-start.3 = (f32[592,128]{1,0:T(8,128)S(1)}, f32[592,128]{1,0:T(8,128)S(1)}, u32[]{:S(2)}, u32[]{:S(2)}) collective-permute-start(f32[592,128]{1,0:T(8,128)S(1)} %density.1), channel_id=1, source_target_pairs={{0,2},{1,3},{2,0},{3,1},{4,6},{5,7},{6,4},{7,5},{8,10},{9,11},{10,... | collective-permute-start | bytes 909320 | tf_op jit(solution)/shard_map/ppermute | solution.py:875
  57.8 8.9 %collective-permute-done.3 = f32[592,128]{1,0:T(8,128)S(1)} collective-permute-done((f32[592,128]{1,0:T(8,128)S(1)}, f32[592,128]{1,0:T(8,128)S(1)}, u32[]{:S(2)}, u32[]{:S(2)}) %collective-permute-start.3) | collective-permute-done | bytes 303136 | tf_op jit(solution)/shard_map/ppermute | solution.py:875
  66.7 1.4 %collective-permute-start.4 = (f32[592,128]{1,0:T(8,128)S(1)}, f32[592,128]{1,0:T(8,128)S(1)}, u32[]{:S(2)}, u32[]{:S(2)}) collective-permute-start(f32[592,128]{1,0:T(8,128)S(1)} %add.3.mine), channel_id=1, source_target_pairs={{0,1},{1,0},{2,3},{3,2},{4,5},{5,4},{6,7},{7,6},{8,9},{9,8},{10,11... | collective-permute-start | bytes 909320 | tf_op jit(solution)/shard_map/ppermute | solution.py:876
  68.1 1.2 %collective-permute-done.4.other = f32[592,128]{1,0:T(8,128)S(1)} collective-permute-done((f32[592,128]{1,0:T(8,128)S(1)}, f32[592,128]{1,0:T(8,128)S(1)}, u32[]{:S(2)}, u32[]{:S(2)}) %collective-permute-start.4) | collective-permute-done | bytes 303136 | tf_op jit(solution)/shard_map/ppermute | solution.py:876
  69.3 1.1 %new_potential.1 = f32[4,32,1024]{2,1,0:T(8,128)} custom-call(f32[592,128]{1,0:T(8,128)S(1)} %add.3.mine, f32[592,128]{1,0:T(8,128)S(1)} %collective-permute-done.4.other), custom_call_target="tpu_custom_call" | custom-call | flops 1000000 | bytes 2000000 | tf_op jit(solution)/shard_map/new_potential/pallas_call | solution.py:834
  (1 shorter events, 0.0 us)
Async XLA Ops:
  3.8 24.5 %collective-permute-start.1 = (f32[8,144,128]{2,1,0:T(8,128)}, f32[8,144,128]{2,1,0:T(8,128)}, u32[]{:S(2)}, u32[]{:S(2)}) collective-permute-start(f32[8,144,128]{2,1,0:T(8,128)} %get-tuple-element.13.after.own_short), channel_id=1, source_target_pairs={{0,4},{4,0},{8,12},{12,8},{16,20},{20,16},{24,28},{28,24},{32,36},... | collective-permute-start | bytes 1769480 | tf_op jit(solution)/shard_map/ppermute | solution.py:865
  6.0 22.3 %collective-permute-start = (f32[8,144,128]{2,1,0:T(8,128)}, f32[8,144,128]{2,1,0:T(8,128)}, u32[]{:S(2)}, u32[]{:S(2)}) collective-permute-start(f32[8,144,128]{2,1,0:T(8,128)} %get-tuple-element.15.own_long), channel_id=1, source_target_pairs={{0,252},{4,8},{8,4},{12,16},{16,12},{20,24},{24,20},{28,32},{32,28... | collective-permute-start | bytes 1769480 | tf_op jit(solution)/shard_map/ppermute | solution.py:864
  31.6 10.8 %collective-permute-start.2 = (f32[5,4,8,16,128]{4,3,2,1,0:T(8,128)}, f32[5,4,8,16,128]{4,3,2,1,0:T(8,128)}, u32[]{:S(2)}, u32[]{:S(2)}) collective-permute-start(f32[5,4,8,16,128]{4,3,2,1,0:T(8,128)} %get-tuple-element.20), channel_id=1, source_target_pairs={{0,1},{1,0},{2,3},{3,2},{4,5},{5,4},{6,7},{7,6},{8,9},{9,8},{10,11... | collective-permute-start | bytes 3932168 | tf_op jit(solution)/shard_map/ppermute | solution.py:870
  33.1 21.7 %all-to-all-start = ((f32[256,1,128]{2,1,0:T(1,128)}), f32[256,1,128]{2,1,0:T(1,128)S(1)}, u32[]{:S(2)}, u32[]{:S(2)}) async-start(f32[256,1,128]{2,1,0:T(1,128)} %bitcast.9), calls=%async_computation | async-start | bytes 262144 | tf_op jit(solution)/shard_map/all_to_all | solution.py:872
  54.8 1.4 %copy-start = (f32[5,592,128]{2,1,0:T(8,128)S(1)}, f32[5,592,128]{2,1,0:T(8,128)}, u32[]{:S(2)}) copy-start(f32[5,592,128]{2,1,0:T(8,128)} %edges.1.slabs) | copy-start | bytes 4546564
  56.8 9.9 %collective-permute-start.3 = (f32[592,128]{1,0:T(8,128)S(1)}, f32[592,128]{1,0:T(8,128)S(1)}, u32[]{:S(2)}, u32[]{:S(2)}) collective-permute-start(f32[592,128]{1,0:T(8,128)S(1)} %density.1), channel_id=1, source_target_pairs={{0,2},{1,3},{2,0},{3,1},{4,6},{5,7},{6,4},{7,5},{8,10},{9,11},{10,... | collective-permute-start | bytes 909320 | tf_op jit(solution)/shard_map/ppermute | solution.py:875
  66.7 2.6 %collective-permute-start.4 = (f32[592,128]{1,0:T(8,128)S(1)}, f32[592,128]{1,0:T(8,128)S(1)}, u32[]{:S(2)}, u32[]{:S(2)}) collective-permute-start(f32[592,128]{1,0:T(8,128)S(1)} %add.3.mine), channel_id=1, source_target_pairs={{0,1},{1,0},{2,3},{3,2},{4,5},{5,4},{6,7},{7,6},{8,9},{9,8},{10,11... | collective-permute-start | bytes 909320 | tf_op jit(solution)/shard_map/ppermute | solution.py:876

commit v4 on v3

--- a/solution.py
+++ b/solution.py
@@ -17,6 +17,11 @@
 F32 = jnp.float32
 VMEM_LIMIT = 44 * 1024 * 1024
 VMEM_WIDE = 64 * 1024 * 1024 - 256 * 1024
+SLOT = (0, 3, 5, 8, 1, 4, 6, 9, 10, 12, 11, 13, 7, 2)
+FAR = COEF + 8
+NEAR = 2 * REC
+MESSAGE = NEAR + FAR
+EXTRA = REC + 8
 
 
 def jackson(count):
@@ -140,27 +145,45 @@
                 table = [inter[w, k] * 0.25 for k in range(inter.shape[1])]
                 coef.append(pick(classes, table))
             for k, value in enumerate(coef):
-                rec[band, c, pl.ds(COEF + k, 4, stride=REC), :] = value[first : first + 4]
+                at = pl.ds(COEF + SLOT[k], 4, stride=REC)
+                rec[band, c, at, :] = value[first : first + 4]
             zero = jnp.zeros((4, LANES), F32)
             for k in range(len(coef), REC - COEF):
                 rec[band, c, pl.ds(COEF + k, 4, stride=REC), :] = zero
-            message = rec.at[band, c, pl.ds(band * REC, 3 * REC)]
-            spare = rec.at[band, c, pl.ds((1 - band) * 3 * REC, REC)]
-            away = pltpu.make_async_copy(spare, extra.at[band, c], sems.at[n])
-            away.start()
-            outs.append(away)
-            n += 1
-
-            @pl.when(odd == band)
-            def _():
-                pltpu.make_async_copy(message, long_out.at[c], sems.at[n]).start()
-
-            @pl.when(odd != band)
-            def _():
-                pltpu.make_async_copy(message, short_out.at[c], sems.at[n]).start()
-
-            outs.append(pltpu.make_async_copy(message, long_out.at[c], sems.at[n]))
-            n += 1
+            third = (2, 5)[band]
+            for r, slot, k in (
+                ((0, 14, 8), (0, 15, 10)),
+                ((2, 14, 3), (2, 15, 7), (3, 14, 9), (3, 15, 11)),
+            )[band]:
+                rec[band, c, pl.ds(r * REC + COEF + slot, 1), :] = coef[k][third : third + 1]
+            third_at = (2, 1)[band] * REC
+            parts = (
+                (pl.ds((0, 2)[band] * REC, NEAR), pl.ds(0, NEAR)),
+                (pl.ds(third_at, FAR), pl.ds(NEAR, FAR)),
+            )
+            for src_at, dst_at in (
+                (pl.ds((1 - band) * 3 * REC, REC), pl.ds(0, REC)),
+                (pl.ds(third_at + FAR, REC - FAR), pl.ds(REC, REC - FAR)),
+            ):
+                away = pltpu.make_async_copy(
+                    rec.at[band, c, src_at], extra.at[band, c, dst_at], sems.at[n]
+                )
+                away.start()
+                outs.append(away)
+                n += 1
+            for src_at, dst_at in parts:
+                src, sem = rec.at[band, c, src_at], sems.at[n]
+
+                @pl.when(odd == band)
+                def _():
+                    pltpu.make_async_copy(src, long_out.at[c, dst_at], sem).start()
+
+                @pl.when(odd != band)
+                def _():
+                    pltpu.make_async_copy(src, short_out.at[c, dst_at], sem).start()
+
+                outs.append(pltpu.make_async_copy(src, long_out.at[c, dst_at], sem))
+                n += 1
     for copy in outs:
         copy.wait()
 
@@ -169,11 +192,11 @@
     fields, rows, width = vec.shape
     chunks = width // LANES
     any_ = pl.BlockSpec(memory_space=pl.ANY)
-    message = jax.ShapeDtypeStruct((chunks, 3 * REC, LANES), F32)
+    message = jax.ShapeDtypeStruct((chunks, MESSAGE, LANES), F32)
     n_in = 2 * chunks * 4 + 1
     return pl.pallas_call(
         functools.partial(pack_kernel, rows, chunks),
-        out_shape=[message, message, jax.ShapeDtypeStruct((2, chunks, REC, LANES), F32)],
+        out_shape=[message, message, jax.ShapeDtypeStruct((2, chunks, EXTRA, LANES), F32)],
         in_specs=[any_, any_, any_, any_, any_],
         out_specs=[any_, any_, any_],
         scratch_shapes=[
@@ -183,7 +206,7 @@
             pltpu.VMEM((2, chunks, 4, SUB, LANES), F32),
             pltpu.VMEM((2, chunks, SUB, LANES), jnp.int32),
             pltpu.VMEM((2, chunks, 4 * REC, LANES), F32),
-            pltpu.SemaphoreType.DMA((n_in + 4 * chunks,)),
+            pltpu.SemaphoreType.DMA((n_in + 8 * chunks,)),
         ],
         compiler_params=pltpu.CompilerParams(vmem_limit_bytes=VMEM_WIDE),
         cost_estimate=pl.CostEstimate(flops=1_000_000, bytes_accessed=4_000_000, transcendentals=0),
@@ -195,7 +218,7 @@
 
 
 def interior_kernel(rows, chunks, nvec, group, table, vec, hop, pot, stk, after, keep, send, tot,
-                    inter, x, t1, t2, hp, pt, st, ww, mom, dots, sems):
+                    inter, x, t1, t2, hp, pt, st, ww, mom, dots, ends, sems):
     del after
     halves = nvec // group
     copies = [pltpu.make_async_copy(table, inter, sems.at[0])]
@@ -300,6 +323,8 @@
                     for s in range(4):
                         if order == 1:
                             value = new[s] * 0.5
+                        elif order == CHEB:
+                            value = new[s]
                         else:
                             ref, shift = before
                             value = new[s] - load(ref, s, v + shift, c, mid)
@@ -318,6 +343,8 @@
                 for s in range(4):
                     if q > 0:
                         sums[s] = sums[s] + mom[order, s, c, plain, :]
+                    if order == CHEB and q == halves - 1:
+                        sums[s] = sums[s] - mom[order - 2, s, c, plain, :]
                     mom[order, s, c, plain, :] = sums[s]
                     if order == 1:
                         if q > 0:
@@ -377,9 +404,12 @@
 
     sums = lax.fori_loop(0, groups, add_up, tuple(jnp.zeros((SUB, LANES), F32) for _ in range(3)))
     for m in range(3):
-        tot[m] = sums[m]
+        ends[m] = sums[m]
     for k in range(2):
-        tot[3 + k] = dots[k]
+        ends[3 + k] = dots[k]
+    last = pltpu.make_async_copy(ends, tot, sems.at[n + 2 * (CHEB + 1)])
+    last.start()
+    outs.append(last)
     for copy in outs:
         copy.wait()
 
@@ -390,12 +420,12 @@
     group = 2
     any_ = pl.BlockSpec(memory_space=pl.ANY)
     half = jax.ShapeDtypeStruct((CHEB + 1, 4, chunks, rows // 2, LANES), F32)
-    n = 1 + chunks * (3 + nvec // group) + 2 * (CHEB + 1)
+    n = 2 + chunks * (3 + nvec // group) + 2 * (CHEB + 1)
     return pl.pallas_call(
         functools.partial(interior_kernel, rows, chunks, nvec, group),
         out_shape=[half, half, jax.ShapeDtypeStruct((CHEB + 1, SUB, LANES), F32)],
         in_specs=[any_] * 6,
-        out_specs=[any_, any_, pl.BlockSpec(memory_space=pltpu.VMEM)],
+        out_specs=[any_, any_, any_],
         scratch_shapes=[
             pltpu.SMEM(inter.shape, F32),
             pltpu.VMEM((4, nvec, chunks, rows + 2 * PAD, LANES), F32),
@@ -407,6 +437,7 @@
             pltpu.VMEM((2, chunks, rows, LANES), F32),
             pltpu.VMEM((CHEB + 1, 4, chunks, rows, LANES), F32),
             pltpu.VMEM((2, SUB, LANES), F32),
+            pltpu.VMEM((CHEB + 1, SUB, LANES), F32),
             pltpu.SemaphoreType.DMA((n,)),
         ],
         compiler_params=pltpu.CompilerParams(vmem_limit_bytes=VMEM_WIDE),
@@ -421,14 +452,13 @@
 GUARD = REC
 
 
-def gather_window(refs, w, sems, part=None, dots=None, beside=()):
+def gather_window(refs, w, sems, part=None, dots=None, share=None, filling=None, beside=()):
     own_long, own_short, got_long, got_short, extra = refs
     odd = place()[0]
     even = odd == 0
     copies = []
 
-    def both(first, second, take, band, place_at, count):
-        src_at, dst_at = pl.ds(take * REC, count * REC), pl.ds(GUARD + place_at * REC, count * REC)
+    def both(first, second, band, src_at, dst_at):
         dst, sem = w.at[band, :, dst_at], sems.at[len(copies)]
 
         @pl.when(even)
@@ -441,31 +471,45 @@
 
         copies.append(pltpu.make_async_copy(first.at[:, src_at], dst, sem))
 
+    def at(record, size):
+        return pl.ds(GUARD + record * REC, size)
+
     few = part is not None
     if few:
-        both(got_long, got_short, 2, 0, 2, 1)
-        both(got_short, got_long, 0, 1, 4, 1)
+        both(got_long, got_short, 0, pl.ds(REC, REC), at(2, REC))
+        both(got_short, got_long, 1, pl.ds(0, REC), at(4, REC))
     else:
-        both(got_long, got_short, 0, 0, 0, 3)
-        both(got_short, got_long, 0, 1, 4, 3)
-    both(own_long, own_short, 0, 0, 3, 3)
-    both(own_short, own_long, 0, 1, 1, 3)
+        both(got_long, got_short, 0, pl.ds(0, NEAR), at(1, NEAR))
+        both(got_short, got_long, 1, pl.ds(0, NEAR), at(4, NEAR))
+        both(got_long, got_short, 0, pl.ds(NEAR, FAR), at(0, FAR))
+        both(got_short, got_long, 1, pl.ds(NEAR, FAR), at(6, FAR))
+    both(own_long, own_short, 0, pl.ds(0, NEAR), at(3, NEAR))
+    both(own_short, own_long, 1, pl.ds(0, NEAR), at(2, NEAR))
+    both(own_long, own_short, 0, pl.ds(NEAR, FAR), at(5, FAR))
+    both(own_short, own_long, 1, pl.ds(NEAR, FAR), at(1, FAR))
+    plain = [
+        (extra.at[0, :, pl.ds(REC, REC - FAR)], w.at[0, :, pl.ds(GUARD + 5 * REC + FAR, REC - FAR)]),
+        (extra.at[1, :, pl.ds(REC, REC - FAR)], w.at[1, :, pl.ds(GUARD + REC + FAR, REC - FAR)]),
+    ]
     if few:
-        copy = pltpu.make_async_copy(part, dots, sems.at[len(copies)])
+        plain.extend(((part, dots), (share, filling)))
+    else:
+        plain.append((extra.at[0, :, pl.ds(0, REC)], w.at[0, :, at(6, REC)]))
+        plain.append((extra.at[1, :, pl.ds(0, REC)], w.at[1, :, at(0, REC)]))
+    for src, dst in plain:
+        copy = pltpu.make_async_copy(src, dst, sems.at[len(copies)])
         copy.start()
         copies.append(copy)
-    else:
-        for band, place_at in ((0, 6), (1, 0)):
-            copy = pltpu.make_async_copy(
-                extra.at[band], w.at[band, :, pl.ds(GUARD + place_at * REC, REC)],
-                sems.at[len(copies)],
-            )
-            copy.start()
-            copies.append(copy)
+    for copy in copies:
+        copy.wait()
     for copy in beside:
         copy.start()
-    for copy in copies:
-        copy.wait()
+    if not few:
+        for band, r, slot, to, to_slot in ((0, 1, 14, 0, 8), (0, 2, 14, 0, 12), (1, 4, 14, 6, 10)):
+            for c in range(w.shape[1]):
+                w[band, c, pl.ds(GUARD + to * REC + COEF + to_slot, 2), :] = w[
+                    band, c, pl.ds(GUARD + r * REC + COEF + slot, 2), :
+                ]
 
 
 def window_slice(ref, is_w, band, c, i, site):
@@ -480,7 +524,7 @@
         return window_slice(source, from_w, band, c, i + shift, site)
 
     def coef_at(k, c, shift=0):
-        at = GUARD + (i + shift) * REC + COEF + k
+        at = GUARD + (i + shift) * REC + COEF + SLOT[k]
         return jnp.broadcast_to(w[band, c, pl.ds(at, 1), :], (SUB, LANES))
 
     b_prev = [roll_right(here(2 * l + 1, chunks - 1)) for l in range(2)]
@@ -517,9 +561,10 @@
     return emit
 
 
-def totals_kernel(chunks, parts, own_long, own_short, got_long, got_short, part, tot, w, t1, dots,
-                  sems):
-    gather_window((own_long, own_short, got_long, got_short, None), w, sems, part, dots)
+def totals_kernel(chunks, parts, own_long, own_short, got_long, got_short, extra, part, share, tot,
+                  w, t1, dots, filling, sems):
+    records = (own_long, own_short, got_long, got_short, extra)
+    gather_window(records, w, sems, part, dots, share, filling)
 
     def first(j, carry):
         for band in range(2):
@@ -553,36 +598,38 @@
     row = jnp.zeros((SUB, LANES), F32)
     for m in range(5):
         row = jnp.where(lane == m, jnp.sum(dots[m]), row)
+    row = jnp.where(lane == 5, filling[0], row)
     for k in range(parts // SUB):
         tot[pl.ds(k * SUB, SUB), :] = row
 
 
-def totals_of(records, part, parts):
+def totals_of(records, part, filling, parts):
     chunks = records[0].shape[0]
     any_ = pl.BlockSpec(memory_space=pl.ANY)
     vmem = pl.BlockSpec(memory_space=pltpu.VMEM)
     return pl.pallas_call(
         functools.partial(totals_kernel, chunks, parts),
         out_shape=jax.ShapeDtypeStruct((parts, LANES), F32),
-        in_specs=[any_] * 5,
+        in_specs=[any_] * 7,
         out_specs=vmem,
         scratch_shapes=[
             pltpu.VMEM((2, chunks, (WIN + 2) * REC, LANES), F32),
             pltpu.VMEM((2, chunks, (WIN + 2) * 32, LANES), F32),
             pltpu.VMEM((5, SUB, LANES), F32),
-            pltpu.SemaphoreType.DMA((5,)),
+            pltpu.SMEM((1,), F32),
+            pltpu.SemaphoreType.DMA((10,)),
         ],
         compiler_params=pltpu.CompilerParams(vmem_limit_bytes=VMEM_WIDE),
         cost_estimate=pl.CostEstimate(flops=8_000_000, bytes_accessed=4_000_000, transcendentals=0),
         name="totals",
-    )(*records[:4], part)
+    )(*records, part, filling)
 
 
 def edges_kernel(chunks, half, own_long, own_short, got_long, got_short, extra, mine_in, other_in,
                  after, out, w, t1, t2, res, mine, other, slab, sems):
     del after
     inner = [
-        pltpu.make_async_copy(src, dst, sems.at[7 + k])
+        pltpu.make_async_copy(src, dst, sems.at[12 + k])
         for k, (src, dst) in enumerate(((mine_in, mine), (other_in, other)))
     ]
     gather_window((own_long, own_short, got_long, got_short, extra), w, sems, beside=inner)
@@ -643,35 +690,34 @@
     tall = 4 * half + SUB
     core = place()[1]
 
-    def assemble(m, carry):
+    outs = []
+    for m in range(CHEB + 1):
         for c in range(chunks):
+            upper = [res[0, r + 1, c, pl.ds(4 * m, 4), :] for r in range(2)]
+            lower = [res[1, r, c, pl.ds(4 * m, 4), :] for r in range(2)]
+            own = [jnp.where(core == 0, upper[r], lower[r]) for r in range(2)]
+            rest = [jnp.where(core == 0, lower[r], upper[r]) for r in range(2)]
+            places = [jnp.where(core == 0, r, half - 2 + r) for r in range(2)]
             for s in range(4):
                 for g in range(half // SUB):
                     at = pl.ds(g * SUB, SUB)
-                    slab[m, pl.ds(c * tall + s * half + g * SUB, SUB), :] = (
-                        mine[m, s, c, at, :] + other[m, s, c, at, :]
-                    )
+                    value = mine[m, s, c, at, :] + other[m, s, c, at, :]
+                    for r in range(2):
+                        hit = row + g * SUB == places[r]
+                        value = jnp.where(hit, own[r][s : s + 1], value)
+                    slab[m, pl.ds(c * tall + s * half + g * SUB, SUB), :] = value
+            for r in range(2):
+                slab[m, pl.ds(c * tall + 4 * half + 4 * r, 4), :] = rest[r]
             for band, r in ((0, 0), (1, 2)):
                 halo = res[band, r, c, pl.ds(4 * m, 4), :]
                 slab[m, pl.ds(chunks * tall + band * SUB + c, 1), :] = jnp.sum(
                     halo, axis=0, keepdims=True
                 )
-            for r in range(2):
-                upper = res[0, r + 1, c, pl.ds(4 * m, 4), :]
-                lower = res[1, r, c, pl.ds(4 * m, 4), :]
-                here = jnp.where(core == 0, upper, lower)
-                place_at = jnp.where(core == 0, r, half - 2 + r)
-                for s in range(4):
-                    slab[m, pl.ds(c * tall + s * half + place_at, 1), :] = here[s : s + 1]
-                slab[m, pl.ds(c * tall + 4 * half + 4 * r, 4), :] = jnp.where(
-                    core == 0, lower, upper
-                )
-        return carry
-
-    lax.fori_loop(0, CHEB + 1, assemble, 0)
-    away = pltpu.make_async_copy(slab, out, sems.at[6])
-    away.start()
-    away.wait()
+        away = pltpu.make_async_copy(slab.at[m], out.at[m], sems.at[m])
+        away.start()
+        outs.append(away)
+    for copy in outs:
+        copy.wait()
 
 
 def edges(records, mine, other, after):
@@ -691,7 +737,7 @@
             pltpu.VMEM(mine.shape, F32),
             pltpu.VMEM(mine.shape, F32),
             pltpu.VMEM(slabs, F32),
-            pltpu.SemaphoreType.DMA((9,)),
+            pltpu.SemaphoreType.DMA((14,)),
         ],
         compiler_params=pltpu.CompilerParams(vmem_limit_bytes=VMEM_WIDE),
         cost_estimate=pl.CostEstimate(
@@ -733,13 +779,13 @@
     return out
 
 
-def density_kernel(scale, sites, filling, sums, slabs, out):
+def density_kernel(scale, sites, sums, slabs, out):
     added = jnp.sum(sums[...], axis=0, keepdims=True) * scale
     lane = lax.broadcasted_iota(jnp.int32, (1, LANES), 1)
     totals = [jnp.sum(jnp.where(lane == m, added, 0.0)) for m in range(CHEB + 1)]
     totals[3] = 2.0 * totals[3] - totals[1]
     totals[4] = 2.0 * totals[4] - totals[0]
-    target = filling[0] * sites
+    target = jnp.sum(jnp.where(lane == 5, sums[0:1, :], 0.0)) * sites
 
     point = (
         lax.broadcasted_iota(jnp.int32, (SUB, LANES), 0) * LANES
@@ -760,7 +806,7 @@
         below = jnp.sum(jnp.where(valid & (count < target), 1.0, 0.0))
         low = low + below * step
     chem = jnp.full((SUB, LANES), low + 0.5 * step, F32)
-    weights = [value * scale for value in weights_of(chem)]
+    weights = weights_of(chem)
     for k in range(out.shape[0] // SUB):
         at = pl.ds(k * SUB, SUB)
         acc = None
@@ -770,18 +816,17 @@
         out[at, :] = acc
 
 
-def density(filling, sums, slabs, vectors, sites):
-    smem = pl.BlockSpec(memory_space=pltpu.SMEM)
+def density(sums, slabs, vectors, sites):
     vmem = pl.BlockSpec(memory_space=pltpu.VMEM)
     return pl.pallas_call(
         functools.partial(density_kernel, 1.0 / vectors, float(sites)),
         out_shape=jax.ShapeDtypeStruct(slabs.shape[1:], F32),
-        in_specs=[smem, vmem, vmem],
+        in_specs=[vmem, vmem],
         out_specs=vmem,
         compiler_params=pltpu.CompilerParams(vmem_limit_bytes=VMEM_LIMIT),
         cost_estimate=pl.CostEstimate(flops=2_000_000, bytes_accessed=4_000_000, transcendentals=0),
         name="density",
-    )(filling, sums, slabs)
+    )(sums, slabs)
 
 
 def potential_kernel(chunks, half, mine, other, out, dens, charge):
@@ -863,15 +908,15 @@
     )
     got_long = lax.ppermute(own_long, "dom", long_way)
     got_short = lax.ppermute(own_short, "dom", short_way)
-    mine, yours, part = interior(interlayer, vectors, hoppings, potential, stacking, own_short)
+    mine, yours, part = interior(interlayer, vectors, hoppings, potential, stacking, own_long)
     records = (own_long, own_short, got_long, got_short, extra)
-    totals = totals_of(records, part, strips * ranks)
+    totals = totals_of(records, part, filling, strips * ranks)
     yours, ready = lax.optimization_barrier((yours, totals))
     other = lax.ppermute(yours, "vec", sibling)
-    slabs = edges(records, mine, other, totals)
+    slabs = edges(records, mine, other, totals) * (1.0 / (nvec * ranks))
     sums = lax.all_to_all(ready, ("dom", "vec"), 0, 0, tiled=True)
     sites = 4 * rows * width * strips
-    chip = density(filling, sums, slabs, nvec * ranks, sites)
+    chip = density(sums, slabs, nvec * ranks, sites)
     whole = chip + lax.ppermute(chip, "vec", across)
     return new_potential(whole, lax.ppermute(whole, "vec", sibling), width // LANES)
 

time: 70.6 us -> 68.4 us (0.969)
  other arithmetic: 0.05 us -> 1.52 us
  local copies, waits for them, and re-layouts: 1.39 us -> 0 us
  starting transfers between devices: 22.9 us -> 21.7 us
    ppermute x1, starting transfers between devices: 2.21 us -> 0.01 us  [per_device(): got_short = lax.ppermute(own_short, 'dom', short_way)]
    ppermute x1, starting transfers between devices: 8.12 us -> 9.87 us  [per_device(): got_long = lax.ppermute(own_long, 'dom', long_way)]
    mul x0 -> x1, other arithmetic: none -> 1.49 us  [per_device(): slabs = edges(records, mine, other, totals) * (1.0 / (nvec * ranks))]
    unnamed x2 -> x0, local copies, waits for them, and re-layouts: 1.39 us -> none
    pallas_call x1, Pallas kernels: 14.2 us -> 13.4 us  [interior(): pl.pallas_call(functools.partial(interior_kernel, rows, chunks, nvec, gro...]
  transfers between devices with their start and end apart: 6 -> 6, of which waited for: 3 -> 3; matrix products, arithmetic and copies ran while one was open for 0% -> 2% of each run, Pallas kernels for 30% -> 29%
where the time goes in v4:
time: 68.4 us; the launch traced here: 68.2 us
  Pallas kernels  29.1 us (43%)
  starting transfers between devices  21.7 us (32%)
  waiting for transfers between devices  15.2 us (22%)
  other arithmetic  1.52 us (2%)
  between operations  0.73 us (1%)
    pallas_call x1, Pallas kernels, interior(): pl.pallas_call(functools.partial(interior_kernel, rows, chunks, nvec, gro...  13.4 us
    ppermute x1, starting transfers between devices, per_device(): got_long = lax.ppermute(own_long, 'dom', long_way)  9.87 us
    ppermute x1, waiting for transfers between devices, per_device(): whole = chip + lax.ppermute(chip, 'vec', across)  8.99 us
    all_to_all x1, starting transfers between devices, per_device(): sums = lax.all_to_all(ready, ('dom', 'vec'), 0, 0, tiled=True)  8.02 us
    pallas_call x1, Pallas kernels, edges(): pl.pallas_call(functools.partial(edges_kernel, chunks, half), out_shape=j...  6.65 us
    all_to_all x1, waiting for transfers between devices, per_device(): sums = lax.all_to_all(ready, ('dom', 'vec'), 0, 0, tiled=True)  4.94 us
    pallas_call x1, Pallas kernels, pack(): pl.pallas_call(functools.partial(pack_kernel, rows, chunks), out_shape=[m...  4.11 us
    pallas_call x1, Pallas kernels, totals_of(): pl.pallas_call(functools.partial(totals_kernel, chunks, parts), out_shape...  3.23 us
  transfers between devices with their start and end apart: 6, of which 3 were waited for; matrix products, arithmetic and copies ran while one was open for 2% of the time, Pallas kernels for 29%

profile of v4, /device:TPU:1, one launch (start us, length us, event | category | flops | bytes accessed | tf_op | source)
XLA Modules:
  0.0 68.2 jit_solution(16359796399816959693)
XLA Ops:
  0.0 4.1 %pack.1 = (f32[8,136,128]{2,1,0:T(8,128)}, f32[8,136,128]{2,1,0:T(8,128)}, f32[2,8,56,128]{3,2,1,0:T(8,128)}) custom-call(f32[2,8]{1,0:T(2,128)} %table.3, f32[32,32,1024]{2,1,0:T(8,128)} %bitcast.7, f32[6,32,1024]{2,1,0:T(8,128)} %bitcast.8, f32[4,32,1024]{2,1,0:T(8,128)} %pot.3, s32[32,1024]{1,0:T(8,128)} %stk.3), custom_call_target="tpu_custom_call" | custom-call | flops 1000000 | bytes 4000000 | tf_op jit(solution)/shard_map/pack/pallas_call | solution.py:197
  4.1 9.9 %collective-permute-start = (f32[8,136,128]{2,1,0:T(8,128)}, f32[8,136,128]{2,1,0:T(8,128)}, u32[]{:S(2)}, u32[]{:S(2)}) collective-permute-start(f32[8,136,128]{2,1,0:T(8,128)} %get-tuple-element.13.after.own_long), channel_id=1, source_target_pairs={{0,252},{4,8},{8,4},{12,16},{16,12},{20,24},{24,20},{28,32},{32,28... | collective-permute-start | bytes 1671176 | tf_op jit(solution)/shard_map/ppermute | solution.py:909
  14.0 0.0 collective-permute-start.1
  14.6 13.4 %interior.1 = (f32[5,4,8,16,128]{4,3,2,1,0:T(8,128)}, f32[5,4,8,16,128]{4,3,2,1,0:T(8,128)}, f32[5,8,128]{2,1,0:T(8,128)}) custom-call(f32[2,8]{1,0:T(2,128)} %table.3, f32[4,8,32,1024]{3,2,1,0:T(8,128)} %vec.1, f32[2,3,32,1024]{3,2,1,0:T(8,128)} %hop.1, f32[4,32,1024]{2,1,0:T(8,128)} %pot.3, s32[32,1024]{1,0:T(8,128)} %stk.3, ...), custom_call_target="tpu_custom_call" | custom-call | flops 60000000 | bytes 9000000 | tf_op jit(solution)/shard_map/interior/pallas_call | solution.py:424
  28.0 0.0 collective-permute-done.got_long
  28.1 0.0 collective-permute-done.1.got_short
  28.1 3.2 %totals.1.after = f32[256,128]{1,0:T(8,128)} custom-call(f32[8,136,128]{2,1,0:T(8,128)} %get-tuple-element.13.after.own_long, f32[8,136,128]{2,1,0:T(8,128)} %get-tuple-element.15.own_short, f32[8,136,128]{2,1,0:T(8,128)} %collective-permute-done.got_long, f32[8,136,128]{2,1,0:T(8,128)} %collective-permute-done.1.got_short, ...), custom_call_target="tpu_custom_call" | custom-call | flops 8000000 | bytes 4000000 | tf_op jit(solution)/shard_map/totals/pallas_call | solution.py:610
  31.3 1.5 %collective-permute-start.2 = (f32[5,4,8,16,128]{4,3,2,1,0:T(8,128)}, f32[5,4,8,16,128]{4,3,2,1,0:T(8,128)}, u32[]{:S(2)}, u32[]{:S(2)}) collective-permute-start(f32[5,4,8,16,128]{4,3,2,1,0:T(8,128)} %get-tuple-element.20), channel_id=1, source_target_pairs={{0,1},{1,0},{2,3},{3,2},{4,5},{5,4},{6,7},{7,6},{8,9},{9,8},{10,11... | collective-permute-start | bytes 3932168 | tf_op jit(solution)/shard_map/ppermute | solution.py:915
  32.8 8.0 %all-to-all-start = ((f32[256,1,128]{2,1,0:T(1,128)}), f32[256,1,128]{2,1,0:T(1,128)S(1)}, u32[]{:S(2)}, u32[]{:S(2)}) async-start(f32[256,1,128]{2,1,0:T(1,128)} %bitcast.9), calls=%async_computation | async-start | bytes 262144 | tf_op jit(solution)/shard_map/all_to_all | solution.py:917
  40.9 0.0 collective-permute-done.2.other_in
  40.9 6.6 %edges.1 = f32[5,592,128]{2,1,0:T(8,128)} custom-call(f32[8,136,128]{2,1,0:T(8,128)} %get-tuple-element.13.after.own_long, f32[8,136,128]{2,1,0:T(8,128)} %get-tuple-element.15.own_short, f32[8,136,128]{2,1,0:T(8,128)} %collective-permute-done.got_long, f32[8,136,128]{2,1,0:T(8,128)} %collective-permute-done.1.got_short, ...), custom_call_target="tpu_custom_call" | custom-call | flops 20000000 | bytes 4000000 | tf_op jit(solution)/shard_map/edges/pallas_call | solution.py:727
  47.5 1.5 %broadcast_multiply_fusion.slabs = f32[5,592,128]{2,1,0:T(8,128)S(1)} fusion(f32[5,592,128]{2,1,0:T(8,128)} %edges.1), kind=kLoop, calls=%fused_computation | loop fusion | flops 378880 | bytes 3031040 | tf_op jit(solution)/shard_map/mul | solution.py:916
  49.0 4.9 %all-to-all-done = f32[256,1,128]{2,1,0:T(1,128)S(1)} async-done(((f32[256,1,128]{2,1,0:T(1,128)}), f32[256,1,128]{2,1,0:T(1,128)S(1)}, u32[]{:S(2)}, u32[]{:S(2)}) %all-to-all-start) | async-done | bytes 131104 | tf_op jit(solution)/shard_map/all_to_all | solution.py:917
  54.0 0.6 density.1
  54.5 1.0 %collective-permute-start.3 = (f32[592,128]{1,0:T(8,128)S(1)}, f32[592,128]{1,0:T(8,128)S(1)}, u32[]{:S(2)}, u32[]{:S(2)}) collective-permute-start(f32[592,128]{1,0:T(8,128)S(1)} %density.1), channel_id=1, source_target_pairs={{0,2},{1,3},{2,0},{3,1},{4,6},{5,7},{6,4},{7,5},{8,10},{9,11},{10,... | collective-permute-start | bytes 909320 | tf_op jit(solution)/shard_map/ppermute | solution.py:920
  55.5 9.0 %collective-permute-done.3 = f32[592,128]{1,0:T(8,128)S(1)} collective-permute-done((f32[592,128]{1,0:T(8,128)S(1)}, f32[592,128]{1,0:T(8,128)S(1)}, u32[]{:S(2)}, u32[]{:S(2)}) %collective-permute-start.3) | collective-permute-done | bytes 303136 | tf_op jit(solution)/shard_map/ppermute | solution.py:920
  64.5 1.3 %collective-permute-start.4 = (f32[592,128]{1,0:T(8,128)S(1)}, f32[592,128]{1,0:T(8,128)S(1)}, u32[]{:S(2)}, u32[]{:S(2)}) collective-permute-start(f32[592,128]{1,0:T(8,128)S(1)} %add.3.mine), channel_id=1, source_target_pairs={{0,1},{1,0},{2,3},{3,2},{4,5},{5,4},{6,7},{7,6},{8,9},{9,8},{10,11... | collective-permute-start | bytes 909320 | tf_op jit(solution)/shard_map/ppermute | solution.py:921
  65.8 1.2 %collective-permute-done.4.other = f32[592,128]{1,0:T(8,128)S(1)} collective-permute-done((f32[592,128]{1,0:T(8,128)S(1)}, f32[592,128]{1,0:T(8,128)S(1)}, u32[]{:S(2)}, u32[]{:S(2)}) %collective-permute-start.4) | collective-permute-done | bytes 303136 | tf_op jit(solution)/shard_map/ppermute | solution.py:921
  67.1 1.1 %new_potential.1 = f32[4,32,1024]{2,1,0:T(8,128)} custom-call(f32[592,128]{1,0:T(8,128)S(1)} %add.3.mine, f32[592,128]{1,0:T(8,128)S(1)} %collective-permute-done.4.other), custom_call_target="tpu_custom_call" | custom-call | flops 1000000 | bytes 2000000 | tf_op jit(solution)/shard_map/new_potential/pallas_call | solution.py:879
  (1 shorter events, 0.0 us)
Async XLA Ops:
  4.1 23.9 %collective-permute-start = (f32[8,136,128]{2,1,0:T(8,128)}, f32[8,136,128]{2,1,0:T(8,128)}, u32[]{:S(2)}, u32[]{:S(2)}) collective-permute-start(f32[8,136,128]{2,1,0:T(8,128)} %get-tuple-element.13.after.own_long), channel_id=1, source_target_pairs={{0,252},{4,8},{8,4},{12,16},{16,12},{20,24},{24,20},{28,32},{32,28... | collective-permute-start | bytes 1671176 | tf_op jit(solution)/shard_map/ppermute | solution.py:909
  14.0 14.1 %collective-permute-start.1 = (f32[8,136,128]{2,1,0:T(8,128)}, f32[8,136,128]{2,1,0:T(8,128)}, u32[]{:S(2)}, u32[]{:S(2)}) collective-permute-start(f32[8,136,128]{2,1,0:T(8,128)} %get-tuple-element.15.own_short), channel_id=1, source_target_pairs={{0,4},{4,0},{8,12},{12,8},{16,20},{20,16},{24,28},{28,24},{32,36},... | collective-permute-start | bytes 1671176 | tf_op jit(solution)/shard_map/ppermute | solution.py:910
  31.3 9.6 %collective-permute-start.2 = (f32[5,4,8,16,128]{4,3,2,1,0:T(8,128)}, f32[5,4,8,16,128]{4,3,2,1,0:T(8,128)}, u32[]{:S(2)}, u32[]{:S(2)}) collective-permute-start(f32[5,4,8,16,128]{4,3,2,1,0:T(8,128)} %get-tuple-element.20), channel_id=1, source_target_pairs={{0,1},{1,0},{2,3},{3,2},{4,5},{5,4},{6,7},{7,6},{8,9},{9,8},{10,11... | collective-permute-start | bytes 3932168 | tf_op jit(solution)/shard_map/ppermute | solution.py:915
  32.8 21.1 %all-to-all-start = ((f32[256,1,128]{2,1,0:T(1,128)}), f32[256,1,128]{2,1,0:T(1,128)S(1)}, u32[]{:S(2)}, u32[]{:S(2)}) async-start(f32[256,1,128]{2,1,0:T(1,128)} %bitcast.9), calls=%async_computation | async-start | bytes 262144 | tf_op jit(solution)/shard_map/all_to_all | solution.py:917
  54.5 10.0 %collective-permute-start.3 = (f32[592,128]{1,0:T(8,128)S(1)}, f32[592,128]{1,0:T(8,128)S(1)}, u32[]{:S(2)}, u32[]{:S(2)}) collective-permute-start(f32[592,128]{1,0:T(8,128)S(1)} %density.1), channel_id=1, source_target_pairs={{0,2},{1,3},{2,0},{3,1},{4,6},{5,7},{6,4},{7,5},{8,10},{9,11},{10,... | collective-permute-start | bytes 909320 | tf_op jit(solution)/shard_map/ppermute | solution.py:920
  64.5 2.5 %collective-permute-start.4 = (f32[592,128]{1,0:T(8,128)S(1)}, f32[592,128]{1,0:T(8,128)S(1)}, u32[]{:S(2)}, u32[]{:S(2)}) collective-permute-start(f32[592,128]{1,0:T(8,128)S(1)} %add.3.mine), channel_id=1, source_target_pairs={{0,1},{1,0},{2,3},{3,2},{4,5},{5,4},{6,7},{7,6},{8,9},{9,8},{10,11... | collective-permute-start | bytes 909320 | tf_op jit(solution)/shard_map/ppermute | solution.py:921

commit v5 on v4

--- a/solution.py
+++ b/solution.py
@@ -93,16 +93,17 @@
     n = 1
     for band in range(2):
         at = pl.ds(band * (rows - SUB), SUB)
+        for src, dst in (
+            (hop.at[:, at], h8.at[band]),
+            (pot.at[:, at], p8.at[band]),
+            (stk.at[at], s8.at[band]),
+        ):
+            copies.append(pltpu.make_async_copy(src, dst, sems.at[n]))
+            n += 1
         for c in range(chunks):
-            lanes = pl.ds(c * LANES, LANES)
-            for src, dst in (
-                (hop.at[:, at, lanes], h8.at[band, c]),
-                (pot.at[:, at, lanes], p8.at[band, c]),
-                (stk.at[at, lanes], s8.at[band, c]),
-                (vec.at[:, at, lanes], v8.at[band, c]),
-            ):
-                copies.append(pltpu.make_async_copy(src, dst, sems.at[n]))
-                n += 1
+            src = vec.at[:, at, pl.ds(c * LANES, LANES)]
+            copies.append(pltpu.make_async_copy(src, v8.at[band, c], sems.at[n]))
+            n += 1
     for copy in copies:
         copy.start()
     nf = vec.shape[0]
@@ -110,37 +111,31 @@
     odd = place()[0]
     outs = []
     copies[0].wait()
-    waited = set()
-
-    def wait_tile(band, c):
-        if (band, c) not in waited:
-            waited.add((band, c))
-            for copy in copies[1 + 4 * (chunks * band + c) :][:4]:
-                copy.wait()
 
     for band in range(2):
+        for copy in copies[1 + band * (3 + chunks) :][: 3 + chunks]:
+            copy.wait()
         for c in range(chunks):
-            wait_tile(band, c)
+            lanes = pl.ds(c * LANES, LANES)
             first = 0 if band == 0 else SUB - 4
             for r in range(4):
                 for s in range(nf // SUB):
                     rec[band, c, pl.ds(r * REC + s * SUB, SUB), :] = flat[
                         band, c, pl.ds(s * SUB * SUB + first + r, SUB, stride=SUB), :
                     ]
-            after = (c + 1) % chunks
-            wait_tile(band, after)
+            after = pl.ds((c + 1) % chunks * LANES, LANES)
             coef = []
             for layer in range(2):
                 for k in range(3):
-                    coef.append(h8[band, c, 3 * layer + k] * -0.25)
+                    coef.append(h8[band, 3 * layer + k, :, lanes] * -0.25)
                     if k == 1:
-                        here = h8[band, c, 3 * layer + 1]
-                        there = h8[band, after, 3 * layer + 1]
+                        here = h8[band, 3 * layer + 1, :, lanes]
+                        there = h8[band, 3 * layer + 1, :, after]
                         shifted = from_right(roll_left(here), roll_left(there)) * -0.25
                 coef.append(shifted)
             for s in range(4):
-                coef.append(p8[band, c, s] * 0.25)
-            classes = s8[band, c]
+                coef.append(p8[band, s, :, lanes] * 0.25)
+            classes = s8[band, :, lanes]
             for w in range(2):
                 table = [inter[w, k] * 0.25 for k in range(inter.shape[1])]
                 coef.append(pick(classes, table))
@@ -156,34 +151,34 @@
                 ((2, 14, 3), (2, 15, 7), (3, 14, 9), (3, 15, 11)),
             )[band]:
                 rec[band, c, pl.ds(r * REC + COEF + slot, 1), :] = coef[k][third : third + 1]
-            third_at = (2, 1)[band] * REC
-            parts = (
-                (pl.ds((0, 2)[band] * REC, NEAR), pl.ds(0, NEAR)),
-                (pl.ds(third_at, FAR), pl.ds(NEAR, FAR)),
+        third_at = (2, 1)[band] * REC
+        parts = (
+            (pl.ds((0, 2)[band] * REC, NEAR), pl.ds(0, NEAR)),
+            (pl.ds(third_at, FAR), pl.ds(NEAR, FAR)),
+        )
+        for src_at, dst_at in (
+            (pl.ds((1 - band) * 3 * REC, REC), pl.ds(0, REC)),
+            (pl.ds(third_at + FAR, REC - FAR), pl.ds(REC, REC - FAR)),
+        ):
+            away = pltpu.make_async_copy(
+                rec.at[band, :, src_at], extra.at[band, :, dst_at], sems.at[n]
             )
-            for src_at, dst_at in (
-                (pl.ds((1 - band) * 3 * REC, REC), pl.ds(0, REC)),
-                (pl.ds(third_at + FAR, REC - FAR), pl.ds(REC, REC - FAR)),
-            ):
-                away = pltpu.make_async_copy(
-                    rec.at[band, c, src_at], extra.at[band, c, dst_at], sems.at[n]
-                )
-                away.start()
-                outs.append(away)
-                n += 1
-            for src_at, dst_at in parts:
-                src, sem = rec.at[band, c, src_at], sems.at[n]
-
-                @pl.when(odd == band)
-                def _():
-                    pltpu.make_async_copy(src, long_out.at[c, dst_at], sem).start()
-
-                @pl.when(odd != band)
-                def _():
-                    pltpu.make_async_copy(src, short_out.at[c, dst_at], sem).start()
-
-                outs.append(pltpu.make_async_copy(src, long_out.at[c, dst_at], sem))
-                n += 1
+            away.start()
+            outs.append(away)
+            n += 1
+        for src_at, dst_at in parts:
+            src, sem = rec.at[band, :, src_at], sems.at[n]
+
+            @pl.when(odd == band)
+            def _():
+                pltpu.make_async_copy(src, long_out.at[:, dst_at], sem).start()
+
+            @pl.when(odd != band)
+            def _():
+                pltpu.make_async_copy(src, short_out.at[:, dst_at], sem).start()
+
+            outs.append(pltpu.make_async_copy(src, long_out.at[:, dst_at], sem))
+            n += 1
     for copy in outs:
         copy.wait()
 
@@ -193,7 +188,7 @@
     chunks = width // LANES
     any_ = pl.BlockSpec(memory_space=pl.ANY)
     message = jax.ShapeDtypeStruct((chunks, MESSAGE, LANES), F32)
-    n_in = 2 * chunks * 4 + 1
+    n_in = 2 * (chunks + 3) + 1
     return pl.pallas_call(
         functools.partial(pack_kernel, rows, chunks),
         out_shape=[message, message, jax.ShapeDtypeStruct((2, chunks, EXTRA, LANES), F32)],
@@ -202,11 +197,11 @@
         scratch_shapes=[
             pltpu.SMEM(inter.shape, F32),
             pltpu.VMEM((2, chunks, fields, SUB, LANES), F32),
-            pltpu.VMEM((2, chunks, 6, SUB, LANES), F32),
-            pltpu.VMEM((2, chunks, 4, SUB, LANES), F32),
-            pltpu.VMEM((2, chunks, SUB, LANES), jnp.int32),
+            pltpu.VMEM((2, 6, SUB, width), F32),
+            pltpu.VMEM((2, 4, SUB, width), F32),
+            pltpu.VMEM((2, SUB, width), jnp.int32),
             pltpu.VMEM((2, chunks, 4 * REC, LANES), F32),
-            pltpu.SemaphoreType.DMA((n_in + 8 * chunks,)),
+            pltpu.SemaphoreType.DMA((n_in + 8,)),
         ],
         compiler_params=pltpu.CompilerParams(vmem_limit_bytes=VMEM_WIDE),
         cost_estimate=pl.CostEstimate(flops=1_000_000, bytes_accessed=4_000_000, transcendentals=0),
@@ -218,20 +213,15 @@
 
 
 def interior_kernel(rows, chunks, nvec, group, table, vec, hop, pot, stk, after, keep, send, tot,
-                    inter, x, t1, t2, hp, pt, st, ww, mom, dots, ends, sems):
+                    inter, hop_raw, pot_raw, x, t1, t2, hp, pt, st, ww, mom, dots, ends,
+                    sems):
     del after
     halves = nvec // group
     copies = [pltpu.make_async_copy(table, inter, sems.at[0])]
     n = 1
-    for c in range(chunks):
-        lanes = pl.ds(c * LANES, LANES)
-        for src, dst in (
-            (hop.at[:, :, :, lanes], hp.at[:, 0:3, c, pl.ds(0, rows)]),
-            (pot.at[:, :, lanes], pt.at[:, c]),
-            (stk.at[:, lanes], st.at[c]),
-        ):
-            copies.append(pltpu.make_async_copy(src, dst, sems.at[n]))
-            n += 1
+    for src, dst in ((hop, hop_raw), (pot, pot_raw), (stk, st)):
+        copies.append(pltpu.make_async_copy(src, dst, sems.at[n]))
+        n += 1
     late = []
     for q in range(halves):
         part = []
@@ -255,21 +245,20 @@
 
     def prepare(g, carry):
         at = pl.ds(pl.multiple_of(g * SUB, SUB), SUB)
+        lanes = [pl.ds(c * LANES, LANES) for c in range(chunks)]
         for layer in range(2):
-            rolled = {}
-            for c in range(chunks):
-                rolled[c] = roll_left(hp[layer, 1, c, at, :])
+            rolled = [roll_left(hop_raw[layer, 1, at, lanes[c]]) for c in range(chunks)]
             for c in range(chunks):
                 hp[layer, 3, c, at, :] = (
                     from_right(rolled[c], rolled[(c + 1) % chunks]) * -0.25
                 )
             for k in range(3):
                 for c in range(chunks):
-                    hp[layer, k, c, at, :] = hp[layer, k, c, at, :] * -0.25
+                    hp[layer, k, c, at, :] = hop_raw[layer, k, at, lanes[c]] * -0.25
         for c in range(chunks):
             for s in range(4):
-                pt[s, c, at, :] = pt[s, c, at, :] * 0.25
-            classes = st[c, at, :]
+                pt[s, c, at, :] = pot_raw[s, at, lanes[c]] * 0.25
+            classes = st[at, lanes[c]]
             for w in range(2):
                 table = [inter[w, k] * 0.25 for k in range(inter.shape[1])]
                 ww[w, c, at, :] = pick(classes, table)
@@ -420,7 +409,7 @@
     group = 2
     any_ = pl.BlockSpec(memory_space=pl.ANY)
     half = jax.ShapeDtypeStruct((CHEB + 1, 4, chunks, rows // 2, LANES), F32)
-    n = 2 + chunks * (3 + nvec // group) + 2 * (CHEB + 1)
+    n = 5 + chunks * (nvec // group) + 2 * (CHEB + 1)
     return pl.pallas_call(
         functools.partial(interior_kernel, rows, chunks, nvec, group),
         out_shape=[half, half, jax.ShapeDtypeStruct((CHEB + 1, SUB, LANES), F32)],
@@ -428,12 +417,14 @@
         out_specs=[any_, any_, any_],
         scratch_shapes=[
             pltpu.SMEM(inter.shape, F32),
+            pltpu.VMEM(hop.shape, F32),
+            pltpu.VMEM(pot.shape, F32),
             pltpu.VMEM((4, nvec, chunks, rows + 2 * PAD, LANES), F32),
             pltpu.VMEM((4, group, chunks, rows + 2 * PAD, LANES), F32),
             pltpu.VMEM((4, group, chunks, rows + 2 * PAD, LANES), F32),
             pltpu.VMEM((2, 4, chunks, rows + SUB, LANES), F32),
             pltpu.VMEM((4, chunks, rows, LANES), F32),
-            pltpu.VMEM((chunks, rows, LANES), jnp.int32),
+            pltpu.VMEM((rows, width), jnp.int32),
             pltpu.VMEM((2, chunks, rows, LANES), F32),
             pltpu.VMEM((CHEB + 1, 4, chunks, rows, LANES), F32),
             pltpu.VMEM((2, SUB, LANES), F32),

time: 68.4 us -> 67.5 us (0.987)
  Pallas kernels: 29.1 us -> 27.9 us
    pallas_call x1, Pallas kernels: 4.11 us -> 3.23 us  [pack(): pl.pallas_call(functools.partial(pack_kernel, rows, chunks), out_shape=[m...]
where the time goes in v5:
time: 67.5 us; the launch traced here: 67.3 us
  Pallas kernels  27.9 us (41%)
  starting transfers between devices  22 us (33%)
  waiting for transfers between devices  15.2 us (23%)
  other arithmetic  1.52 us (2%)
  between operations  0.73 us (1%)
    pallas_call x1, Pallas kernels, interior(): pl.pallas_call(functools.partial(interior_kernel, rows, chunks, nvec, gro...  13.1 us
    ppermute x1, starting transfers between devices, per_device(): got_long = lax.ppermute(own_long, 'dom', long_way)  9.85 us
    ppermute x1, waiting for transfers between devices, per_device(): whole = chip + lax.ppermute(chip, 'vec', across)  8.99 us
    all_to_all x1, starting transfers between devices, per_device(): sums = lax.all_to_all(ready, ('dom', 'vec'), 0, 0, tiled=True)  8.02 us
    pallas_call x1, Pallas kernels, edges(): pl.pallas_call(functools.partial(edges_kernel, chunks, half), out_shape=j...  6.65 us
    all_to_all x1, waiting for transfers between devices, per_device(): sums = lax.all_to_all(ready, ('dom', 'vec'), 0, 0, tiled=True)  4.94 us
    pallas_call x1, Pallas kernels, totals_of(): pl.pallas_call(functools.partial(totals_kernel, chunks, parts), out_shape...  3.23 us
    pallas_call x1, Pallas kernels, pack(): pl.pallas_call(functools.partial(pack_kernel, rows, chunks), out_shape=[m...  3.23 us
  transfers between devices with their start and end apart: 6, of which 3 were waited for; matrix products, arithmetic and copies ran while one was open for 2% of the time, Pallas kernels for 29%

profile of v5, /device:TPU:1, one launch (start us, length us, event | category | flops | bytes accessed | tf_op | source)
XLA Modules:
  0.0 67.3 jit_solution(10232675646717330906)
XLA Ops:
  0.0 3.2 %pack.1 = (f32[8,136,128]{2,1,0:T(8,128)}, f32[8,136,128]{2,1,0:T(8,128)}, f32[2,8,56,128]{3,2,1,0:T(8,128)}) custom-call(f32[2,8]{1,0:T(2,128)} %table.3, f32[32,32,1024]{2,1,0:T(8,128)} %bitcast.7, f32[6,32,1024]{2,1,0:T(8,128)} %bitcast.8, f32[4,32,1024]{2,1,0:T(8,128)} %pot.3, s32[32,1024]{1,0:T(8,128)} %stk.3), custom_call_target="tpu_custom_call" | custom-call | flops 1000000 | bytes 4000000 | tf_op jit(solution)/shard_map/pack/pallas_call | solution.py:192
  3.2 9.8 %collective-permute-start = (f32[8,136,128]{2,1,0:T(8,128)}, f32[8,136,128]{2,1,0:T(8,128)}, u32[]{:S(2)}, u32[]{:S(2)}) collective-permute-start(f32[8,136,128]{2,1,0:T(8,128)} %get-tuple-element.13.after.own_long), channel_id=1, source_target_pairs={{0,252},{4,8},{8,4},{12,16},{16,12},{20,24},{24,20},{28,32},{32,28... | collective-permute-start | bytes 1671176 | tf_op jit(solution)/shard_map/ppermute | solution.py:900
  13.1 0.0 collective-permute-start.1
  13.7 13.1 %interior.1 = (f32[5,4,8,16,128]{4,3,2,1,0:T(8,128)}, f32[5,4,8,16,128]{4,3,2,1,0:T(8,128)}, f32[5,8,128]{2,1,0:T(8,128)}) custom-call(f32[2,8]{1,0:T(2,128)} %table.3, f32[4,8,32,1024]{3,2,1,0:T(8,128)} %vec.1, f32[2,3,32,1024]{3,2,1,0:T(8,128)} %hop.1, f32[4,32,1024]{2,1,0:T(8,128)} %pot.3, s32[32,1024]{1,0:T(8,128)} %stk.3, ...), custom_call_target="tpu_custom_call" | custom-call | flops 60000000 | bytes 9000000 | tf_op jit(solution)/shard_map/interior/pallas_call | solution.py:413
  26.9 0.0 collective-permute-done.got_long
  26.9 0.0 collective-permute-done.1.got_short
  26.9 3.2 %totals.1.after = f32[256,128]{1,0:T(8,128)} custom-call(f32[8,136,128]{2,1,0:T(8,128)} %get-tuple-element.13.after.own_long, f32[8,136,128]{2,1,0:T(8,128)} %get-tuple-element.15.own_short, f32[8,136,128]{2,1,0:T(8,128)} %collective-permute-done.got_long, f32[8,136,128]{2,1,0:T(8,128)} %collective-permute-done.1.got_short, ...), custom_call_target="tpu_custom_call" | custom-call | flops 8000000 | bytes 4000000 | tf_op jit(solution)/shard_map/totals/pallas_call | solution.py:601
  30.1 1.8 %collective-permute-start.2 = (f32[5,4,8,16,128]{4,3,2,1,0:T(8,128)}, f32[5,4,8,16,128]{4,3,2,1,0:T(8,128)}, u32[]{:S(2)}, u32[]{:S(2)}) collective-permute-start(f32[5,4,8,16,128]{4,3,2,1,0:T(8,128)} %get-tuple-element.20), channel_id=1, source_target_pairs={{0,1},{1,0},{2,3},{3,2},{4,5},{5,4},{6,7},{7,6},{8,9},{9,8},{10,11... | collective-permute-start | bytes 3932168 | tf_op jit(solution)/shard_map/ppermute | solution.py:906
  31.9 8.0 %all-to-all-start = ((f32[256,1,128]{2,1,0:T(1,128)}), f32[256,1,128]{2,1,0:T(1,128)S(1)}, u32[]{:S(2)}, u32[]{:S(2)}) async-start(f32[256,1,128]{2,1,0:T(1,128)} %bitcast.9), calls=%async_computation | async-start | bytes 262144 | tf_op jit(solution)/shard_map/all_to_all | solution.py:908
  40.0 0.0 collective-permute-done.2.other_in
  40.0 6.6 %edges.1 = f32[5,592,128]{2,1,0:T(8,128)} custom-call(f32[8,136,128]{2,1,0:T(8,128)} %get-tuple-element.13.after.own_long, f32[8,136,128]{2,1,0:T(8,128)} %get-tuple-element.15.own_short, f32[8,136,128]{2,1,0:T(8,128)} %collective-permute-done.got_long, f32[8,136,128]{2,1,0:T(8,128)} %collective-permute-done.1.got_short, ...), custom_call_target="tpu_custom_call" | custom-call | flops 20000000 | bytes 4000000 | tf_op jit(solution)/shard_map/edges/pallas_call | solution.py:718
  46.6 1.5 %broadcast_multiply_fusion.slabs = f32[5,592,128]{2,1,0:T(8,128)S(1)} fusion(f32[5,592,128]{2,1,0:T(8,128)} %edges.1), kind=kLoop, calls=%fused_computation | loop fusion | flops 378880 | bytes 3031040 | tf_op jit(solution)/shard_map/mul | solution.py:907
  48.1 4.9 %all-to-all-done = f32[256,1,128]{2,1,0:T(1,128)S(1)} async-done(((f32[256,1,128]{2,1,0:T(1,128)}), f32[256,1,128]{2,1,0:T(1,128)S(1)}, u32[]{:S(2)}, u32[]{:S(2)}) %all-to-all-start) | async-done | bytes 131104 | tf_op jit(solution)/shard_map/all_to_all | solution.py:908
  53.1 0.6 density.1
  53.6 1.0 %collective-permute-start.3 = (f32[592,128]{1,0:T(8,128)S(1)}, f32[592,128]{1,0:T(8,128)S(1)}, u32[]{:S(2)}, u32[]{:S(2)}) collective-permute-start(f32[592,128]{1,0:T(8,128)S(1)} %density.1), channel_id=1, source_target_pairs={{0,2},{1,3},{2,0},{3,1},{4,6},{5,7},{6,4},{7,5},{8,10},{9,11},{10,... | collective-permute-start | bytes 909320 | tf_op jit(solution)/shard_map/ppermute | solution.py:911
  54.6 9.0 %collective-permute-done.3 = f32[592,128]{1,0:T(8,128)S(1)} collective-permute-done((f32[592,128]{1,0:T(8,128)S(1)}, f32[592,128]{1,0:T(8,128)S(1)}, u32[]{:S(2)}, u32[]{:S(2)}) %collective-permute-start.3) | collective-permute-done | bytes 303136 | tf_op jit(solution)/shard_map/ppermute | solution.py:911
  63.6 1.3 %collective-permute-start.4 = (f32[592,128]{1,0:T(8,128)S(1)}, f32[592,128]{1,0:T(8,128)S(1)}, u32[]{:S(2)}, u32[]{:S(2)}) collective-permute-start(f32[592,128]{1,0:T(8,128)S(1)} %add.3.mine), channel_id=1, source_target_pairs={{0,1},{1,0},{2,3},{3,2},{4,5},{5,4},{6,7},{7,6},{8,9},{9,8},{10,11... | collective-permute-start | bytes 909320 | tf_op jit(solution)/shard_map/ppermute | solution.py:912
  64.9 1.2 %collective-permute-done.4.other = f32[592,128]{1,0:T(8,128)S(1)} collective-permute-done((f32[592,128]{1,0:T(8,128)S(1)}, f32[592,128]{1,0:T(8,128)S(1)}, u32[]{:S(2)}, u32[]{:S(2)}) %collective-permute-start.4) | collective-permute-done | bytes 303136 | tf_op jit(solution)/shard_map/ppermute | solution.py:912
  66.2 1.1 %new_potential.1 = f32[4,32,1024]{2,1,0:T(8,128)} custom-call(f32[592,128]{1,0:T(8,128)S(1)} %add.3.mine, f32[592,128]{1,0:T(8,128)S(1)} %collective-permute-done.4.other), custom_call_target="tpu_custom_call" | custom-call | flops 1000000 | bytes 2000000 | tf_op jit(solution)/shard_map/new_potential/pallas_call | solution.py:870
  (1 shorter events, 0.0 us)
Async XLA Ops:
  3.2 23.6 %collective-permute-start = (f32[8,136,128]{2,1,0:T(8,128)}, f32[8,136,128]{2,1,0:T(8,128)}, u32[]{:S(2)}, u32[]{:S(2)}) collective-permute-start(f32[8,136,128]{2,1,0:T(8,128)} %get-tuple-element.13.after.own_long), channel_id=1, source_target_pairs={{0,252},{4,8},{8,4},{12,16},{16,12},{20,24},{24,20},{28,32},{32,28... | collective-permute-start | bytes 1671176 | tf_op jit(solution)/shard_map/ppermute | solution.py:900
  13.1 13.8 %collective-permute-start.1 = (f32[8,136,128]{2,1,0:T(8,128)}, f32[8,136,128]{2,1,0:T(8,128)}, u32[]{:S(2)}, u32[]{:S(2)}) collective-permute-start(f32[8,136,128]{2,1,0:T(8,128)} %get-tuple-element.15.own_short), channel_id=1, source_target_pairs={{0,4},{4,0},{8,12},{12,8},{16,20},{20,16},{24,28},{28,24},{32,36},... | collective-permute-start | bytes 1671176 | tf_op jit(solution)/shard_map/ppermute | solution.py:901
  30.1 9.8 %collective-permute-start.2 = (f32[5,4,8,16,128]{4,3,2,1,0:T(8,128)}, f32[5,4,8,16,128]{4,3,2,1,0:T(8,128)}, u32[]{:S(2)}, u32[]{:S(2)}) collective-permute-start(f32[5,4,8,16,128]{4,3,2,1,0:T(8,128)} %get-tuple-element.20), channel_id=1, source_target_pairs={{0,1},{1,0},{2,3},{3,2},{4,5},{5,4},{6,7},{7,6},{8,9},{9,8},{10,11... | collective-permute-start | bytes 3932168 | tf_op jit(solution)/shard_map/ppermute | solution.py:906
  31.9 21.1 %all-to-all-start = ((f32[256,1,128]{2,1,0:T(1,128)}), f32[256,1,128]{2,1,0:T(1,128)S(1)}, u32[]{:S(2)}, u32[]{:S(2)}) async-start(f32[256,1,128]{2,1,0:T(1,128)} %bitcast.9), calls=%async_computation | async-start | bytes 262144 | tf_op jit(solution)/shard_map/all_to_all | solution.py:908
  53.6 10.0 %collective-permute-start.3 = (f32[592,128]{1,0:T(8,128)S(1)}, f32[592,128]{1,0:T(8,128)S(1)}, u32[]{:S(2)}, u32[]{:S(2)}) collective-permute-start(f32[592,128]{1,0:T(8,128)S(1)} %density.1), channel_id=1, source_target_pairs={{0,2},{1,3},{2,0},{3,1},{4,6},{5,7},{6,4},{7,5},{8,10},{9,11},{10,... | collective-permute-start | bytes 909320 | tf_op jit(solution)/shard_map/ppermute | solution.py:911
  63.6 2.5 %collective-permute-start.4 = (f32[592,128]{1,0:T(8,128)S(1)}, f32[592,128]{1,0:T(8,128)S(1)}, u32[]{:S(2)}, u32[]{:S(2)}) collective-permute-start(f32[592,128]{1,0:T(8,128)S(1)} %add.3.mine), channel_id=1, source_target_pairs={{0,1},{1,0},{2,3},{3,2},{4,5},{5,4},{6,7},{7,6},{8,9},{9,8},{10,11... | collective-permute-start | bytes 909320 | tf_op jit(solution)/shard_map/ppermute | solution.py:912

commit v6 on v5

--- a/solution.py
+++ b/solution.py
@@ -63,23 +63,28 @@
     return values[0]
 
 
-def hop_apply(a, b, a_right, b_left, a_down, b_up, coef, t2_down):
+def hop_apply(a, b, a_right, b_left, a_down, b_up, coef, t2_down, sites="AB"):
     pot = coef[8:12]
     aa, ab = coef[12:14]
     out = []
     for layer in range(2):
         t0, t1, t2, t1r = coef[4 * layer : 4 * layer + 4]
-        h_a = t0 * b[layer] + t1 * b_left[layer] + t2 * b_up[layer] + pot[2 * layer] * a[layer]
-        h_b = (
-            t0 * a[layer]
-            + t1r * a_right[layer]
-            + t2_down[layer] * a_down[layer]
-            + pot[2 * layer + 1] * b[layer]
-        )
+        h_a = h_b = None
+        if "A" in sites:
+            h_a = t0 * b[layer] + t1 * b_left[layer] + t2 * b_up[layer] + pot[2 * layer] * a[layer]
+        if "B" in sites:
+            h_b = (
+                t0 * a[layer]
+                + t1r * a_right[layer]
+                + t2_down[layer] * a_down[layer]
+                + pot[2 * layer + 1] * b[layer]
+            )
         out.append([h_a, h_b])
-    out[0][0] = out[0][0] + aa * a[1] + ab * b[1]
-    out[1][0] = out[1][0] + aa * a[0]
-    out[1][1] = out[1][1] + ab * a[0]
+    if "A" in sites:
+        out[0][0] = out[0][0] + aa * a[1] + ab * b[1]
+        out[1][0] = out[1][0] + aa * a[0]
+    if "B" in sites:
+        out[1][1] = out[1][1] + ab * a[0]
     return [out[0][0], out[0][1], out[1][0], out[1][1]]
 
 
@@ -156,6 +161,19 @@
             (pl.ds((0, 2)[band] * REC, NEAR), pl.ds(0, NEAR)),
             (pl.ds(third_at, FAR), pl.ds(NEAR, FAR)),
         )
+        for src_at, dst_at in parts:
+            src, sem = rec.at[band, :, src_at], sems.at[n]
+
+            @pl.when(odd == band)
+            def _():
+                pltpu.make_async_copy(src, long_out.at[:, dst_at], sem).start()
+
+            @pl.when(odd != band)
+            def _():
+                pltpu.make_async_copy(src, short_out.at[:, dst_at], sem).start()
+
+            outs.append(pltpu.make_async_copy(src, long_out.at[:, dst_at], sem))
+            n += 1
         for src_at, dst_at in (
             (pl.ds((1 - band) * 3 * REC, REC), pl.ds(0, REC)),
             (pl.ds(third_at + FAR, REC - FAR), pl.ds(REC, REC - FAR)),
@@ -165,19 +183,6 @@
             )
             away.start()
             outs.append(away)
-            n += 1
-        for src_at, dst_at in parts:
-            src, sem = rec.at[band, :, src_at], sems.at[n]
-
-            @pl.when(odd == band)
-            def _():
-                pltpu.make_async_copy(src, long_out.at[:, dst_at], sem).start()
-
-            @pl.when(odd != band)
-            def _():
-                pltpu.make_async_copy(src, short_out.at[:, dst_at], sem).start()
-
-            outs.append(pltpu.make_async_copy(src, long_out.at[:, dst_at], sem))
             n += 1
     for copy in outs:
         copy.wait()
@@ -508,7 +513,7 @@
     return ref[band, c, pl.ds(pl.multiple_of(start, SUB), SUB), :]
 
 
-def window_step(chunks, order, w, source, before, band, i, emit):
+def window_step(chunks, order, w, source, before, band, i, emit, sites="AB"):
     from_w = order == 1
 
     def here(site, c, shift=0):
@@ -532,8 +537,10 @@
         b_up = [here(2 * l + 1, c, -1) for l in range(2)]
         a_right = [from_right(a_here[l], a_next[l]) for l in range(2)]
         b_left = [from_left(b_here[l], b_prev[l]) for l in range(2)]
-        new = hop_apply(a, b, a_right, b_left, a_down, b_up, coef, t2_down)
+        new = hop_apply(a, b, a_right, b_left, a_down, b_up, coef, t2_down, sites)
         for s in range(4):
+            if new[s] is None:
+                continue
             if order == 1:
                 new[s] = new[s] * 0.5
             else:
@@ -547,7 +554,8 @@
     def emit(c, values):
         for s in range(4):
             at = pl.multiple_of((i + 1) * 32 + s * SUB, SUB)
-            target[band, c, pl.ds(at, SUB), :] = values[s]
+            if values[s] is not None:
+                target[band, c, pl.ds(at, SUB), :] = values[s]
 
     return emit
 
@@ -645,17 +653,22 @@
             4: (t1, t2, None),
         }[order]
 
-        def body(j, carry):
-            i = first + j
+        def step(i, sites):
             for band in range(2):
-                if order < 4:
+                if order < CHEB:
                     emit = store_row(target, band, i)
                 else:
-                    emit = lambda c, values, band=band: moments(band, i, c, 4, values)
-                window_step(chunks, order, w, source, before, band, i, emit)
+                    emit = lambda c, values, band=band: moments(band, i, c, CHEB, values)
+                window_step(chunks, order, w, source, before, band, i, emit, sites)
+
+        def body(j, carry):
+            step(first + j, "AB")
             return carry
 
-        lax.fori_loop(0, last - first + 1, body, 0, unroll=1 if order == 4 else 2)
+        if order in (1, 3):
+            step(first - 1, "B")
+            step(last + 1, "A")
+        lax.fori_loop(0, last - first + 1, body, 0, unroll=1 if order == CHEB else 2)
 
     def collect(order, ref):
         def body(j, carry):
@@ -669,11 +682,11 @@
         lax.fori_loop(0, 3, body, 0)
 
     collect(0, w)
-    sweep(1, 0, 6)
+    sweep(1, 1, 5)
     collect(1, t1)
     sweep(2, 1, 5)
     collect(2, t2)
-    sweep(3, 1, 5)
+    sweep(3, 2, 4)
     collect(3, t1)
     sweep(4, 2, 4)
     for copy in inner:

time: 67.5 us -> 67.5 us (level)
  no operation moved by 1% of the time
where the time goes in v6:
time: 67.5 us; the launch traced here: 67.3 us
  Pallas kernels  27.5 us (41%)
  starting transfers between devices  22 us (33%)
  waiting for transfers between devices  15.5 us (23%)
  other arithmetic  1.52 us (2%)
  between operations  0.73 us (1%)
    pallas_call x1, Pallas kernels, interior(): pl.pallas_call(functools.partial(interior_kernel, rows, chunks, nvec, gro...  13.1 us
    ppermute x1, starting transfers between devices, per_device(): got_long = lax.ppermute(own_long, 'dom', long_way)  9.87 us
    ppermute x1, waiting for transfers between devices, per_device(): whole = chip + lax.ppermute(chip, 'vec', across)  8.99 us
    all_to_all x1, starting transfers between devices, per_device(): sums = lax.all_to_all(ready, ('dom', 'vec'), 0, 0, tiled=True)  8.02 us
    pallas_call x1, Pallas kernels, edges(): pl.pallas_call(functools.partial(edges_kernel, chunks, half), out_shape=j...  6.29 us
    all_to_all x1, waiting for transfers between devices, per_device(): sums = lax.all_to_all(ready, ('dom', 'vec'), 0, 0, tiled=True)  5.29 us
    pallas_call x1, Pallas kernels, totals_of(): pl.pallas_call(functools.partial(totals_kernel, chunks, parts), out_shape...  3.23 us
    pallas_call x1, Pallas kernels, pack(): pl.pallas_call(functools.partial(pack_kernel, rows, chunks), out_shape=[m...  3.19 us
  transfers between devices with their start and end apart: 6, of which 3 were waited for; matrix products, arithmetic and copies ran while one was open for 2% of the time, Pallas kernels for 29%

profile of v6, /device:TPU:1, one launch (start us, length us, event | category | flops | bytes accessed | tf_op | source)
XLA Modules:
  0.0 67.3 jit_solution(9239467693277122520)
XLA Ops:
  0.0 3.2 %pack.1 = (f32[8,136,128]{2,1,0:T(8,128)}, f32[8,136,128]{2,1,0:T(8,128)}, f32[2,8,56,128]{3,2,1,0:T(8,128)}) custom-call(f32[2,8]{1,0:T(2,128)} %table.3, f32[32,32,1024]{2,1,0:T(8,128)} %bitcast.7, f32[6,32,1024]{2,1,0:T(8,128)} %bitcast.8, f32[4,32,1024]{2,1,0:T(8,128)} %pot.3, s32[32,1024]{1,0:T(8,128)} %stk.3), custom_call_target="tpu_custom_call" | custom-call | flops 1000000 | bytes 4000000 | tf_op jit(solution)/shard_map/pack/pallas_call | solution.py:197
  3.2 9.9 %collective-permute-start = (f32[8,136,128]{2,1,0:T(8,128)}, f32[8,136,128]{2,1,0:T(8,128)}, u32[]{:S(2)}, u32[]{:S(2)}) collective-permute-start(f32[8,136,128]{2,1,0:T(8,128)} %get-tuple-element.13.after.own_long), channel_id=1, source_target_pairs={{0,252},{4,8},{8,4},{12,16},{16,12},{20,24},{24,20},{28,32},{32,28... | collective-permute-start | bytes 1671176 | tf_op jit(solution)/shard_map/ppermute | solution.py:913
  13.1 0.0 collective-permute-start.1
  13.7 13.1 %interior.1 = (f32[5,4,8,16,128]{4,3,2,1,0:T(8,128)}, f32[5,4,8,16,128]{4,3,2,1,0:T(8,128)}, f32[5,8,128]{2,1,0:T(8,128)}) custom-call(f32[2,8]{1,0:T(2,128)} %table.3, f32[4,8,32,1024]{3,2,1,0:T(8,128)} %vec.1, f32[2,3,32,1024]{3,2,1,0:T(8,128)} %hop.1, f32[4,32,1024]{2,1,0:T(8,128)} %pot.3, s32[32,1024]{1,0:T(8,128)} %stk.3, ...), custom_call_target="tpu_custom_call" | custom-call | flops 60000000 | bytes 9000000 | tf_op jit(solution)/shard_map/interior/pallas_call | solution.py:418
  26.9 0.0 collective-permute-done.got_long
  26.9 0.0 collective-permute-done.1.got_short
  26.9 3.2 %totals.1.after = f32[256,128]{1,0:T(8,128)} custom-call(f32[8,136,128]{2,1,0:T(8,128)} %get-tuple-element.13.after.own_long, f32[8,136,128]{2,1,0:T(8,128)} %get-tuple-element.15.own_short, f32[8,136,128]{2,1,0:T(8,128)} %collective-permute-done.got_long, f32[8,136,128]{2,1,0:T(8,128)} %collective-permute-done.1.got_short, ...), custom_call_target="tpu_custom_call" | custom-call | flops 8000000 | bytes 4000000 | tf_op jit(solution)/shard_map/totals/pallas_call | solution.py:609
  30.1 1.8 %collective-permute-start.2 = (f32[5,4,8,16,128]{4,3,2,1,0:T(8,128)}, f32[5,4,8,16,128]{4,3,2,1,0:T(8,128)}, u32[]{:S(2)}, u32[]{:S(2)}) collective-permute-start(f32[5,4,8,16,128]{4,3,2,1,0:T(8,128)} %get-tuple-element.20), channel_id=1, source_target_pairs={{0,1},{1,0},{2,3},{3,2},{4,5},{5,4},{6,7},{7,6},{8,9},{9,8},{10,11... | collective-permute-start | bytes 3932168 | tf_op jit(solution)/shard_map/ppermute | solution.py:919
  31.9 8.0 %all-to-all-start = ((f32[256,1,128]{2,1,0:T(1,128)}), f32[256,1,128]{2,1,0:T(1,128)S(1)}, u32[]{:S(2)}, u32[]{:S(2)}) async-start(f32[256,1,128]{2,1,0:T(1,128)} %bitcast.9), calls=%async_computation | async-start | bytes 262144 | tf_op jit(solution)/shard_map/all_to_all | solution.py:921
  40.0 0.0 collective-permute-done.2.other_in
  40.0 6.3 %edges.1 = f32[5,592,128]{2,1,0:T(8,128)} custom-call(f32[8,136,128]{2,1,0:T(8,128)} %get-tuple-element.13.after.own_long, f32[8,136,128]{2,1,0:T(8,128)} %get-tuple-element.15.own_short, f32[8,136,128]{2,1,0:T(8,128)} %collective-permute-done.got_long, f32[8,136,128]{2,1,0:T(8,128)} %collective-permute-done.1.got_short, ...), custom_call_target="tpu_custom_call" | custom-call | flops 20000000 | bytes 4000000 | tf_op jit(solution)/shard_map/edges/pallas_call | solution.py:731
  46.3 1.5 %broadcast_multiply_fusion.slabs = f32[5,592,128]{2,1,0:T(8,128)S(1)} fusion(f32[5,592,128]{2,1,0:T(8,128)} %edges.1), kind=kLoop, calls=%fused_computation | loop fusion | flops 378880 | bytes 3031040 | tf_op jit(solution)/shard_map/mul | solution.py:920
  47.8 5.3 %all-to-all-done = f32[256,1,128]{2,1,0:T(1,128)S(1)} async-done(((f32[256,1,128]{2,1,0:T(1,128)}), f32[256,1,128]{2,1,0:T(1,128)S(1)}, u32[]{:S(2)}, u32[]{:S(2)}) %all-to-all-start) | async-done | bytes 131104 | tf_op jit(solution)/shard_map/all_to_all | solution.py:921
  53.0 0.6 density.1
  53.6 1.0 %collective-permute-start.3 = (f32[592,128]{1,0:T(8,128)S(1)}, f32[592,128]{1,0:T(8,128)S(1)}, u32[]{:S(2)}, u32[]{:S(2)}) collective-permute-start(f32[592,128]{1,0:T(8,128)S(1)} %density.1), channel_id=1, source_target_pairs={{0,2},{1,3},{2,0},{3,1},{4,6},{5,7},{6,4},{7,5},{8,10},{9,11},{10,... | collective-permute-start | bytes 909320 | tf_op jit(solution)/shard_map/ppermute | solution.py:924
  54.6 9.0 %collective-permute-done.3 = f32[592,128]{1,0:T(8,128)S(1)} collective-permute-done((f32[592,128]{1,0:T(8,128)S(1)}, f32[592,128]{1,0:T(8,128)S(1)}, u32[]{:S(2)}, u32[]{:S(2)}) %collective-permute-start.3) | collective-permute-done | bytes 303136 | tf_op jit(solution)/shard_map/ppermute | solution.py:924
  63.6 1.3 %collective-permute-start.4 = (f32[592,128]{1,0:T(8,128)S(1)}, f32[592,128]{1,0:T(8,128)S(1)}, u32[]{:S(2)}, u32[]{:S(2)}) collective-permute-start(f32[592,128]{1,0:T(8,128)S(1)} %add.3.mine), channel_id=1, source_target_pairs={{0,1},{1,0},{2,3},{3,2},{4,5},{5,4},{6,7},{7,6},{8,9},{9,8},{10,11... | collective-permute-start | bytes 909320 | tf_op jit(solution)/shard_map/ppermute | solution.py:925
  64.9 1.2 %collective-permute-done.4.other = f32[592,128]{1,0:T(8,128)S(1)} collective-permute-done((f32[592,128]{1,0:T(8,128)S(1)}, f32[592,128]{1,0:T(8,128)S(1)}, u32[]{:S(2)}, u32[]{:S(2)}) %collective-permute-start.4) | collective-permute-done | bytes 303136 | tf_op jit(solution)/shard_map/ppermute | solution.py:925
  66.2 1.1 %new_potential.1 = f32[4,32,1024]{2,1,0:T(8,128)} custom-call(f32[592,128]{1,0:T(8,128)S(1)} %add.3.mine, f32[592,128]{1,0:T(8,128)S(1)} %collective-permute-done.4.other), custom_call_target="tpu_custom_call" | custom-call | flops 1000000 | bytes 2000000 | tf_op jit(solution)/shard_map/new_potential/pallas_call | solution.py:883
  (1 shorter events, 0.0 us)
Async XLA Ops:
  3.2 23.7 %collective-permute-start = (f32[8,136,128]{2,1,0:T(8,128)}, f32[8,136,128]{2,1,0:T(8,128)}, u32[]{:S(2)}, u32[]{:S(2)}) collective-permute-start(f32[8,136,128]{2,1,0:T(8,128)} %get-tuple-element.13.after.own_long), channel_id=1, source_target_pairs={{0,252},{4,8},{8,4},{12,16},{16,12},{20,24},{24,20},{28,32},{32,28... | collective-permute-start | bytes 1671176 | tf_op jit(solution)/shard_map/ppermute | solution.py:913
  13.1 13.8 %collective-permute-start.1 = (f32[8,136,128]{2,1,0:T(8,128)}, f32[8,136,128]{2,1,0:T(8,128)}, u32[]{:S(2)}, u32[]{:S(2)}) collective-permute-start(f32[8,136,128]{2,1,0:T(8,128)} %get-tuple-element.15.own_short), channel_id=1, source_target_pairs={{0,4},{4,0},{8,12},{12,8},{16,20},{20,16},{24,28},{28,24},{32,36},... | collective-permute-start | bytes 1671176 | tf_op jit(solution)/shard_map/ppermute | solution.py:914
  30.1 9.8 %collective-permute-start.2 = (f32[5,4,8,16,128]{4,3,2,1,0:T(8,128)}, f32[5,4,8,16,128]{4,3,2,1,0:T(8,128)}, u32[]{:S(2)}, u32[]{:S(2)}) collective-permute-start(f32[5,4,8,16,128]{4,3,2,1,0:T(8,128)} %get-tuple-element.20), channel_id=1, source_target_pairs={{0,1},{1,0},{2,3},{3,2},{4,5},{5,4},{6,7},{7,6},{8,9},{9,8},{10,11... | collective-permute-start | bytes 3932168 | tf_op jit(solution)/shard_map/ppermute | solution.py:919
  31.9 21.1 %all-to-all-start = ((f32[256,1,128]{2,1,0:T(1,128)}), f32[256,1,128]{2,1,0:T(1,128)S(1)}, u32[]{:S(2)}, u32[]{:S(2)}) async-start(f32[256,1,128]{2,1,0:T(1,128)} %bitcast.9), calls=%async_computation | async-start | bytes 262144 | tf_op jit(solution)/shard_map/all_to_all | solution.py:921
  53.6 10.0 %collective-permute-start.3 = (f32[592,128]{1,0:T(8,128)S(1)}, f32[592,128]{1,0:T(8,128)S(1)}, u32[]{:S(2)}, u32[]{:S(2)}) collective-permute-start(f32[592,128]{1,0:T(8,128)S(1)} %density.1), channel_id=1, source_target_pairs={{0,2},{1,3},{2,0},{3,1},{4,6},{5,7},{6,4},{7,5},{8,10},{9,11},{10,... | collective-permute-start | bytes 909320 | tf_op jit(solution)/shard_map/ppermute | solution.py:924
  63.6 2.5 %collective-permute-start.4 = (f32[592,128]{1,0:T(8,128)S(1)}, f32[592,128]{1,0:T(8,128)S(1)}, u32[]{:S(2)}, u32[]{:S(2)}) collective-permute-start(f32[592,128]{1,0:T(8,128)S(1)} %add.3.mine), channel_id=1, source_target_pairs={{0,1},{1,0},{2,3},{3,2},{4,5},{5,4},{6,7},{7,6},{8,9},{9,8},{10,11... | collective-permute-start | bytes 909320 | tf_op jit(solution)/shard_map/ppermute | solution.py:925
